TPU v7x, 32 devices: a whole 2x2x4 slice. The times are simulated.
32 devices in a mesh: segment: 4 (over y, x), tensor: 8 (over z, core).
Axes of the slice: x: 2, y: 2, z: 4, core: 2. Of those that a mesh axis runs over, the one named last changes fastest.
Arguments:
- tokens: int32 [192], replicated, may hold values from 0 to 64127
- embedding: bfloat16 [64128, 4096], P('segment', 'tensor'), may hold values from -36 to 36
- gain: float32 [2, 4096], replicated, may hold values from 0.1 to 1.9
- gate_weight: bfloat16 [4, 4096, 7168], P('segment', None, 'tensor'), may hold values from -0.09375 to 0.09375
- down_weight: bfloat16 [4, 7168, 4096], P('segment', 'tensor'), may hold values from -0.0625 to 0.0625
- basis: bfloat16 [4096, 512], P('tensor'), may hold values from -0.09375 to 0.09375
Outputs:
- collected: bfloat16 [4, 192, 512], P('segment')
All inputs are finite; a program needn't handle non-finite values.
Results may differ from a plain program's by a relative error of at most 0.02.
Values may be sent and summed in bfloat16 or wider, within the bound.
No kernel may reach another device: no remote copies, remote signals or barrier semaphores. Data moves between devices by JAX's collectives and lax.ppermute only.
A program may use at most 128 MiB of HBM per device.

v0:
```python
import jax
import jax.numpy as jnp
from jax import lax
from jax.sharding import PartitionSpec as P

D = 4096
MICRO = 3
ROWS = 64


def from_partner(value, axis, bit):
    mask = 2**bit
    pairs = [(source, source ^ mask) for source in range(lax.axis_size(axis))]
    return lax.ppermute(value, axis, pairs)


def shifted_2(block, axis, distance):
    devices = range(lax.axis_size(axis))
    route = [(i - distance, i) for i in devices if i - distance in devices]
    return lax.ppermute(block, axis, route)


def per_device(tokens, embedding, gain, gate_weight, down_weight, basis):
    local_vocab = embedding.shape[0]
    segment_index = lax.axis_index("segment")
    shifted = tokens - segment_index * local_vocab
    inside = (shifted >= 0) & (shifted < local_vocab)
    picked = jnp.take(embedding, jnp.clip(shifted, 0, local_vocab - 1), axis=0)
    picked = jnp.where(inside[:, None], picked, jnp.zeros_like(picked))
    embedded = lax.psum(picked.astype(jnp.float32).astype(jnp.bfloat16), "segment")
    sections = lax.axis_size("segment") // 2
    section = segment_index // 2
    parity = segment_index % 2
    gate_local = gate_weight[0]
    down_local = down_weight[0]
    gain_row = lax.dynamic_slice_in_dim(gain, section, 1, 0)[0]
    basis_wide = basis.astype(jnp.float32)
    rank = basis.shape[1]
    basis_whole = None
    basis_whole = lax.all_gather(basis, "tensor", axis=0, tiled=True)

    def accumulate(piece):
        wide_piece = piece.astype(jnp.float32)
        scaled = (wide_piece * gain_row[None, :]).astype(jnp.bfloat16)
        total = jnp.dot(scaled, gate_local, preferred_element_type=jnp.float32)
        squares = jnp.sum(wide_piece * wide_piece, axis=1)
        return (total, squares)

    def one_step(step, received, collected):
        micro_index = step - section
        valid = (micro_index >= 0) & (micro_index < MICRO)
        clipped = jnp.clip(micro_index, 0, MICRO - 1)
        embed_rows = lax.dynamic_slice_in_dim(embedded, clipped * ROWS, ROWS, 0)
        expanded = lax.dot_general(
            received, basis, (((1,), (1,)), ((), ())), preferred_element_type=jnp.float32
        )
        rebuilt = (expanded + embed_rows.astype(jnp.float32)).astype(jnp.bfloat16)
        layer_input = jnp.where(section == 0, embed_rows, rebuilt)
        total, squares = accumulate(lax.all_gather(layer_input, "tensor", axis=1, tiled=True))
        inverse_norm = lax.rsqrt(squares / D + 1e-05)
        activation = jax.nn.silu(total * inverse_norm[:, None]).astype(jnp.bfloat16)
        partial_value = jnp.dot(activation, down_local, preferred_element_type=jnp.float32).astype(
            jnp.bfloat16
        )
        partial_value = lax.optimization_barrier(partial_value)
        difference = layer_input.astype(jnp.float32) - embed_rows.astype(jnp.float32)
        projected = jnp.dot(partial_value, basis_whole, preferred_element_type=jnp.float32)
        own_term = jnp.dot(difference, basis_wide, precision=lax.Precision.HIGHEST) * (
            1 - parity
        ).astype(jnp.float32)
        combined = lax.psum((projected + own_term).astype(jnp.bfloat16), "tensor").astype(
            jnp.float32
        )
        coefficients = combined + from_partner(combined.astype(jnp.bfloat16), "segment", 0).astype(
            combined.dtype
        )
        result = coefficients.astype(jnp.bfloat16)
        current = lax.dynamic_slice_in_dim(collected[0], clipped * ROWS, ROWS, 0)
        written = jnp.where(valid, result, current)
        collected = lax.dynamic_update_slice_in_dim(collected, written[None], clipped * ROWS, 1)
        return (result, collected)

    collected = jnp.zeros((1, MICRO * ROWS, rank), jnp.bfloat16)
    result, collected = one_step(0, jnp.zeros((ROWS, rank), jnp.bfloat16), collected)

    def advance(step, carry):
        result, collected = carry
        received = shifted_2(result, "segment", 2)
        return one_step(step, received, collected)

    result, collected = lax.fori_loop(1, MICRO + sections - 1, advance, (result, collected))
    return collected


def solution(mesh):
    placed = (
        P(),
        P("segment", "tensor"),
        P(),
        P("segment", None, "tensor"),
        P("segment", "tensor", None),
        P("tensor", None),
    )
    return jax.shard_map(
        per_device, mesh=mesh, in_specs=placed, out_specs=P("segment", None, None), check_vma=False
    )
```

profile of v0, /device:TPU:0, one launch (start us, length us, event | category | flops | bytes accessed | tf_op | source)
XLA Modules:
  0.0 434.8 jit_solution(15297847655245517652)
XLA Ops:
  7.4 0.7 compare_and_fusion
  8.1 8.8 %gather_fusion = bf16[192,512]{1,0:T(8,128)(2,1)S(1)} fusion(bf16[16032,512]{1,0:T(8,128)(2,1)} %param.9, s32[1024]{0:T(1024)S(1)} %pad_clamp_fusion), kind=kCustom, calls=%fused_computation | custom fusion | bytes 393984 | tf_op jit(solution)/shard_map/jit(_take)/gather | solution.py:28
  16.9 0.8 select_select_fusion
  17.7 0.0 all-reduce.4.cloned.1.call-update
  17.7 0.0 all-gather.2.cloned.1.call-start
  17.8 0.5 all-gather.2.cloned.1.call-update
  18.3 0.0 all-reduce.6.cloned.1.call-start
  18.4 44.6 %all-reduce.4.cloned.1.call-done = bf16[192,512]{1,0:T(8,128)(2,1)} async-done(((bf16[192,512]{1,0:T(8,128)(2,1)}), bf16[192,512]{1,0:T(8,128)(2,1)}) %all-reduce.4.cloned.1.call-update) | async-done | bytes 196624 | tf_op jit(solution)/shard_map/psum | solution.py:30
  63.0 1.3 fusion.20
  64.4 14.7 %all_gather.15 = bf16[64,4096]{1,0:T(8,128)(2,1)S(1)} all-gather(bf16[64,512]{1,0:T(8,128)(2,1)S(1)} %fusion.20), channel_id=1, replica_groups=mesh['segment'=4,'tensor'=8] {'tensor'}, dimensions={1}, use_global_device_ids=true | all-gather | bytes 589824 | tf_op jit(solution)/shard_map/all_gather | solution.py:59
  79.1 0.2 fusion.22
  79.3 8.0 %convolution_convert_fusion.1 = bf16[64,4096]{1,0:T(8,128)(2,1)S(1)} fusion(bf16[64,4096]{1,0:T(8,128)(2,1)S(1)} %all_gather.15, f32[4096]{0:T(1024)S(1)} %bitcast.50, f32[64]{0:T(128)S(1)} %add_rsqrt_fusion.1, bf16[1,896,4096]{2,1,0:T(8,128)(2,1)} %param.12, bf16[1,4096,896]{2,1,0:T(8,128)(2,1)} %param.11), kind=kOutput, calls=%fused_computation.27 | convolution fusion | flops 940916736 | bytes 15745280 | tf_op jit(solution)/shard_map/dot_general | solution.py:62
  87.3 0.0 all-gather.2.cloned.1.call-done
  87.3 3.0 fusion.40
  90.4 1.0 fusion.19
  91.4 0.0 all-reduce.6.cloned.1.call-update
  91.4 53.7 %all-reduce.6.cloned.1.call-done = bf16[64,512]{1,0:T(8,128)(2,1)} async-done(((bf16[64,512]{1,0:T(8,128)(2,1)}), bf16[64,512]{1,0:T(8,128)(2,1)}) %all-reduce.6.cloned.1.call-update) | async-done | bytes 65552 | tf_op jit(solution)/shard_map/psum | solution.py:71
  145.1 1.5 collective-permute-start.2
  146.6 0.1 convert_element_type.165
  146.7 2.9 collective-permute-done.2
  149.6 0.9 bitcast_dynamic-update-slice_fusion.1
  150.5 276.5 %while.17 = (s32[]{:T(128)}, bf16[64,512]{1,0:T(8,128)(2,1)S(1)}, bf16[1,192,512]{2,1,0:T(8,128)(2,1)S(1)}, pred[]{:T(512)}, s32[]{:T(128)}, /*index=5*/bf16[192...) while((s32[]{:T(128)}, bf16[64,512]{1,0:T(8,128)(2,1)S(1)}, ...), condition=%wide.region_6.7_spmd, body=%wide.region_3.6_spmd.sunk | while | flops 1445544064 | bytes 25183648 | solution.py:91
  150.5 0.0 all-reduce.8.cloned.1.call-start
  150.6 3.4 collective-permute-start
  154.0 1.9 collective-permute-done
  155.8 0.3 fusion.71
  156.1 14.8 %all_gather.18 = bf16[64,4096]{1,0:T(8,128)(2,1)S(1)} all-gather(bf16[64,512]{1,0:T(8,128)(2,1)S(1)} %fusion.71), channel_id=1, replica_groups=mesh['segment'=4,'tensor'=8] {'tensor'}, dimensions={1}, use_global_device_ids=true | all-gather | bytes 589824 | tf_op jit(solution)/shard_map/while/body/eval_jaxpr/all_gather | solution.py:59
  171.0 0.2 fusion.72
  171.2 7.9 %convolution_convert_fusion.3 = bf16[64,4096]{1,0:T(8,128)(2,1)S(1)} fusion(bf16[896,4096]{1,0:T(8,128)(2,1)} %get-tuple-element.451, bf16[4096,896]{1,0:T(8,128)(2,1)} %get-tuple-element.450, bf16[64,4096]{1,0:T(8,128)(2,1)S(1)} %all_gather.18, f32[4096]{0:T(1024)S(1)} %bitcast.51, f32[64]{0:T(128)S(1)} %add_rsqrt_fusion.3), kind=kOutput, calls=%fused_computation.1.clone.1 | convolution fusion | flops 940916736 | bytes 15745280 | tf_op jit(solution)/shard_map/while/body/eval_jaxpr/dot_general | solution.py:62
  179.1 0.8 convolution_multiply_fusion.5
  179.8 3.7 fusion.73
  183.5 0.0 all-reduce.8.cloned.1.call-update
  183.5 53.8 %all-reduce.8.cloned.1.call-done = bf16[64,512]{1,0:T(8,128)(2,1)} async-done(((bf16[64,512]{1,0:T(8,128)(2,1)}), bf16[64,512]{1,0:T(8,128)(2,1)}) %all-reduce.8.cloned.1.call-update) | async-done | bytes 65552 | tf_op jit(solution)/shard_map/while/body/eval_jaxpr/psum | solution.py:71
  237.3 1.5 collective-permute-start.1
  238.8 3.0 collective-permute-done.1
  241.8 0.9 bitcast_dynamic-update-slice_fusion.3
  242.7 0.0 all-reduce.8.cloned.1.call-start
  242.7 3.4 collective-permute-start
  246.1 1.9 collective-permute-done
  248.0 0.3 fusion.71
  248.3 14.8 %all_gather.18 = bf16[64,4096]{1,0:T(8,128)(2,1)S(1)} all-gather(bf16[64,512]{1,0:T(8,128)(2,1)S(1)} %fusion.71), channel_id=1, replica_groups=mesh['segment'=4,'tensor'=8] {'tensor'}, dimensions={1}, use_global_device_ids=true | all-gather | bytes 589824 | tf_op jit(solution)/shard_map/while/body/eval_jaxpr/all_gather | solution.py:59
  263.1 0.2 fusion.72
  263.3 7.9 %convolution_convert_fusion.3 = bf16[64,4096]{1,0:T(8,128)(2,1)S(1)} fusion(bf16[896,4096]{1,0:T(8,128)(2,1)} %get-tuple-element.451, bf16[4096,896]{1,0:T(8,128)(2,1)} %get-tuple-element.450, bf16[64,4096]{1,0:T(8,128)(2,1)S(1)} %all_gather.18, f32[4096]{0:T(1024)S(1)} %bitcast.51, f32[64]{0:T(128)S(1)} %add_rsqrt_fusion.3), kind=kOutput, calls=%fused_computation.1.clone.1 | convolution fusion | flops 940916736 | bytes 15745280 | tf_op jit(solution)/shard_map/while/body/eval_jaxpr/dot_general | solution.py:62
  271.2 0.8 convolution_multiply_fusion.5
  272.0 3.7 fusion.73
  275.7 0.0 all-reduce.8.cloned.1.call-update
  275.7 53.8 %all-reduce.8.cloned.1.call-done = bf16[64,512]{1,0:T(8,128)(2,1)} async-done(((bf16[64,512]{1,0:T(8,128)(2,1)}), bf16[64,512]{1,0:T(8,128)(2,1)}) %all-reduce.8.cloned.1.call-update) | async-done | bytes 65552 | tf_op jit(solution)/shard_map/while/body/eval_jaxpr/psum | solution.py:71
  329.5 1.5 collective-permute-start.1
  330.9 3.0 collective-permute-done.1
  334.0 0.9 bitcast_dynamic-update-slice_fusion.3
  334.8 0.0 all-reduce.8.cloned.1.call-start
  334.9 3.4 collective-permute-start
  338.3 1.9 collective-permute-done
  340.2 0.3 fusion.71
  340.4 14.8 %all_gather.18 = bf16[64,4096]{1,0:T(8,128)(2,1)S(1)} all-gather(bf16[64,512]{1,0:T(8,128)(2,1)S(1)} %fusion.71), channel_id=1, replica_groups=mesh['segment'=4,'tensor'=8] {'tensor'}, dimensions={1}, use_global_device_ids=true | all-gather | bytes 589824 | tf_op jit(solution)/shard_map/while/body/eval_jaxpr/all_gather | solution.py:59
  355.3 0.2 fusion.72
  355.5 7.9 %convolution_convert_fusion.3 = bf16[64,4096]{1,0:T(8,128)(2,1)S(1)} fusion(bf16[896,4096]{1,0:T(8,128)(2,1)} %get-tuple-element.451, bf16[4096,896]{1,0:T(8,128)(2,1)} %get-tuple-element.450, bf16[64,4096]{1,0:T(8,128)(2,1)S(1)} %all_gather.18, f32[4096]{0:T(1024)S(1)} %bitcast.51, f32[64]{0:T(128)S(1)} %add_rsqrt_fusion.3), kind=kOutput, calls=%fused_computation.1.clone.1 | convolution fusion | flops 940916736 | bytes 15745280 | tf_op jit(solution)/shard_map/while/body/eval_jaxpr/dot_general | solution.py:62
  363.4 0.7 convolution_multiply_fusion.5
  364.2 3.7 fusion.73
  367.9 53.8 %all-reduce.8.cloned.1.call-done = bf16[64,512]{1,0:T(8,128)(2,1)} async-done(((bf16[64,512]{1,0:T(8,128)(2,1)}), bf16[64,512]{1,0:T(8,128)(2,1)}) %all-reduce.8.cloned.1.call-update) | async-done | bytes 65552 | tf_op jit(solution)/shard_map/while/body/eval_jaxpr/psum | solution.py:71
  421.6 1.5 collective-permute-start.1
  423.1 3.0 collective-permute-done.1
  426.1 0.9 bitcast_dynamic-update-slice_fusion.3
  427.0 0.7 copy-done.3
  (19 shorter events, 0.1 us)
Async XLA Ops:
  7.4 11.0 %copy-start = (f32[2,4096]{1,0:T(2,128)S(1)}, f32[2,4096]{1,0:T(2,128)}, u32[]{:S(2)}) copy-start(f32[2,4096]{1,0:T(2,128)} %param.10) | copy-start | bytes 98308
  7.4 55.7 %all-reduce.4.cloned.1.call-start = ((), (), s32[]{:S(2)}) async-start(), calls=%async_computation | async-start | bytes 393216 | tf_op jit(solution)/shard_map/psum | solution.py:30
  17.7 69.6 %all-gather.2.cloned.1.call-start = ((), (), s32[]{:S(2)}) async-start(), calls=%async_computation.1 | async-start | bytes 4718592 | tf_op jit(solution)/shard_map/all_gather | solution.py:40
  18.3 126.8 %all-reduce.6.cloned.1.call-start = ((), (), s32[]{:S(2)}) async-start(), calls=%async_computation.2 | async-start | bytes 131072 | tf_op jit(solution)/shard_map/psum | solution.py:71
  79.3 11.1 %copy-start.1 = (bf16[512,512]{1,0:T(8,128)(2,1)S(1)}, bf16[512,512]{1,0:T(8,128)(2,1)}, u32[]{:S(2)}) copy-start(bf16[512,512]{1,0:T(8,128)(2,1)} %param.13) | copy-start | bytes 1572868
  79.3 11.1 %copy-start.2 = (bf16[192,512]{1,0:T(8,128)(2,1)S(1)}, bf16[192,512]{1,0:T(8,128)(2,1)}, u32[]{:S(2)}) copy-start(bf16[192,512]{1,0:T(8,128)(2,1)} %all-reduce.4.cloned.1.call-done) | copy-start | bytes 589828
  145.1 4.5 %collective-permute-start.2 = (bf16[64,512]{1,0:T(8,128)(2,1)}, bf16[64,512]{1,0:T(8,128)(2,1)S(1)}, u32[]{:S(2)}, u32[]{:S(2)}) collective-permute-start(bf16[64,512]{1,0:T(8,128)(2,1)} %all-reduce.6.cloned.1.call-done), channel_id=1, source_target_pairs={{0,8},{8,0},{16,24},{24,16},{1,9},{9,1},{17,25},{25,17},{2,10},{10... | collective-permute-start | bytes 196616 | tf_op jit(solution)/shard_map/ppermute | solution.py:14
  150.5 86.8 %all-reduce.8.cloned.1.call-start = ((), (), s32[]{:S(2)}) async-start(), calls=%async_computation.3 | async-start | bytes 131072 | tf_op jit(solution)/shard_map/while/body/eval_jaxpr/psum | solution.py:71
  150.6 5.3 %collective-permute-start = (bf16[64,512]{1,0:T(8,128)(2,1)S(1)}, bf16[64,512]{1,0:T(8,128)(2,1)S(1)}, u32[]{:S(2)}, u32[]{:S(2)}) collective-permute-start(bf16[64,512]{1,0:T(8,128)(2,1)S(1)} %get-tuple-element.424), channel_id=1, source_target_pairs={{0,16},{8,24},{1,17},{9,25},{2,18},{10,26},{3,19},{11,27},{4,20},{... | collective-permute-start | bytes 196616 | tf_op jit(solution)/shard_map/while/body/eval_jaxpr/ppermute | solution.py:20
  237.3 4.5 %collective-permute-start.1 = (bf16[64,512]{1,0:T(8,128)(2,1)}, bf16[64,512]{1,0:T(8,128)(2,1)S(1)}, u32[]{:S(2)}, u32[]{:S(2)}) collective-permute-start(bf16[64,512]{1,0:T(8,128)(2,1)} %all-reduce.8.cloned.1.call-done), channel_id=1, source_target_pairs={{0,8},{8,0},{16,24},{24,16},{1,9},{9,1},{17,25},{25,17},{2,10},{10... | collective-permute-start | bytes 196616 | tf_op jit(solution)/shard_map/while/body/eval_jaxpr/ppermute | solution.py:14
  242.7 86.8 %all-reduce.8.cloned.1.call-start = ((), (), s32[]{:S(2)}) async-start(), calls=%async_computation.3 | async-start | bytes 131072 | tf_op jit(solution)/shard_map/while/body/eval_jaxpr/psum | solution.py:71
  242.7 5.3 %collective-permute-start = (bf16[64,512]{1,0:T(8,128)(2,1)S(1)}, bf16[64,512]{1,0:T(8,128)(2,1)S(1)}, u32[]{:S(2)}, u32[]{:S(2)}) collective-permute-start(bf16[64,512]{1,0:T(8,128)(2,1)S(1)} %get-tuple-element.424), channel_id=1, source_target_pairs={{0,16},{8,24},{1,17},{9,25},{2,18},{10,26},{3,19},{11,27},{4,20},{... | collective-permute-start | bytes 196616 | tf_op jit(solution)/shard_map/while/body/eval_jaxpr/ppermute | solution.py:20
  329.5 4.5 %collective-permute-start.1 = (bf16[64,512]{1,0:T(8,128)(2,1)}, bf16[64,512]{1,0:T(8,128)(2,1)S(1)}, u32[]{:S(2)}, u32[]{:S(2)}) collective-permute-start(bf16[64,512]{1,0:T(8,128)(2,1)} %all-reduce.8.cloned.1.call-done), channel_id=1, source_target_pairs={{0,8},{8,0},{16,24},{24,16},{1,9},{9,1},{17,25},{25,17},{2,10},{10... | collective-permute-start | bytes 196616 | tf_op jit(solution)/shard_map/while/body/eval_jaxpr/ppermute | solution.py:14
  334.8 86.8 %all-reduce.8.cloned.1.call-start = ((), (), s32[]{:S(2)}) async-start(), calls=%async_computation.3 | async-start | bytes 131072 | tf_op jit(solution)/shard_map/while/body/eval_jaxpr/psum | solution.py:71
  334.9 5.3 %collective-permute-start = (bf16[64,512]{1,0:T(8,128)(2,1)S(1)}, bf16[64,512]{1,0:T(8,128)(2,1)S(1)}, u32[]{:S(2)}, u32[]{:S(2)}) collective-permute-start(bf16[64,512]{1,0:T(8,128)(2,1)S(1)} %get-tuple-element.424), channel_id=1, source_target_pairs={{0,16},{8,24},{1,17},{9,25},{2,18},{10,26},{3,19},{11,27},{4,20},{... | collective-permute-start | bytes 196616 | tf_op jit(solution)/shard_map/while/body/eval_jaxpr/ppermute | solution.py:20
  421.6 4.5 %collective-permute-start.1 = (bf16[64,512]{1,0:T(8,128)(2,1)}, bf16[64,512]{1,0:T(8,128)(2,1)S(1)}, u32[]{:S(2)}, u32[]{:S(2)}) collective-permute-start(bf16[64,512]{1,0:T(8,128)(2,1)} %all-reduce.8.cloned.1.call-done), channel_id=1, source_target_pairs={{0,8},{8,0},{16,24},{24,16},{1,9},{9,1},{17,25},{25,17},{2,10},{10... | collective-permute-start | bytes 196616 | tf_op jit(solution)/shard_map/while/body/eval_jaxpr/ppermute | solution.py:14
  427.0 0.7 copy-start.3
Sparse Core Ops, SparseCore 0:
  17.9 45.1 all-reduce.3
  183.6 53.6 all-reduce.7
  275.8 53.6 all-reduce.7
  368.0 53.6 all-reduce.7
Sparse Core Ops, SparseCore 1:
  19.8 49.4 all-gather.1
  91.5 53.6 all-reduce.5
where the time goes:
time: 435 us
  waiting for transfers between devices  278 us (64%)
  blocking collectives  59.2 us (14%)
  matrix products  51.1 us (12%)
  starting transfers between devices  16.2 us (4%)
  between operations  14.7 us (3%)
  local copies, waits for them, and re-layouts  9.56 us (2%)
  other arithmetic  5.98 us (1%)
    psum x4, waiting for transfers between devices, one_step(): lax.psum((projected + own_term).astype(jnp.bfloat16), 'tensor')  215 us
    all_gather x4, blocking collectives, one_step(): lax.all_gather(layer_input, 'tensor', axis=1, tiled=True)  59.2 us
    psum x1, waiting for transfers between devices, per_device(): lax.psum(picked.astype(jnp.float32).astype(jnp.bfloat16), 'segment')  44.6 us
    dot_general x4, matrix products, one_step(): jnp.dot(activation, down_local, preferred_element_type=jnp.float32)  31.7 us
    dot_general x4, matrix products, one_step(): jnp.dot(partial_value, basis_whole, preferred_element_type=jnp.float32)  14 us
    ppermute x4, waiting for transfers between devices, from_partner(): return lax.ppermute(value, axis, pairs)  11.9 us
    ppermute x3, starting transfers between devices, shifted_2(): return lax.ppermute(block, axis, route)  10.1 us
    gather x1, local copies, waits for them, and re-layouts, per_device(): picked = jnp.take(embedding, jnp.clip(shifted, 0, local_vocab - 1), axis=0)  8.82 us
  transfers between devices with their start and end apart: 13, of which 12 were waited for; matrix products, arithmetic and copies ran while one was open for 2% of the time, Pallas kernels for 0%

commit v1 on v0

v1 whole, which is shorter than its diff:
```python
import functools

import jax
import jax.numpy as jnp
from jax import lax
from jax.experimental import pallas as pl
from jax.experimental.pallas import tpu as pltpu
from jax.sharding import PartitionSpec as P

EPSILON = 1e-05
GROUP = 4
TILE = 16
CHUNK = 512
F32 = jnp.float32
BF16 = jnp.bfloat16


def swap(value, axis, mask):
    return lax.ppermute(value, axis, [(i, i ^ mask) for i in range(lax.axis_size(axis))])


def onward(value, flip):
    size = lax.axis_size("segment")
    return lax.ppermute(value, "segment", [(i, (i ^ flip) + 2) for i in range(size - 2)])


def tree_sum(values):
    while len(values) > 1:
        values = [values[i] + values[i + 1] for i in range(0, len(values), 2)]
    return values[0]


def fetch_kernel(block_rows, vocab, tokens_smem, tokens_row, table, *refs):
    outs, buffer, sem = refs[:GROUP], refs[GROUP], refs[GROUP + 1]
    segment = lax.axis_index("segment")
    low = segment * vocab
    count = GROUP * block_rows

    def start(i, carry):
        local = jnp.clip(tokens_smem[i] - low, 0, vocab - 1)
        first = pl.multiple_of((local // TILE) * TILE, TILE)
        place = pl.multiple_of(i * TILE, TILE)
        pltpu.make_async_copy(
            table.at[pl.ds(first, TILE), :], buffer.at[pl.ds(place, TILE), :], sem
        ).start()
        return carry

    lax.fori_loop(0, count, start, 0, unroll=8)
    wanted = tokens_row[...] - low
    inside = (wanted >= 0) & (wanted < vocab)
    code = jnp.where(inside, lax.rem(wanted, TILE), TILE)
    rows = lax.broadcasted_iota(jnp.int32, (count, count), 0)
    columns = lax.broadcasted_iota(jnp.int32, (count, count), 1)
    code_column = jnp.sum(jnp.where(rows == columns, code, 0), axis=1, keepdims=True)
    pltpu.make_async_copy(buffer, buffer, sem).wait()
    home = lax.rem(segment, GROUP)
    wide = block_rows * TILE
    row_of = lax.broadcasted_iota(jnp.int32, (block_rows, wide), 0)
    lane_of = lax.broadcasted_iota(jnp.int32, (block_rows, wide), 1)
    results = []
    for block in range(GROUP):
        code_block = code_column[block * block_rows : (block + 1) * block_rows]
        hot = (lane_of == row_of * TILE + code_block) & (code_block < TILE)
        hot = jnp.where(hot, 1.0, 0.0).astype(BF16)
        results.append(
            jnp.dot(
                hot, buffer[block * wide : (block + 1) * wide, :], preferred_element_type=F32
            ).astype(BF16)
        )
    for block in range(GROUP):
        for mask in range(GROUP):

            @pl.when(jnp.bitwise_xor(home, mask) == block)
            def _(block=block, mask=mask):
                outs[mask][...] = results[block]


def fetch_rows(tokens, embedding):
    vocab, features = embedding.shape
    block_rows = tokens.shape[0] // GROUP
    if vocab % TILE:
        segment = lax.axis_index("segment")
        local = tokens - segment * vocab
        inside = (local >= 0) & (local < vocab)
        picked = jnp.take(embedding, jnp.clip(local, 0, vocab - 1), axis=0)
        picked = jnp.where(inside[:, None], picked, jnp.zeros_like(picked))
        picked = picked.reshape(GROUP, block_rows, features)
        home = segment % GROUP
        return [lax.dynamic_index_in_dim(picked, home ^ m, 0, False) for m in range(GROUP)]
    return pl.pallas_call(
        functools.partial(fetch_kernel, block_rows, vocab),
        out_shape=[jax.ShapeDtypeStruct((block_rows, features), BF16)] * GROUP,
        in_specs=[
            pl.BlockSpec(memory_space=pltpu.SMEM),
            pl.BlockSpec(memory_space=pltpu.VMEM),
            pl.BlockSpec(memory_space=pl.ANY),
        ],
        out_specs=[pl.BlockSpec(memory_space=pltpu.VMEM)] * GROUP,
        scratch_shapes=[
            pltpu.VMEM((tokens.shape[0] * TILE, features), BF16),
            pltpu.SemaphoreType.DMA,
        ],
        compiler_params=pltpu.CompilerParams(vmem_limit_bytes=32 * 2**20),
        name="fetch_rows",
    )(tokens, tokens.reshape(1, -1), embedding)


def section_kernel(first, chips, *refs):
    if first:
        pieces, refs = refs[: 2 * GROUP], refs[2 * GROUP :]
    else:
        (half_own, half_other, embedded), refs = refs[:3], refs[3:]
    (gain, gate, down, basis), refs = refs[:4], refs[4:]
    (own, send), refs = refs[:2], refs[2:]
    if first:
        embedded, refs = refs[0], refs[1:]
    gates, downs, bases, total, projected, sems = refs
    tokens, width = embedded.shape
    segment = lax.axis_index("segment")
    place = lax.axis_index("tensor")
    core = lax.rem(place, 2)
    chip = place // 2
    chunks = width // CHUNK

    def gate_copy(k):
        return pltpu.make_async_copy(gate.at[0, pl.ds(k * CHUNK, CHUNK), :], gates.at[k], sems.at[0, k])

    def down_copy(k):
        return pltpu.make_async_copy(down.at[0, :, pl.ds(k * CHUNK, CHUNK)], downs.at[k], sems.at[1, k])

    def basis_copy(k):
        return pltpu.make_async_copy(basis.at[pl.ds(k * CHUNK, CHUNK), :], bases.at[k], sems.at[2, k])

    if first:
        order = [gate_copy, down_copy, basis_copy]
        for copy in order:
            for k in range(chunks):
                copy(k).start()
        features = width // (2 * chips)
        rows = tokens // GROUP
        home = lax.rem(segment, GROUP)
        for side in range(2):
            for block in range(GROUP):
                row = pl.multiple_of(jnp.bitwise_xor(home, block) * rows, rows)
                for turn in range(chips):
                    column = (jnp.bitwise_xor(chip, turn) * 2 + jnp.bitwise_xor(core, side)) * features
                    embedded[pl.ds(row, rows), pl.ds(pl.multiple_of(column, features), features)] = (
                        pieces[side * GROUP + block][turn]
                    )
    else:
        for k in range(chunks):
            basis_copy(k).start()
            gate_copy(k).start()
        for k in range(chunks):
            down_copy(k).start()
        half = tokens // 2
        flipped = jnp.where(core == 0, half_own[...], half_other[...])
        second = jnp.where(core == 0, half_other[...], half_own[...])
        received = jnp.concatenate([flipped, second], axis=0)

    gain_row = gain[pl.ds(segment // 2, 1), :]
    squares = jnp.zeros((tokens, 1), F32)
    for k in range(chunks):
        span = slice(k * CHUNK, (k + 1) * CHUNK)
        if first:
            wide = embedded[:, span].astype(F32)
        else:
            basis_copy(k).wait()
            expanded = lax.dot_general(
                received, bases[k], (((1,), (1,)), ((), ())), preferred_element_type=F32
            )
            wide = (expanded + embedded[:, span].astype(F32)).astype(BF16).astype(F32)
        squares = squares + jnp.sum(wide * wide, axis=1, keepdims=True)
        scaled = (wide * gain_row[:, span]).astype(BF16)
        gate_copy(k).wait()
        product = jnp.dot(scaled, gates[k], preferred_element_type=F32)
        total[...] = product if k == 0 else total[...] + product
    inverse_norm = lax.rsqrt(squares / width + EPSILON)
    activation = jax.nn.silu(total[...] * inverse_norm).astype(BF16)

    if first:
        projected[...] = jnp.zeros_like(projected)
    else:
        share = width // (2 * chips)
        at = pl.multiple_of(place * share, share)
        table = bases[place * share // CHUNK]
        table = bases.at[place * share // CHUNK][
            pl.ds(pl.multiple_of(lax.rem(place * share, CHUNK), share), share), :
        ]
        expanded = lax.dot_general(
            received, table, (((1,), (1,)), ((), ())), preferred_element_type=F32
        )
        base = embedded[:, pl.ds(at, share)].astype(F32)
        difference = (expanded + base).astype(BF16).astype(F32) - base
        coarse = difference.astype(BF16)
        fine = (difference - coarse.astype(F32)).astype(BF16)
        term = jnp.dot(coarse, table, preferred_element_type=F32) + jnp.dot(
            fine, table, preferred_element_type=F32
        )
        projected[...] = jnp.where(lax.rem(segment, 2) == 0, term, jnp.zeros_like(term))
    for k in range(chunks):
        down_copy(k).wait()
        partial = jnp.dot(activation, downs[k], preferred_element_type=F32).astype(BF16)
        if first:
            basis_copy(k).wait()
        projected[...] += jnp.dot(partial, bases[k], preferred_element_type=F32)
    half = tokens // 2
    own[...] = projected[pl.ds(pl.multiple_of(core * half, half), half), :].astype(BF16)
    send[...] = projected[pl.ds(pl.multiple_of((1 - core) * half, half), half), :].astype(BF16)


def run_section(first, inputs, gain, gate, down, basis, tokens):
    width, rank = basis.shape
    hidden = gate.shape[2]
    chunks = width // CHUNK
    halves = [jax.ShapeDtypeStruct((tokens // 2, rank), BF16)] * 2
    outs = halves + ([jax.ShapeDtypeStruct((tokens, width), BF16)] if first else [])
    vmem = pl.BlockSpec(memory_space=pltpu.VMEM)
    anywhere = pl.BlockSpec(memory_space=pl.ANY)
    return pl.pallas_call(
        functools.partial(section_kernel, first, lax.axis_size("tensor") // 2),
        out_shape=outs,
        in_specs=[vmem] * (len(inputs) + 1) + [anywhere] * 3,
        out_specs=[vmem] * len(outs),
        scratch_shapes=[
            pltpu.VMEM((chunks, CHUNK, hidden), BF16),
            pltpu.VMEM((chunks, hidden, CHUNK), BF16),
            pltpu.VMEM((chunks, CHUNK, rank), BF16),
            pltpu.VMEM((tokens, hidden), F32),
            pltpu.VMEM((tokens, rank), F32),
            pltpu.SemaphoreType.DMA((3, chunks)),
        ],
        compiler_params=pltpu.CompilerParams(vmem_limit_bytes=48 * 2**20),
        cost_estimate=pl.CostEstimate(
            flops=2 * tokens * width * (2 * hidden + rank),
            bytes_accessed=2 * width * (2 * hidden + rank),
            transcendentals=tokens * hidden,
        ),
        name="section_first" if first else "section_next",
    )(*inputs, gain, gate, down, basis)


def per_device(tokens, embedding, gain, gate_weight, down_weight, basis):
    segments = lax.axis_size("segment")
    chips = lax.axis_size("tensor") // 2
    sections = segments // 2
    section = lax.axis_index("segment") // 2
    core = lax.axis_index("tensor") % 2
    count = tokens.shape[0]
    whole_basis = lax.all_gather(basis, "tensor", axis=0, tiled=True)

    blocks = fetch_rows(tokens, embedding)
    mask = GROUP
    while mask < segments:
        blocks = [block + swap(block, "segment", mask) for block in blocks]
        mask *= 2
    complete = tree_sum(
        [block if m == 0 else swap(block, "segment", m) for m, block in enumerate(blocks)]
    )
    along = jnp.stack([complete] + [swap(complete, "tensor", 2 * m) for m in range(1, chips)])
    mine = [along] + [swap(along, "segment", m) for m in range(1, GROUP)]
    theirs = [swap(piece, "tensor", 1) for piece in mine]

    received = embedded = None
    kept = None
    for step in range(sections):
        if step == 0:
            own, send, embedded = run_section(
                True, mine + theirs, gain, gate_weight, down_weight, whole_basis, count
            )
        else:
            own, send = run_section(
                False, [*received, embedded], gain, gate_weight, down_weight, whole_basis, count
            )
        chip_sum = (own.astype(F32) + swap(send, "tensor", 1).astype(F32)).astype(BF16)
        terms = [chip_sum] + [swap(chip_sum, "tensor", 2 * m) for m in range(1, chips)]
        half_sum = tree_sum([term.astype(F32) for term in terms]).astype(BF16)
        result = half_sum.astype(F32) + swap(half_sum, "segment", 1).astype(F32)
        if step + 1 < sections:
            handed = onward(half_sum, 0).astype(F32) + onward(half_sum, 1).astype(F32)
            result = jnp.where(section <= step, result, handed)
        result = result.astype(BF16)
        received = (result, swap(result, "tensor", 1))
        if step == 0:
            kept = received
        else:
            kept = tuple(jnp.where(section == step, new, old) for new, old in zip(received, kept))
    near, far = kept
    first = jnp.where(core == 0, near, far)
    second = jnp.where(core == 0, far, near)
    return jnp.concatenate([first, second], axis=0)[None]


def solution(mesh):
    placed = (
        P(),
        P("segment", "tensor"),
        P(),
        P("segment", None, "tensor"),
        P("segment", "tensor", None),
        P("tensor", None),
    )
    return jax.shard_map(
        per_device, mesh=mesh, in_specs=placed, out_specs=P("segment", None, None), check_vma=False
    )
```

time: 435 us -> 138 us (0.32)
  waiting for transfers between devices: 278 us -> 53.4 us
  blocking collectives: 59.2 us -> 0 us
  matrix products: 51.1 us -> 0 us
  Pallas kernels: 0 us -> 29.1 us
  starting transfers between devices: 16.2 us -> 30.6 us
  other arithmetic: 5.98 us -> 0.99 us
    psum x5 -> x0, waiting for transfers between devices: 260 us -> none  [the longest x4 215 us: one_step(): lax.psum((projected + own_term).astype(jnp.bfloat16), 'tensor')]
    all_gather x4 -> x0, blocking collectives: 59.2 us -> none  [one_step(): lax.all_gather(layer_input, 'tensor', axis=1, tiled=True)]
    dot_general x16 -> x0, matrix products: 51.1 us -> none  [the longest x4 31.7 us: one_step(): jnp.dot(activation, down_local, preferred_element_type=jnp.float32)]
    pallas_call x0 -> x3, Pallas kernels: none -> 29.1 us  [the longest x2 21.4 us: run_section(): pl.pallas_call(functools.partial(section_kernel, first, lax.axis_size('te...]
    ppermute x7 -> x27, waiting for transfers between devices: 17.5 us -> 42.7 us  [the longest x25 40.7 us: swap(): lax.ppermute(value, axis, [(i, i ^ mask) for i in range(lax.axis_size(axi...]
    ppermute x7 -> x27, starting transfers between devices: 16 us -> 30.6 us  [the longest x25 25.8 us: swap(): lax.ppermute(value, axis, [(i, i ^ mask) for i in range(lax.axis_size(axi...]
    all_gather x1, waiting for transfers between devices: 0.03 us -> 10.1 us  [per_device(): whole_basis = lax.all_gather(basis, 'tensor', axis=0, tiled=True)]
    gather x1 -> x0, local copies, waits for them, and re-layouts: 8.82 us -> none  [per_device(): picked = jnp.take(embedding, jnp.clip(shifted, 0, local_vocab - 1), axis=0)]
  transfers between devices with their start and end apart: 13 -> 28, of which waited for: 12 -> 21; matrix products, arithmetic and copies ran while one was open for 2% -> 0% of each run, Pallas kernels for 0% -> 6%
where the time goes in v1:
time: 138 us; the launch traced here: 136 us
  waiting for transfers between devices  53.4 us (39%)
  starting transfers between devices  30.6 us (22%)
  Pallas kernels  29.1 us (21%)
  between operations  13.6 us (10%)
  local copies, waits for them, and re-layouts  8.53 us (6%)
    ppermute x25, waiting for transfers between devices, swap(): lax.ppermute(value, axis, [(i, i ^ mask) for i in range(lax.axis_size(axi...  40.7 us
    ppermute x25, starting transfers between devices, swap(): lax.ppermute(value, axis, [(i, i ^ mask) for i in range(lax.axis_size(axi...  25.8 us
    pallas_call x2, Pallas kernels, run_section(): pl.pallas_call(functools.partial(section_kernel, first, lax.axis_size('te...  21.4 us
    all_gather x1, waiting for transfers between devices, per_device(): whole_basis = lax.all_gather(basis, 'tensor', axis=0, tiled=True)  10.1 us
    unnamed x8, local copies, waits for them, and re-layouts  8.53 us
    pallas_call x1, Pallas kernels, fetch_rows(): pl.pallas_call(functools.partial(fetch_kernel, block_rows, vocab), out_sh...  7.7 us
    ppermute x2, starting transfers between devices, onward(): lax.ppermute(value, 'segment', [(i, (i ^ flip) + 2) for i in range(size -...  4.76 us
  transfers between devices with their start and end apart: 28, of which 21 were waited for; matrix products, arithmetic and copies ran while one was open for 0% of the time, Pallas kernels for 6%

profile of v1, /device:TPU:0, one launch (start us, length us, event | category | flops | bytes accessed | tf_op | source)
XLA Modules:
  0.0 136.2 jit_solution(13928787170421885007)
XLA Ops:
  6.5 0.7 all-gather.2.cloned.1.call-update
  7.3 5.7 %copy-done.1 = bf16[16032,512]{1,0:T(8,128)(2,1)S(1)} copy-done((bf16[16032,512]{1,0:T(8,128)(2,1)S(1)}, bf16[16032,512]{1,0:T(8,128)(2,1)}, u32[]{:S(2)}) %copy-start.1) | copy-done | bytes 16416792
  12.9 0.7 copy-done.3
  13.6 7.7 %fetch_rows.1 = (bf16[48,512]{1,0:T(8,128)(2,1)S(1)}, bf16[48,512]{1,0:T(8,128)(2,1)S(1)}, bf16[48,512]{1,0:T(8,128)(2,1)S(1)}, bf16[48,512]{1,0:T(8,128)(2,1)S(1)}) custom-call(s32[192]{0:T(256)S(1)} %copy-done.3, s32[1,192]{1,0:T(1,128)S(1)} %bitcast.7, bf16[16032,512]{1,0:T(8,128)(2,1)S(1)} %copy-done.1), custom_call_target="tpu_custom_call" | custom-call | tf_op jit(solution)/shard_map/fetch_rows/pallas_call | solution.py:90
  21.3 3.0 %collective-permute-start = (bf16[48,512]{1,0:T(8,128)(2,1)S(1)}, bf16[48,512]{1,0:T(8,128)(2,1)S(1)}, u32[]{:S(2)}, u32[]{:S(2)}) collective-permute-start(bf16[48,512]{1,0:T(8,128)(2,1)S(1)} %get-tuple-element.15), channel_id=1, source_target_pairs={{0,8},{8,0},{16,24},{24,16},{1,9},{9,1},{17,25},{25,17},{2,10},{10... | collective-permute-start | bytes 147464 | tf_op jit(solution)/shard_map/ppermute | solution.py:19
  24.3 1.5 %collective-permute-start.1 = (bf16[48,512]{1,0:T(8,128)(2,1)S(1)}, bf16[48,512]{1,0:T(8,128)(2,1)S(1)}, u32[]{:S(2)}, u32[]{:S(2)}) collective-permute-start(bf16[48,512]{1,0:T(8,128)(2,1)S(1)} %get-tuple-element.16), channel_id=1, source_target_pairs={{0,16},{8,24},{16,0},{24,8},{1,17},{9,25},{17,1},{25,9},{2,18},{10... | collective-permute-start | bytes 147464 | tf_op jit(solution)/shard_map/ppermute | solution.py:19
  25.8 0.0 collective-permute-start.2
  25.9 0.5 collective-permute-done
  26.4 2.0 %collective-permute-done.1 = bf16[48,512]{1,0:T(8,128)(2,1)S(1)} collective-permute-done((bf16[48,512]{1,0:T(8,128)(2,1)S(1)}, bf16[48,512]{1,0:T(8,128)(2,1)S(1)}, u32[]{:S(2)}, u32[]{:S(2)}) %collective-permute-start.1) | collective-permute-done | bytes 49184 | tf_op jit(solution)/shard_map/ppermute | solution.py:19
  28.4 2.4 %collective-permute-done.2 = bf16[48,512]{1,0:T(8,128)(2,1)S(1)} collective-permute-done((bf16[48,512]{1,0:T(8,128)(2,1)S(1)}, bf16[48,512]{1,0:T(8,128)(2,1)S(1)}, u32[]{:S(2)}, u32[]{:S(2)}) %collective-permute-start.2) | collective-permute-done | bytes 49184 | tf_op jit(solution)/shard_map/ppermute | solution.py:19
  30.8 1.6 %collective-permute-start.3 = (bf16[48,512]{1,0:T(8,128)(2,1)S(1)}, bf16[48,512]{1,0:T(8,128)(2,1)S(1)}, u32[]{:S(2)}, u32[]{:S(2)}) collective-permute-start(bf16[48,512]{1,0:T(8,128)(2,1)S(1)} %add_add_fusion), channel_id=1, source_target_pairs={{0,2},{1,3},{2,0},{3,1},{4,6},{5,7},{6,4},{7,5},{8,10},{9,11},{10,... | collective-permute-start | bytes 147464 | tf_op jit(solution)/shard_map/ppermute | solution.py:19
  32.5 2.6 %collective-permute-start.4 = (bf16[48,512]{1,0:T(8,128)(2,1)S(1)}, bf16[48,512]{1,0:T(8,128)(2,1)S(1)}, u32[]{:S(2)}, u32[]{:S(2)}) collective-permute-start(bf16[48,512]{1,0:T(8,128)(2,1)S(1)} %add_add_fusion), channel_id=1, source_target_pairs={{0,4},{1,5},{2,6},{3,7},{4,0},{5,1},{6,2},{7,3},{8,12},{9,13},{10,... | collective-permute-start | bytes 147464 | tf_op jit(solution)/shard_map/ppermute | solution.py:19
  35.1 0.2 collective-permute-start.5
  35.3 2.5 %collective-permute-done.3 = bf16[48,512]{1,0:T(8,128)(2,1)S(1)} collective-permute-done((bf16[48,512]{1,0:T(8,128)(2,1)S(1)}, bf16[48,512]{1,0:T(8,128)(2,1)S(1)}, u32[]{:S(2)}, u32[]{:S(2)}) %collective-permute-start.3) | collective-permute-done | bytes 49184 | tf_op jit(solution)/shard_map/ppermute | solution.py:19
  37.8 5.1 %collective-permute-done.4 = bf16[48,512]{1,0:T(8,128)(2,1)S(1)} collective-permute-done((bf16[48,512]{1,0:T(8,128)(2,1)S(1)}, bf16[48,512]{1,0:T(8,128)(2,1)S(1)}, u32[]{:S(2)}, u32[]{:S(2)}) %collective-permute-start.4) | collective-permute-done | bytes 49184 | tf_op jit(solution)/shard_map/ppermute | solution.py:19
  42.8 0.0 collective-permute-done.5
  42.9 0.1 collective-permute-start.6
  42.9 0.4 collective-permute-start.7
  43.3 3.1 %collective-permute-start.8 = (bf16[4,48,512]{2,1,0:T(8,128)(2,1)S(1)}, bf16[4,48,512]{2,1,0:T(8,128)(2,1)S(1)}, u32[]{:S(2)}, u32[]{:S(2)}) collective-permute-start(bf16[4,48,512]{2,1,0:T(8,128)(2,1)S(1)} %pad_maximum_fusion.refs_0_), channel_id=1, source_target_pairs={{0,24},{8,16},{16,8},{24,0},{1,25},{9,17},{17,9},{25,1},{2,26},{10... | collective-permute-start | bytes 589832 | tf_op jit(solution)/shard_map/ppermute | solution.py:19
  46.4 0.0 collective-permute-start.9
  46.4 2.2 %collective-permute-done.6.refs_1_ = bf16[4,48,512]{2,1,0:T(8,128)(2,1)S(1)} collective-permute-done((bf16[4,48,512]{2,1,0:T(8,128)(2,1)S(1)}, bf16[4,48,512]{2,1,0:T(8,128)(2,1)S(1)}, u32[]{:S(2)}, u32[]{:S(2)}) %collective-permute-start.6) | collective-permute-done | bytes 196640 | tf_op jit(solution)/shard_map/ppermute | solution.py:19
  48.6 0.0 collective-permute-start.10
  48.6 2.3 %collective-permute-done.7.refs_2_ = bf16[4,48,512]{2,1,0:T(8,128)(2,1)S(1)} collective-permute-done((bf16[4,48,512]{2,1,0:T(8,128)(2,1)S(1)}, bf16[4,48,512]{2,1,0:T(8,128)(2,1)S(1)}, u32[]{:S(2)}, u32[]{:S(2)}) %collective-permute-start.7) | collective-permute-done | bytes 196640 | tf_op jit(solution)/shard_map/ppermute | solution.py:19
  50.9 0.0 collective-permute-start.11
  50.9 0.5 collective-permute-start.12
  51.5 0.0 collective-permute-done.9.refs_4_
  51.5 0.0 collective-permute-done.10.refs_5_
  51.5 0.9 collective-permute-done.11.refs_6_
  52.4 0.5 collective-permute-done.12.refs_7_
  52.9 10.1 %all-gather.2.cloned.1.call-done.refs_11_.refs_6_ = bf16[4096,512]{1,0:T(8,128)(2,1)} async-done(((bf16[512,512]{1,0:T(8,128)(2,1)}), bf16[4096,512]{1,0:T(8,128)(2,1)}) %all-gather.2.cloned.1.call-update) | async-done | bytes 4194320 | tf_op jit(solution)/shard_map/all_gather | solution.py:250
  62.9 9.7 %section_first.1 = (bf16[96,512]{1,0:T(8,128)(2,1)S(1)}, bf16[96,512]{1,0:T(8,128)(2,1)S(1)}, bf16[192,4096]{1,0:T(8,128)(2,1)S(1)}) custom-call(bf16[4,48,512]{2,1,0:T(8,128)(2,1)S(1)} %pad_maximum_fusion.refs_0_, bf16[4,48,512]{2,1,0:T(8,128)(2,1)S(1)} %collective-permute-done.6.refs_1_, bf16[4,48,512]{2,1,0:T(8,128)(2,1)S(1)} %collective-permute-done.7.refs_2_, ...), custom_call_target="tpu_custom_call" | custom-call | flops 3623878656 | bytes 18874368 | tf_op jit(solution)/shard_map/section_first/pallas_call | solution.py:220
  72.6 0.3 collective-permute-start.13
  72.9 1.1 collective-permute-done.13
  74.0 0.1 collective-permute-start.14
  74.1 1.7 %collective-permute-start.15 = (bf16[96,512]{1,0:T(8,128)(2,1)S(1)}, bf16[96,512]{1,0:T(8,128)(2,1)S(1)}, u32[]{:S(2)}, u32[]{:S(2)}) collective-permute-start(bf16[96,512]{1,0:T(8,128)(2,1)S(1)} %add_convert_fusion.4), channel_id=1, source_target_pairs={{0,4},{1,5},{2,6},{3,7},{4,0},{5,1},{6,2},{7,3},{8,12},{9,13},{10,... | collective-permute-start | bytes 294920 | tf_op jit(solution)/shard_map/ppermute | solution.py:19
  75.8 2.7 %collective-permute-start.16 = (bf16[96,512]{1,0:T(8,128)(2,1)S(1)}, bf16[96,512]{1,0:T(8,128)(2,1)S(1)}, u32[]{:S(2)}, u32[]{:S(2)}) collective-permute-start(bf16[96,512]{1,0:T(8,128)(2,1)S(1)} %add_convert_fusion.4), channel_id=1, source_target_pairs={{0,6},{1,7},{2,4},{3,5},{4,2},{5,3},{6,0},{7,1},{8,14},{9,15},{10,... | collective-permute-start | bytes 294920 | tf_op jit(solution)/shard_map/ppermute | solution.py:19
  78.5 1.7 %collective-permute-done.14 = bf16[96,512]{1,0:T(8,128)(2,1)S(1)} collective-permute-done((bf16[96,512]{1,0:T(8,128)(2,1)S(1)}, bf16[96,512]{1,0:T(8,128)(2,1)S(1)}, u32[]{:S(2)}, u32[]{:S(2)}) %collective-permute-start.14) | collective-permute-done | bytes 98336 | tf_op jit(solution)/shard_map/ppermute | solution.py:19
  80.2 4.8 %collective-permute-done.15 = bf16[96,512]{1,0:T(8,128)(2,1)S(1)} collective-permute-done((bf16[96,512]{1,0:T(8,128)(2,1)S(1)}, bf16[96,512]{1,0:T(8,128)(2,1)S(1)}, u32[]{:S(2)}, u32[]{:S(2)}) %collective-permute-start.15) | collective-permute-done | bytes 98336 | tf_op jit(solution)/shard_map/ppermute | solution.py:19
  85.0 0.0 collective-permute-done.16
  85.0 0.1 add_convert_fusion.3
  85.0 1.7 %collective-permute-start.17 = (bf16[96,512]{1,0:T(8,128)(2,1)S(1)}, bf16[96,512]{1,0:T(8,128)(2,1)S(1)}, u32[]{:S(2)}, u32[]{:S(2)}) collective-permute-start(bf16[96,512]{1,0:T(8,128)(2,1)S(1)} %add_convert_fusion.3), channel_id=1, source_target_pairs={{0,8},{8,0},{16,24},{24,16},{1,9},{9,1},{17,25},{25,17},{2,10},{10... | collective-permute-start | bytes 294920 | tf_op jit(solution)/shard_map/ppermute | solution.py:19
  86.7 3.3 %collective-permute-start.18 = (bf16[96,512]{1,0:T(8,128)(2,1)S(1)}, bf16[96,512]{1,0:T(8,128)(2,1)S(1)}, u32[]{:S(2)}, u32[]{:S(2)}) collective-permute-start(bf16[96,512]{1,0:T(8,128)(2,1)S(1)} %add_convert_fusion.3), channel_id=1, source_target_pairs={{0,16},{8,24},{1,17},{9,25},{2,18},{10,26},{3,19},{11,27},{4,20},{... | collective-permute-start | bytes 294920 | tf_op jit(solution)/shard_map/ppermute | solution.py:24
  90.0 1.5 %collective-permute-start.19 = (bf16[96,512]{1,0:T(8,128)(2,1)S(1)}, bf16[96,512]{1,0:T(8,128)(2,1)S(1)}, u32[]{:S(2)}, u32[]{:S(2)}) collective-permute-start(bf16[96,512]{1,0:T(8,128)(2,1)S(1)} %add_convert_fusion.3), channel_id=1, source_target_pairs={{0,24},{8,16},{1,25},{9,17},{2,26},{10,18},{3,27},{11,19},{4,28},{... | collective-permute-start | bytes 294920 | tf_op jit(solution)/shard_map/ppermute | solution.py:24
  91.5 0.0 collective-permute-done.17
  91.5 1.3 collective-permute-done.18
  92.8 0.7 collective-permute-done.19
  93.5 0.1 select_convert_fusion.refs_0_
  93.6 0.1 collective-permute-start.20
  93.6 1.3 collective-permute-done.20.refs_1_
  94.9 2.2 %copy-done = bf16[4096,512]{1,0:T(8,128)(2,1)S(1)} copy-done((bf16[4096,512]{1,0:T(8,128)(2,1)S(1)}, bf16[4096,512]{1,0:T(8,128)(2,1)}, u32[]{:S(2)}) %copy-start) | copy-done | bytes 4194328
  97.1 11.7 %section_next.1 = (bf16[96,512]{1,0:T(8,128)(2,1)S(1)}, bf16[96,512]{1,0:T(8,128)(2,1)S(1)}) custom-call(bf16[96,512]{1,0:T(8,128)(2,1)S(1)} %select_convert_fusion.refs_0_, bf16[96,512]{1,0:T(8,128)(2,1)S(1)} %collective-permute-done.20.refs_1_, bf16[192,4096]{1,0:T(8,128)(2,1)S(1)} %get-tuple-element.20.refs_2_, f32[2,4096]{1,0:T(2,128)S(1)} %copy-done.2, ...), custom_call_target="tpu_custom_call" | custom-call | flops 3623878656 | bytes 18874368 | tf_op jit(solution)/shard_map/section_next/pallas_call | solution.py:220
  108.8 0.2 collective-permute-start.21
  109.0 1.1 collective-permute-done.21
  110.2 2.0 %collective-permute-start.22 = (bf16[96,512]{1,0:T(8,128)(2,1)S(1)}, bf16[96,512]{1,0:T(8,128)(2,1)S(1)}, u32[]{:S(2)}, u32[]{:S(2)}) collective-permute-start(bf16[96,512]{1,0:T(8,128)(2,1)S(1)} %add_convert_fusion.2), channel_id=1, source_target_pairs={{0,2},{1,3},{2,0},{3,1},{4,6},{5,7},{6,4},{7,5},{8,10},{9,11},{10,... | collective-permute-start | bytes 294920 | tf_op jit(solution)/shard_map/ppermute | solution.py:19
  112.2 0.1 collective-permute-start.23
  112.4 2.3 %collective-permute-start.24 = (bf16[96,512]{1,0:T(8,128)(2,1)S(1)}, bf16[96,512]{1,0:T(8,128)(2,1)S(1)}, u32[]{:S(2)}, u32[]{:S(2)}) collective-permute-start(bf16[96,512]{1,0:T(8,128)(2,1)S(1)} %add_convert_fusion.2), channel_id=1, source_target_pairs={{0,6},{1,7},{2,4},{3,5},{4,2},{5,3},{6,0},{7,1},{8,14},{9,15},{10,... | collective-permute-start | bytes 294920 | tf_op jit(solution)/shard_map/ppermute | solution.py:19
  114.7 0.7 collective-permute-done.22
  115.4 7.1 %collective-permute-done.23 = bf16[96,512]{1,0:T(8,128)(2,1)S(1)} collective-permute-done((bf16[96,512]{1,0:T(8,128)(2,1)S(1)}, bf16[96,512]{1,0:T(8,128)(2,1)S(1)}, u32[]{:S(2)}, u32[]{:S(2)}) %collective-permute-start.23) | collective-permute-done | bytes 98336 | tf_op jit(solution)/shard_map/ppermute | solution.py:19
  122.5 0.1 add_convert_fusion.1
  122.6 1.5 %collective-permute-start.25 = (bf16[96,512]{1,0:T(8,128)(2,1)S(1)}, bf16[96,512]{1,0:T(8,128)(2,1)S(1)}, u32[]{:S(2)}, u32[]{:S(2)}) collective-permute-start(bf16[96,512]{1,0:T(8,128)(2,1)S(1)} %add_convert_fusion.1), channel_id=1, source_target_pairs={{0,8},{8,0},{16,24},{24,16},{1,9},{9,1},{17,25},{25,17},{2,10},{10... | collective-permute-start | bytes 294920 | tf_op jit(solution)/shard_map/ppermute | solution.py:19
  124.1 3.2 %collective-permute-done.25 = bf16[96,512]{1,0:T(8,128)(2,1)S(1)} collective-permute-done((bf16[96,512]{1,0:T(8,128)(2,1)S(1)}, bf16[96,512]{1,0:T(8,128)(2,1)S(1)}, u32[]{:S(2)}, u32[]{:S(2)}) %collective-permute-start.25) | collective-permute-done | bytes 98336 | tf_op jit(solution)/shard_map/ppermute | solution.py:19
  127.3 0.1 collective-permute-start.26
  127.4 1.3 collective-permute-done.26
  128.7 0.7 maximum_bitcast_fusion
  (14 shorter events, 0.2 us)
Async XLA Ops:
  6.5 56.4 %all-gather.2.cloned.1.call-start = ((), (), s32[]{:S(2)}) async-start(), calls=%async_computation | async-start | bytes 4718592 | tf_op jit(solution)/shard_map/all_gather | solution.py:250
  7.3 5.7 %copy-start.1 = (bf16[16032,512]{1,0:T(8,128)(2,1)S(1)}, bf16[16032,512]{1,0:T(8,128)(2,1)}, u32[]{:S(2)}) copy-start(bf16[16032,512]{1,0:T(8,128)(2,1)} %table.1) | copy-start | bytes 49250308
  12.9 0.7 copy-start.3
  13.6 49.3 %copy-start.2 = (f32[2,4096]{1,0:T(2,128)S(1)}, f32[2,4096]{1,0:T(2,128)}, u32[]{:S(2)}) copy-start(f32[2,4096]{1,0:T(2,128)} %refs_3_.1) | copy-start | bytes 98308
  21.3 5.1 %collective-permute-start = (bf16[48,512]{1,0:T(8,128)(2,1)S(1)}, bf16[48,512]{1,0:T(8,128)(2,1)S(1)}, u32[]{:S(2)}, u32[]{:S(2)}) collective-permute-start(bf16[48,512]{1,0:T(8,128)(2,1)S(1)} %get-tuple-element.15), channel_id=1, source_target_pairs={{0,8},{8,0},{16,24},{24,16},{1,9},{9,1},{17,25},{25,17},{2,10},{10... | collective-permute-start | bytes 147464 | tf_op jit(solution)/shard_map/ppermute | solution.py:19
  24.3 4.1 %collective-permute-start.1 = (bf16[48,512]{1,0:T(8,128)(2,1)S(1)}, bf16[48,512]{1,0:T(8,128)(2,1)S(1)}, u32[]{:S(2)}, u32[]{:S(2)}) collective-permute-start(bf16[48,512]{1,0:T(8,128)(2,1)S(1)} %get-tuple-element.16), channel_id=1, source_target_pairs={{0,16},{8,24},{16,0},{24,8},{1,17},{9,25},{17,1},{25,9},{2,18},{10... | collective-permute-start | bytes 147464 | tf_op jit(solution)/shard_map/ppermute | solution.py:19
  25.8 5.0 %collective-permute-start.2 = (bf16[48,512]{1,0:T(8,128)(2,1)S(1)}, bf16[48,512]{1,0:T(8,128)(2,1)S(1)}, u32[]{:S(2)}, u32[]{:S(2)}) collective-permute-start(bf16[48,512]{1,0:T(8,128)(2,1)S(1)} %get-tuple-element.17), channel_id=1, source_target_pairs={{0,24},{8,16},{16,8},{24,0},{1,25},{9,17},{17,9},{25,1},{2,26},{10... | collective-permute-start | bytes 147464 | tf_op jit(solution)/shard_map/ppermute | solution.py:19
  30.8 6.9 %collective-permute-start.3 = (bf16[48,512]{1,0:T(8,128)(2,1)S(1)}, bf16[48,512]{1,0:T(8,128)(2,1)S(1)}, u32[]{:S(2)}, u32[]{:S(2)}) collective-permute-start(bf16[48,512]{1,0:T(8,128)(2,1)S(1)} %add_add_fusion), channel_id=1, source_target_pairs={{0,2},{1,3},{2,0},{3,1},{4,6},{5,7},{6,4},{7,5},{8,10},{9,11},{10,... | collective-permute-start | bytes 147464 | tf_op jit(solution)/shard_map/ppermute | solution.py:19
  32.5 10.4 %collective-permute-start.4 = (bf16[48,512]{1,0:T(8,128)(2,1)S(1)}, bf16[48,512]{1,0:T(8,128)(2,1)S(1)}, u32[]{:S(2)}, u32[]{:S(2)}) collective-permute-start(bf16[48,512]{1,0:T(8,128)(2,1)S(1)} %add_add_fusion), channel_id=1, source_target_pairs={{0,4},{1,5},{2,6},{3,7},{4,0},{5,1},{6,2},{7,3},{8,12},{9,13},{10,... | collective-permute-start | bytes 147464 | tf_op jit(solution)/shard_map/ppermute | solution.py:19
  35.1 7.8 %collective-permute-start.5 = (bf16[48,512]{1,0:T(8,128)(2,1)S(1)}, bf16[48,512]{1,0:T(8,128)(2,1)S(1)}, u32[]{:S(2)}, u32[]{:S(2)}) collective-permute-start(bf16[48,512]{1,0:T(8,128)(2,1)S(1)} %add_add_fusion), channel_id=1, source_target_pairs={{0,6},{1,7},{2,4},{3,5},{4,2},{5,3},{6,0},{7,1},{8,14},{9,15},{10,... | collective-permute-start | bytes 147464 | tf_op jit(solution)/shard_map/ppermute | solution.py:19
  42.9 5.7 %collective-permute-start.6 = (bf16[4,48,512]{2,1,0:T(8,128)(2,1)S(1)}, bf16[4,48,512]{2,1,0:T(8,128)(2,1)S(1)}, u32[]{:S(2)}, u32[]{:S(2)}) collective-permute-start(bf16[4,48,512]{2,1,0:T(8,128)(2,1)S(1)} %pad_maximum_fusion.refs_0_), channel_id=1, source_target_pairs={{0,8},{8,0},{16,24},{24,16},{1,9},{9,1},{17,25},{25,17},{2,10},{10... | collective-permute-start | bytes 589832 | tf_op jit(solution)/shard_map/ppermute | solution.py:19
  42.9 8.0 %collective-permute-start.7 = (bf16[4,48,512]{2,1,0:T(8,128)(2,1)S(1)}, bf16[4,48,512]{2,1,0:T(8,128)(2,1)S(1)}, u32[]{:S(2)}, u32[]{:S(2)}) collective-permute-start(bf16[4,48,512]{2,1,0:T(8,128)(2,1)S(1)} %pad_maximum_fusion.refs_0_), channel_id=1, source_target_pairs={{0,16},{8,24},{16,0},{24,8},{1,17},{9,25},{17,1},{25,9},{2,18},{10... | collective-permute-start | bytes 589832 | tf_op jit(solution)/shard_map/ppermute | solution.py:19
  43.3 7.6 %collective-permute-start.8 = (bf16[4,48,512]{2,1,0:T(8,128)(2,1)S(1)}, bf16[4,48,512]{2,1,0:T(8,128)(2,1)S(1)}, u32[]{:S(2)}, u32[]{:S(2)}) collective-permute-start(bf16[4,48,512]{2,1,0:T(8,128)(2,1)S(1)} %pad_maximum_fusion.refs_0_), channel_id=1, source_target_pairs={{0,24},{8,16},{16,8},{24,0},{1,25},{9,17},{17,9},{25,1},{2,26},{10... | collective-permute-start | bytes 589832 | tf_op jit(solution)/shard_map/ppermute | solution.py:19
  46.4 5.0 %collective-permute-start.9 = (bf16[4,48,512]{2,1,0:T(8,128)(2,1)S(1)}, bf16[4,48,512]{2,1,0:T(8,128)(2,1)S(1)}, u32[]{:S(2)}, u32[]{:S(2)}) collective-permute-start(bf16[4,48,512]{2,1,0:T(8,128)(2,1)S(1)} %pad_maximum_fusion.refs_0_), channel_id=1, source_target_pairs={{0,1},{1,0},{2,3},{3,2},{4,5},{5,4},{6,7},{7,6},{8,9},{9,8},{10,11... | collective-permute-start | bytes 589832 | tf_op jit(solution)/shard_map/ppermute | solution.py:19
  48.6 2.9 %collective-permute-start.10 = (bf16[4,48,512]{2,1,0:T(8,128)(2,1)S(1)}, bf16[4,48,512]{2,1,0:T(8,128)(2,1)S(1)}, u32[]{:S(2)}, u32[]{:S(2)}) collective-permute-start(bf16[4,48,512]{2,1,0:T(8,128)(2,1)S(1)} %collective-permute-done.6.refs_1_), channel_id=1, source_target_pairs={{0,1},{1,0},{2,3},{3,2},{4,5},{5,4},{6,7},{7,6},{8,9},{9,8},{10,11... | collective-permute-start | bytes 589832 | tf_op jit(solution)/shard_map/ppermute | solution.py:19
  50.9 1.4 %collective-permute-start.11 = (bf16[4,48,512]{2,1,0:T(8,128)(2,1)S(1)}, bf16[4,48,512]{2,1,0:T(8,128)(2,1)S(1)}, u32[]{:S(2)}, u32[]{:S(2)}) collective-permute-start(bf16[4,48,512]{2,1,0:T(8,128)(2,1)S(1)} %collective-permute-done.7.refs_2_), channel_id=1, source_target_pairs={{0,1},{1,0},{2,3},{3,2},{4,5},{5,4},{6,7},{7,6},{8,9},{9,8},{10,11... | collective-permute-start | bytes 589832 | tf_op jit(solution)/shard_map/ppermute | solution.py:19
  50.9 1.9 %collective-permute-start.12 = (bf16[4,48,512]{2,1,0:T(8,128)(2,1)S(1)}, bf16[4,48,512]{2,1,0:T(8,128)(2,1)S(1)}, u32[]{:S(2)}, u32[]{:S(2)}) collective-permute-start(bf16[4,48,512]{2,1,0:T(8,128)(2,1)S(1)} %collective-permute-done.8.refs_3_), channel_id=1, source_target_pairs={{0,1},{1,0},{2,3},{3,2},{4,5},{5,4},{6,7},{7,6},{8,9},{9,8},{10,11... | collective-permute-start | bytes 589832 | tf_op jit(solution)/shard_map/ppermute | solution.py:19
  72.6 1.4 %collective-permute-start.13 = (bf16[96,512]{1,0:T(8,128)(2,1)S(1)}, bf16[96,512]{1,0:T(8,128)(2,1)S(1)}, u32[]{:S(2)}, u32[]{:S(2)}) collective-permute-start(bf16[96,512]{1,0:T(8,128)(2,1)S(1)} %get-tuple-element.19), channel_id=1, source_target_pairs={{0,1},{1,0},{2,3},{3,2},{4,5},{5,4},{6,7},{7,6},{8,9},{9,8},{10,11... | collective-permute-start | bytes 294920 | tf_op jit(solution)/shard_map/ppermute | solution.py:19
  74.0 6.2 %collective-permute-start.14 = (bf16[96,512]{1,0:T(8,128)(2,1)S(1)}, bf16[96,512]{1,0:T(8,128)(2,1)S(1)}, u32[]{:S(2)}, u32[]{:S(2)}) collective-permute-start(bf16[96,512]{1,0:T(8,128)(2,1)S(1)} %add_convert_fusion.4), channel_id=1, source_target_pairs={{0,2},{1,3},{2,0},{3,1},{4,6},{5,7},{6,4},{7,5},{8,10},{9,11},{10,... | collective-permute-start | bytes 294920 | tf_op jit(solution)/shard_map/ppermute | solution.py:19
  74.1 10.9 %collective-permute-start.15 = (bf16[96,512]{1,0:T(8,128)(2,1)S(1)}, bf16[96,512]{1,0:T(8,128)(2,1)S(1)}, u32[]{:S(2)}, u32[]{:S(2)}) collective-permute-start(bf16[96,512]{1,0:T(8,128)(2,1)S(1)} %add_convert_fusion.4), channel_id=1, source_target_pairs={{0,4},{1,5},{2,6},{3,7},{4,0},{5,1},{6,2},{7,3},{8,12},{9,13},{10,... | collective-permute-start | bytes 294920 | tf_op jit(solution)/shard_map/ppermute | solution.py:19
  75.8 9.1 %collective-permute-start.16 = (bf16[96,512]{1,0:T(8,128)(2,1)S(1)}, bf16[96,512]{1,0:T(8,128)(2,1)S(1)}, u32[]{:S(2)}, u32[]{:S(2)}) collective-permute-start(bf16[96,512]{1,0:T(8,128)(2,1)S(1)} %add_convert_fusion.4), channel_id=1, source_target_pairs={{0,6},{1,7},{2,4},{3,5},{4,2},{5,3},{6,0},{7,1},{8,14},{9,15},{10,... | collective-permute-start | bytes 294920 | tf_op jit(solution)/shard_map/ppermute | solution.py:19
  85.0 6.5 %collective-permute-start.17 = (bf16[96,512]{1,0:T(8,128)(2,1)S(1)}, bf16[96,512]{1,0:T(8,128)(2,1)S(1)}, u32[]{:S(2)}, u32[]{:S(2)}) collective-permute-start(bf16[96,512]{1,0:T(8,128)(2,1)S(1)} %add_convert_fusion.3), channel_id=1, source_target_pairs={{0,8},{8,0},{16,24},{24,16},{1,9},{9,1},{17,25},{25,17},{2,10},{10... | collective-permute-start | bytes 294920 | tf_op jit(solution)/shard_map/ppermute | solution.py:19
  86.7 6.1 %collective-permute-start.18 = (bf16[96,512]{1,0:T(8,128)(2,1)S(1)}, bf16[96,512]{1,0:T(8,128)(2,1)S(1)}, u32[]{:S(2)}, u32[]{:S(2)}) collective-permute-start(bf16[96,512]{1,0:T(8,128)(2,1)S(1)} %add_convert_fusion.3), channel_id=1, source_target_pairs={{0,16},{8,24},{1,17},{9,25},{2,18},{10,26},{3,19},{11,27},{4,20},{... | collective-permute-start | bytes 294920 | tf_op jit(solution)/shard_map/ppermute | solution.py:24
  90.0 3.5 %collective-permute-start.19 = (bf16[96,512]{1,0:T(8,128)(2,1)S(1)}, bf16[96,512]{1,0:T(8,128)(2,1)S(1)}, u32[]{:S(2)}, u32[]{:S(2)}) collective-permute-start(bf16[96,512]{1,0:T(8,128)(2,1)S(1)} %add_convert_fusion.3), channel_id=1, source_target_pairs={{0,24},{8,16},{1,25},{9,17},{2,26},{10,18},{3,27},{11,19},{4,28},{... | collective-permute-start | bytes 294920 | tf_op jit(solution)/shard_map/ppermute | solution.py:24
  93.6 1.4 %collective-permute-start.20 = (bf16[96,512]{1,0:T(8,128)(2,1)S(1)}, bf16[96,512]{1,0:T(8,128)(2,1)S(1)}, u32[]{:S(2)}, u32[]{:S(2)}) collective-permute-start(bf16[96,512]{1,0:T(8,128)(2,1)S(1)} %select_convert_fusion.refs_0_), channel_id=1, source_target_pairs={{0,1},{1,0},{2,3},{3,2},{4,5},{5,4},{6,7},{7,6},{8,9},{9,8},{10,11... | collective-permute-start | bytes 294920 | tf_op jit(solution)/shard_map/ppermute | solution.py:19
  94.9 2.2 %copy-start = (bf16[4096,512]{1,0:T(8,128)(2,1)S(1)}, bf16[4096,512]{1,0:T(8,128)(2,1)}, u32[]{:S(2)}) copy-start(bf16[4096,512]{1,0:T(8,128)(2,1)} %all-gather.2.cloned.1.call-done.refs_11_.refs_6_) | copy-start | bytes 12582916
  108.8 1.4 %collective-permute-start.21 = (bf16[96,512]{1,0:T(8,128)(2,1)S(1)}, bf16[96,512]{1,0:T(8,128)(2,1)S(1)}, u32[]{:S(2)}, u32[]{:S(2)}) collective-permute-start(bf16[96,512]{1,0:T(8,128)(2,1)S(1)} %get-tuple-element.22), channel_id=1, source_target_pairs={{0,1},{1,0},{2,3},{3,2},{4,5},{5,4},{6,7},{7,6},{8,9},{9,8},{10,11... | collective-permute-start | bytes 294920 | tf_op jit(solution)/shard_map/ppermute | solution.py:19
  110.2 5.2 %collective-permute-start.22 = (bf16[96,512]{1,0:T(8,128)(2,1)S(1)}, bf16[96,512]{1,0:T(8,128)(2,1)S(1)}, u32[]{:S(2)}, u32[]{:S(2)}) collective-permute-start(bf16[96,512]{1,0:T(8,128)(2,1)S(1)} %add_convert_fusion.2), channel_id=1, source_target_pairs={{0,2},{1,3},{2,0},{3,1},{4,6},{5,7},{6,4},{7,5},{8,10},{9,11},{10,... | collective-permute-start | bytes 294920 | tf_op jit(solution)/shard_map/ppermute | solution.py:19
  112.2 10.3 %collective-permute-start.23 = (bf16[96,512]{1,0:T(8,128)(2,1)S(1)}, bf16[96,512]{1,0:T(8,128)(2,1)S(1)}, u32[]{:S(2)}, u32[]{:S(2)}) collective-permute-start(bf16[96,512]{1,0:T(8,128)(2,1)S(1)} %add_convert_fusion.2), channel_id=1, source_target_pairs={{0,4},{1,5},{2,6},{3,7},{4,0},{5,1},{6,2},{7,3},{8,12},{9,13},{10,... | collective-permute-start | bytes 294920 | tf_op jit(solution)/shard_map/ppermute | solution.py:19
  112.4 10.1 %collective-permute-start.24 = (bf16[96,512]{1,0:T(8,128)(2,1)S(1)}, bf16[96,512]{1,0:T(8,128)(2,1)S(1)}, u32[]{:S(2)}, u32[]{:S(2)}) collective-permute-start(bf16[96,512]{1,0:T(8,128)(2,1)S(1)} %add_convert_fusion.2), channel_id=1, source_target_pairs={{0,6},{1,7},{2,4},{3,5},{4,2},{5,3},{6,0},{7,1},{8,14},{9,15},{10,... | collective-permute-start | bytes 294920 | tf_op jit(solution)/shard_map/ppermute | solution.py:19
  122.6 4.7 %collective-permute-start.25 = (bf16[96,512]{1,0:T(8,128)(2,1)S(1)}, bf16[96,512]{1,0:T(8,128)(2,1)S(1)}, u32[]{:S(2)}, u32[]{:S(2)}) collective-permute-start(bf16[96,512]{1,0:T(8,128)(2,1)S(1)} %add_convert_fusion.1), channel_id=1, source_target_pairs={{0,8},{8,0},{16,24},{24,16},{1,9},{9,1},{17,25},{25,17},{2,10},{10... | collective-permute-start | bytes 294920 | tf_op jit(solution)/shard_map/ppermute | solution.py:19
  127.3 1.4 %collective-permute-start.26 = (bf16[96,512]{1,0:T(8,128)(2,1)S(1)}, bf16[96,512]{1,0:T(8,128)(2,1)S(1)}, u32[]{:S(2)}, u32[]{:S(2)}) collective-permute-start(bf16[96,512]{1,0:T(8,128)(2,1)S(1)} %add_convert_fusion), channel_id=1, source_target_pairs={{0,1},{1,0},{2,3},{3,2},{4,5},{5,4},{6,7},{7,6},{8,9},{9,8},{10,11... | collective-permute-start | bytes 294920 | tf_op jit(solution)/shard_map/ppermute | solution.py:19
Sparse Core Ops, SparseCore 0:
  9.0 53.9 all-gather.1

commit v2 on v1

v2 whole, which is shorter than its diff:
```python
import functools

import jax
import jax.numpy as jnp
from jax import lax
from jax.experimental import pallas as pl
from jax.experimental.pallas import tpu as pltpu
from jax.sharding import PartitionSpec as P

EPSILON = 1e-05
GROUP = 4
TILE = 16
PARTS = 8
CHUNK = 512
F32 = jnp.float32
BF16 = jnp.bfloat16


def swap(value, axis, mask):
    return lax.ppermute(value, axis, [(i, i ^ mask) for i in range(lax.axis_size(axis))])


def onward(value, flip):
    size = lax.axis_size("segment")
    return lax.ppermute(value, "segment", [(i, (i ^ flip) + 2) for i in range(size - 2)])


def tree_sum(values):
    while len(values) > 1:
        values = [values[i] + values[i + 1] for i in range(0, len(values), 2)]
    return values[0]


def split_copies(source, target, sems):
    rows = source.shape[0]
    parts = max(p for p in range(1, PARTS + 1) if rows % (TILE * p) == 0)
    size = rows // parts
    return [
        pltpu.make_async_copy(
            source.at[pl.ds(k * size, size), :], target.at[pl.ds(k * size, size), :], sems.at[k]
        )
        for k in range(parts)
    ]


def fetch_kernel(block_rows, vocab, tokens_smem, tokens_row, table, gate, down, *refs):
    outs, (near_gate, near_down, buffer, sems, weight_sems) = refs[:GROUP], refs[GROUP:]
    weights = split_copies(gate.at[0], near_gate, weight_sems.at[0])
    weights += split_copies(down.at[0], near_down, weight_sems.at[1])
    segment = lax.axis_index("segment")
    low = segment * vocab
    count = GROUP * block_rows

    def held(i):
        local = tokens_smem[i] - low
        return local, (local >= 0) & (local < vocab)

    def copy(i, local):
        first = pl.multiple_of((local // TILE) * TILE, TILE)
        place = pl.multiple_of(i * TILE, TILE)
        return pltpu.make_async_copy(
            table.at[pl.ds(first, TILE), :], buffer.at[pl.ds(place, TILE), :], sems.at[i]
        )

    def start(i, carry):
        local, here = held(i)

        @pl.when(here)
        def _():
            copy(i, local).start()

        return carry

    def finish(i, carry):
        local, here = held(i)

        @pl.when(here)
        def _():
            copy(i, local).wait()

        return carry

    buffer[...] = jnp.zeros_like(buffer)
    lax.fori_loop(0, count, start, 0, unroll=8)
    for weight in weights:
        weight.start()
    wanted = tokens_row[...] - low
    inside = (wanted >= 0) & (wanted < vocab)
    code = jnp.where(inside, lax.rem(wanted, TILE), TILE)
    rows = lax.broadcasted_iota(jnp.int32, (count, count), 0)
    columns = lax.broadcasted_iota(jnp.int32, (count, count), 1)
    code_column = jnp.sum(jnp.where(rows == columns, code, 0), axis=1, keepdims=True)
    lax.fori_loop(0, count, finish, 0, unroll=8)
    home = lax.rem(segment, GROUP)
    wide = block_rows * TILE
    row_of = lax.broadcasted_iota(jnp.int32, (block_rows, wide), 0)
    lane_of = lax.broadcasted_iota(jnp.int32, (block_rows, wide), 1)
    results = []
    for block in range(GROUP):
        code_block = code_column[block * block_rows : (block + 1) * block_rows]
        hot = (lane_of == row_of * TILE + code_block) & (code_block < TILE)
        hot = jnp.where(hot, 1.0, 0.0).astype(BF16)
        results.append(
            jnp.dot(
                hot, buffer[block * wide : (block + 1) * wide, :], preferred_element_type=F32
            ).astype(BF16)
        )
    for block in range(GROUP):
        for mask in range(GROUP):

            @pl.when(jnp.bitwise_xor(home, mask) == block)
            def _(block=block, mask=mask):
                outs[mask][...] = results[block]
    for weight in weights:
        weight.wait()


def load_kernel(gate, down, near_gate, near_down, sems):
    copies = split_copies(gate.at[0], near_gate, sems.at[0]) + split_copies(down.at[0], near_down, sems.at[1])
    for copy in copies:
        copy.start()
    for copy in copies:
        copy.wait()


def fetch_rows(tokens, embedding, gate, down):
    vocab, features = embedding.shape
    block_rows = tokens.shape[0] // GROUP
    vmem = pl.BlockSpec(memory_space=pltpu.VMEM)
    anywhere = pl.BlockSpec(memory_space=pl.ANY)
    near = [pltpu.VMEM(gate.shape[1:], BF16), pltpu.VMEM(down.shape[1:], BF16)]
    weight_sems = pltpu.SemaphoreType.DMA((2, PARTS))
    params = pltpu.CompilerParams(vmem_limit_bytes=36 * 2**20)
    if vocab % TILE:
        segment = lax.axis_index("segment")
        local = tokens - segment * vocab
        inside = (local >= 0) & (local < vocab)
        picked = jnp.take(embedding, jnp.clip(local, 0, vocab - 1), axis=0)
        picked = jnp.where(inside[:, None], picked, jnp.zeros_like(picked))
        picked = picked.reshape(GROUP, block_rows, features)
        home = segment % GROUP
        blocks = [lax.dynamic_index_in_dim(picked, home ^ m, 0, False) for m in range(GROUP)]
        near = pl.pallas_call(
            load_kernel,
            out_shape=near,
            in_specs=[anywhere] * 2,
            out_specs=[vmem] * 2,
            scratch_shapes=[weight_sems],
            compiler_params=params,
            name="load_weights",
        )(gate, down)
        return blocks, *near
    *blocks, near_gate, near_down = pl.pallas_call(
        functools.partial(fetch_kernel, block_rows, vocab),
        out_shape=[jax.ShapeDtypeStruct((block_rows, features), BF16)] * GROUP + near,
        in_specs=[pl.BlockSpec(memory_space=pltpu.SMEM), vmem] + [anywhere] * 3,
        out_specs=[vmem] * (GROUP + 2),
        scratch_shapes=[
            pltpu.VMEM((tokens.shape[0] * TILE, features), BF16),
            pltpu.SemaphoreType.DMA((tokens.shape[0],)),
            weight_sems,
        ],
        compiler_params=params,
        name="fetch_rows",
    )(tokens, tokens.reshape(1, -1), embedding, gate, down)
    return blocks, near_gate, near_down


def position(chips):
    place = lax.axis_index("tensor")
    segment = lax.axis_index("segment")
    core = lax.rem(place, 2)
    chip = place // 2

    def share(side, turn):
        return jnp.bitwise_xor(chip, turn) * 2 + jnp.bitwise_xor(core, side)

    return segment, place, core, share


def first_kernel(chips, *refs):
    pieces, refs = refs[: 2 * GROUP], refs[2 * GROUP :]
    gain, gate, down, partial, embedded, total, norms = refs
    tokens, width = embedded.shape
    segment, place, core, share = position(chips)
    features = width // (2 * chips)
    rows = tokens // GROUP
    home = lax.rem(segment, GROUP)
    chunks = width // CHUNK
    for side in range(2):
        for turn in range(chips):
            column = pl.multiple_of(share(side, turn) * features, features)
            for block in range(GROUP):
                row = pl.multiple_of(jnp.bitwise_xor(home, block) * rows, rows)
                embedded[pl.ds(row, rows), pl.ds(column, features)] = pieces[side * GROUP + block][turn]
    gain_row = gain[pl.ds(segment // 2, 1), :]
    squares = jnp.zeros((tokens, 1), F32)
    for k in range(chunks):
        span = slice(k * CHUNK, (k + 1) * CHUNK)
        wide = embedded[:, span].astype(F32)
        squares = squares + jnp.sum(wide * wide, axis=1, keepdims=True)
        scaled = (wide * gain_row[:, span]).astype(BF16)
        product = jnp.dot(scaled, gate[span, :], preferred_element_type=F32)
        total[...] = product if k == 0 else total[...] + product
    norms[...] = squares

    @pl.when(segment < 2)
    def _():
        inverse_norm = lax.rsqrt(squares / width + EPSILON)
        activation = jax.nn.silu(total[...] * inverse_norm).astype(BF16)
        for k in range(chunks):
            span = slice(k * CHUNK, (k + 1) * CHUNK)
            product = jnp.dot(activation, down[:, span], preferred_element_type=F32)
            partial[:, span] = product.astype(BF16)


def halves(projected, core, own, send):
    half = projected.shape[0] // 2
    own[...] = projected[pl.ds(pl.multiple_of(core * half, half), half), :].astype(BF16)
    send[...] = projected[pl.ds(pl.multiple_of((1 - core) * half, half), half), :].astype(BF16)


def project_kernel(chips, *refs):
    shares, refs = refs[: 2 * GROUP + 2], refs[2 * GROUP + 2 :]
    partial, embedded, own, send, bases, seen, high, low, projected, square = refs
    width, rank = bases.shape
    segment, place, core, share = position(chips)
    features = width // (2 * chips)
    part = features // GROUP
    home = lax.rem(segment, GROUP)
    chunks = width // CHUNK
    for side in range(2):
        for turn in range(chips):
            for block in range(GROUP):
                row = share(side, turn) * features + jnp.bitwise_xor(home, block) * part
                piece, index = side * (GROUP + 1) + block, turn
                if block == GROUP - 1 and turn >= chips // 2:
                    piece, index = piece + 1, turn - chips // 2
                bases[pl.ds(pl.multiple_of(row, part), part), :] = shares[piece][index]

    @pl.when(segment < 2)
    def _():
        for k in range(chunks):
            span = slice(k * CHUNK, (k + 1) * CHUNK)
            product = jnp.dot(partial[:, span], bases[span, :], preferred_element_type=F32)
            projected[...] = product if k == 0 else projected[...] + product
        halves(projected, core, own, send)

    @pl.when(segment >= 2)
    def _():
        for k in range(chunks):
            span = slice(k * CHUNK, (k + 1) * CHUNK)
            table = bases[span, :]
            turned = table.astype(F32).T.astype(BF16)
            products = jnp.dot(turned, table, preferred_element_type=F32)
            product = jnp.dot(embedded[:, span], table, preferred_element_type=F32)
            square[...] = products if k == 0 else square[...] + products
            seen[...] = product if k == 0 else seen[...] + product
        coarse = square[...].astype(BF16)
        high[...] = coarse
        low[...] = (square[...] - coarse.astype(F32)).astype(BF16)


def enter_kernel(chips, after, bases, gain, gate, through, into, into_sum):
    segment, place, core, share = position(chips)
    through[...] = after[...]

    @pl.when(segment >= 2)
    def _():
        gain_row = gain[pl.ds(segment // 2, 1), :]
        for k in range(bases.shape[0] // CHUNK):
            span = slice(k * CHUNK, (k + 1) * CHUNK)
            turned = (bases[span, :].astype(F32).T * gain_row[:, span]).astype(BF16)
            product = jnp.dot(turned, gate[span, :], preferred_element_type=F32)
            into_sum[...] = product if k == 0 else into_sum[...] + product
        into[...] = into_sum[...].astype(BF16)


def leave_kernel(chips, after, bases, down, through, out, out_sum):
    segment, place, core, share = position(chips)
    through[...] = after[...]

    @pl.when(segment >= 2)
    def _():
        for k in range(bases.shape[0] // CHUNK):
            span = slice(k * CHUNK, (k + 1) * CHUNK)
            product = jnp.dot(down[:, span], bases[span, :], preferred_element_type=F32)
            out_sum[...] = product if k == 0 else out_sum[...] + product
        out[...] = out_sum[...].astype(BF16)


def sum_kernel(chips, *refs):
    *terms, total = refs
    total[...] = tree_sum([term[...].astype(F32) for term in terms]).astype(BF16)


def hand_kernel(step, chips, half_sum, partner, straight, crossed, result):
    @pl.when(lax.axis_index("segment") // 2 <= step)
    def _():
        result[...] = (half_sum[...].astype(F32) + partner[...].astype(F32)).astype(BF16)

    @pl.when(lax.axis_index("segment") // 2 > step)
    def _():
        result[...] = (straight[...].astype(F32) + crossed[...].astype(F32)).astype(BF16)


def collect_kernel(chips, *refs):
    *pairs, collected = refs
    half = collected.shape[1] // 2
    segment, place, core, share = position(chips)
    for section in range(len(pairs) // 2):

        @pl.when(segment // 2 == section)
        def _(section=section):
            collected[0, pl.ds(pl.multiple_of(core * half, half), half), :] = pairs[2 * section][...]
            collected[0, pl.ds(pl.multiple_of((1 - core) * half, half), half), :] = pairs[2 * section + 1][...]


def next_kernel(width, chips, *refs):
    half_own, half_other, total, norms, seen, high, low, into, out, own, send, projected = refs
    segment, place, core, share = position(chips)
    upper = jnp.where(core == 0, half_own[...], half_other[...])
    lower = jnp.where(core == 0, half_other[...], half_own[...])
    received = jnp.concatenate([upper, lower], axis=0)
    rebuilt = jnp.dot(received, high[...], preferred_element_type=F32) + jnp.dot(
        received, low[...], preferred_element_type=F32
    )
    cross = received.astype(F32) * (2.0 * seen[...] + rebuilt)
    squares = norms[...] + jnp.sum(cross, axis=1, keepdims=True)
    inverse_norm = lax.rsqrt(jnp.maximum(squares, 0.0) / width + EPSILON)
    gated = total[...] + jnp.dot(received, into[...], preferred_element_type=F32)
    activation = jax.nn.silu(gated * inverse_norm).astype(BF16)
    product = jnp.dot(activation, out[...], preferred_element_type=F32)
    alone = (lax.rem(segment, 2) == 0) & (place == 0)
    projected[...] = product + jnp.where(alone, rebuilt, jnp.zeros_like(rebuilt))
    halves(projected, core, own, send)


def kernel_call(kernel, name, inputs, outs, scratch, flops, vmem_limit=14):
    vmem = pl.BlockSpec(memory_space=pltpu.VMEM)
    return pl.pallas_call(
        functools.partial(kernel, lax.axis_size("tensor") // 2),
        out_shape=outs,
        in_specs=[vmem] * len(inputs),
        out_specs=[vmem] * len(outs),
        scratch_shapes=scratch,
        compiler_params=pltpu.CompilerParams(vmem_limit_bytes=vmem_limit * 2**20),
        cost_estimate=pl.CostEstimate(flops=flops, bytes_accessed=0, transcendentals=0),
        name=name,
    )(*inputs)


def add(terms):
    (total,) = kernel_call(sum_kernel, "add", terms, [jax.ShapeDtypeStruct(terms[0].shape, BF16)], [], 0, 2)
    return total


def per_device(tokens, embedding, gain, gate_weight, down_weight, basis):
    segments = lax.axis_size("segment")
    chips = lax.axis_size("tensor") // 2
    sections = segments // 2
    count = tokens.shape[0]
    rank = basis.shape[1]
    width, hidden = gate_weight.shape[1:]

    home = lax.axis_index("segment") % GROUP
    part = basis.shape[0] // GROUP
    quarter = lax.dynamic_slice_in_dim(basis, home * part, part, 0)
    bands = [quarter] + [swap(quarter, "tensor", 2 * m) for m in range(1, chips)]
    blocks, gate, down = fetch_rows(tokens, embedding, gate_weight, down_weight)
    blocks, bands = lax.optimization_barrier((blocks, bands))
    bands = jnp.stack(bands)
    mask = GROUP
    while mask < segments:
        blocks = [block + swap(block, "segment", mask) for block in blocks]
        mask *= 2
    complete = tree_sum(
        [block if m == 0 else swap(block, "segment", m) for m, block in enumerate(blocks)]
    )
    complete, bands = lax.optimization_barrier((complete, bands))
    shares = [bands] + [swap(bands, "segment", m) for m in range(1, GROUP - 1)]
    along = jnp.stack([complete] + [swap(complete, "tensor", 2 * m) for m in range(1, chips)])
    along, shares = lax.optimization_barrier((along, shares))
    mine = [along] + [swap(along, "segment", m) for m in range(1, GROUP)]
    mine[GROUP - 1], shares = lax.optimization_barrier((mine[GROUP - 1], shares))
    shares += [swap(shares[1][: chips // 2], "segment", 2), swap(shares[2][chips // 2 :], "segment", 1)]
    theirs = [swap(piece, "tensor", 1) for piece in mine]
    work = 2 * count * width
    partial, embedded, total, norms = kernel_call(
        first_kernel,
        "section_first",
        mine + theirs + [gain, gate, down],
        [
            pltpu.VMEM((count, width), BF16),
            pltpu.VMEM((count, width), BF16),
            pltpu.VMEM((count, hidden), F32),
            pltpu.VMEM((count, 1), F32),
        ],
        [],
        2 * work * hidden,
    )
    partial, shares[GROUP - 1], shares[GROUP] = lax.optimization_barrier(
        (partial, shares[GROUP - 1], shares[GROUP])
    )
    shares = shares + [swap(piece, "tensor", 1) for piece in shares]
    half_shape = jax.ShapeDtypeStruct((count // 2, rank), BF16)
    own, send, bases, *products = kernel_call(
        project_kernel,
        "project_first",
        shares + [partial, embedded],
        [
            half_shape,
            half_shape,
            pltpu.VMEM((width, rank), BF16),
            pltpu.VMEM((count, rank), F32),
            pltpu.VMEM((rank, rank), BF16),
            pltpu.VMEM((rank, rank), BF16),
        ],
        [pltpu.VMEM((count, rank), F32), pltpu.VMEM((rank, rank), F32)],
        work * rank,
    )

    kept = []
    for step in range(sections):
        if step > 0:
            own, send = kernel_call(
                functools.partial(next_kernel, width),
                "section_next",
                [*received, total, norms, *products],
                [half_shape, half_shape],
                [pltpu.VMEM((count, rank), F32)],
                4 * count * rank * (hidden + rank),
            )
        chip_sum = add([own, swap(send, "tensor", 1)])
        terms = [chip_sum] + [swap(chip_sum, "tensor", 2 * m) for m in range(1, chips)]
        if step == 0:
            terms[0], into = kernel_call(
                enter_kernel,
                "enter",
                [chip_sum, bases, gain, gate],
                [half_shape, pltpu.VMEM((rank, hidden), BF16)],
                [pltpu.VMEM((rank, hidden), F32)],
                2 * hidden * width * rank,
            )
        half_sum = add(terms)
        partner = swap(half_sum, "segment", 1)
        if step + 1 < sections:
            straight, crossed = onward(half_sum, 0), onward(half_sum, 1)
            if step == 0:
                half_sum, out = kernel_call(
                    leave_kernel,
                    "leave",
                    [half_sum, bases, down],
                    [half_shape, pltpu.VMEM((hidden, rank), BF16)],
                    [pltpu.VMEM((hidden, rank), F32)],
                    2 * hidden * width * rank,
                )
                products += [into, out]
            (result,) = kernel_call(
                functools.partial(hand_kernel, step),
                "hand",
                [half_sum, partner, straight, crossed],
                [half_shape],
                [],
                0,
                2,
            )
        else:
            result = add([half_sum, partner])
        received = (result, swap(result, "tensor", 1))
        kept += received
    (collected,) = kernel_call(
        collect_kernel, "collect", kept, [jax.ShapeDtypeStruct((1, count, rank), BF16)], [], 0, 2
    )
    return collected


def solution(mesh):
    placed = (
        P(),
        P("segment", "tensor"),
        P(),
        P("segment", None, "tensor"),
        P("segment", "tensor", None),
        P("tensor", None),
    )
    return jax.shard_map(
        per_device, mesh=mesh, in_specs=placed, out_specs=P("segment", None, None), check_vma=False
    )
```

time: 138 us -> 108 us (0.78)
  between operations: 13.6 us -> 0.18 us
  Pallas kernels: 29.1 us -> 16.7 us
  starting transfers between devices: 30.6 us -> 41.9 us
  local copies, waits for them, and re-layouts: 8.53 us -> 1.77 us
  waiting for transfers between devices: 53.4 us -> 46.8 us
    pallas_call x2 -> x12, Pallas kernels: 21.4 us -> 7.17 us  [kernel_call(): pl.pallas_call(functools.partial(kernel, lax.axis_size('tensor') // 2), o...]
    all_gather x1 -> x0, waiting for transfers between devices: 10.1 us -> none  [per_device(): whole_basis = lax.all_gather(basis, 'tensor', axis=0, tiled=True)]
    ppermute x25 -> x37, starting transfers between devices: 25.8 us -> 35 us  [swap(): lax.ppermute(value, axis, [(i, i ^ mask) for i in range(lax.axis_size(axi...]
    unnamed x8, local copies, waits for them, and re-layouts: 8.53 us -> 1.73 us
    ppermute x25 -> x37, waiting for transfers between devices: 40.7 us -> 45 us  [swap(): lax.ppermute(value, axis, [(i, i ^ mask) for i in range(lax.axis_size(axi...]
    ppermute x2, starting transfers between devices: 4.76 us -> 6.93 us  [onward(): lax.ppermute(value, 'segment', [(i, (i ^ flip) + 2) for i in range(size -...]
    pallas_call x1, Pallas kernels: 7.7 us -> 9.58 us  [fetch_rows(): pl.pallas_call(functools.partial(fetch_kernel, block_rows, vocab), out_sh...]
  transfers between devices with their start and end apart: 28 -> 39, of which waited for: 21 -> 26; matrix products, arithmetic and copies ran while one was open for 0% -> 0% of each run, Pallas kernels for 6% -> 13%
where the time goes in v2:
time: 108 us
  waiting for transfers between devices  46.8 us (43%)
  starting transfers between devices  41.9 us (39%)
  Pallas kernels  16.7 us (15%)
  local copies, waits for them, and re-layouts  1.77 us (2%)
    ppermute x37, waiting for transfers between devices, swap(): lax.ppermute(value, axis, [(i, i ^ mask) for i in range(lax.axis_size(axi...  45 us
    ppermute x37, starting transfers between devices, swap(): lax.ppermute(value, axis, [(i, i ^ mask) for i in range(lax.axis_size(axi...  35 us
    pallas_call x1, Pallas kernels, fetch_rows(): pl.pallas_call(functools.partial(fetch_kernel, block_rows, vocab), out_sh...  9.58 us
    pallas_call x12, Pallas kernels, kernel_call(): pl.pallas_call(functools.partial(kernel, lax.axis_size('tensor') // 2), o...  7.17 us
    ppermute x2, starting transfers between devices, onward(): lax.ppermute(value, 'segment', [(i, (i ^ flip) + 2) for i in range(size -...  6.93 us
  transfers between devices with their start and end apart: 39, of which 26 were waited for; matrix products, arithmetic and copies ran while one was open for 0% of the time, Pallas kernels for 13%

profile of v2, /device:TPU:0, one launch (start us, length us, event | category | flops | bytes accessed | tf_op | source)
XLA Modules:
  0.0 107.5 jit_solution(16162873886429313933)
XLA Ops:
  0.0 1.0 copy-done
  1.1 5.1 %collective-permute-start.2 = (bf16[128,512]{1,0:T(8,128)(2,1)S(1)}, bf16[128,512]{1,0:T(8,128)(2,1)S(1)}, u32[]{:S(2)}, u32[]{:S(2)}) collective-permute-start(bf16[128,512]{1,0:T(8,128)(2,1)S(1)} %constant_dynamic-slice_fusion), channel_id=1, source_target_pairs={{0,6},{1,7},{2,4},{3,5},{4,2},{5,3},{6,0},{7,1},{8,14},{9,15},{10,... | collective-permute-start | bytes 393224 | tf_op jit(solution)/shard_map/ppermute | solution.py:20
  6.2 0.6 collective-permute-start
  6.8 0.7 copy-done.3
  7.5 9.6 %fetch_rows.1 = (bf16[48,512]{1,0:T(8,128)(2,1)S(1)}, bf16[48,512]{1,0:T(8,128)(2,1)S(1)}, bf16[48,512]{1,0:T(8,128)(2,1)S(1)}, bf16[48,512]{1,0:T(8,128)(2,1)S(...) custom-call(s32[192]{0:T(256)S(1)} %copy-done.3, s32[1,192]{1,0:T(1,128)S(1)} %bitcast.9, ...), custom_call_target="tpu_custom_call" | custom-call | tf_op jit(solution)/shard_map/fetch_rows/pallas_call | solution.py:153
  17.1 0.2 collective-permute-done.1
  17.2 1.5 %collective-permute-start.3 = (bf16[48,512]{1,0:T(8,128)(2,1)S(1)}, bf16[48,512]{1,0:T(8,128)(2,1)S(1)}, u32[]{:S(2)}, u32[]{:S(2)}) collective-permute-start(bf16[48,512]{1,0:T(8,128)(2,1)S(1)} %get-tuple-element.53), channel_id=1, source_target_pairs={{0,8},{8,0},{16,24},{24,16},{1,9},{9,1},{17,25},{25,17},{2,10},{10... | collective-permute-start | bytes 147464 | tf_op jit(solution)/shard_map/ppermute | solution.py:20
  18.8 1.5 %collective-permute-start.4 = (bf16[48,512]{1,0:T(8,128)(2,1)S(1)}, bf16[48,512]{1,0:T(8,128)(2,1)S(1)}, u32[]{:S(2)}, u32[]{:S(2)}) collective-permute-start(bf16[48,512]{1,0:T(8,128)(2,1)S(1)} %get-tuple-element.54), channel_id=1, source_target_pairs={{0,16},{8,24},{16,0},{24,8},{1,17},{9,25},{17,1},{25,9},{2,18},{10... | collective-permute-start | bytes 147464 | tf_op jit(solution)/shard_map/ppermute | solution.py:20
  20.3 0.4 collective-permute-start.5
  20.7 0.1 pad_maximum_fusion.refs_0_
  20.8 0.5 collective-permute-done.3
  21.3 2.1 %collective-permute-done.4 = bf16[48,512]{1,0:T(8,128)(2,1)S(1)} collective-permute-done((bf16[48,512]{1,0:T(8,128)(2,1)S(1)}, bf16[48,512]{1,0:T(8,128)(2,1)S(1)}, u32[]{:S(2)}, u32[]{:S(2)}) %collective-permute-start.4) | collective-permute-done | bytes 49184 | tf_op jit(solution)/shard_map/ppermute | solution.py:20
  23.4 1.9 %collective-permute-done.5 = bf16[48,512]{1,0:T(8,128)(2,1)S(1)} collective-permute-done((bf16[48,512]{1,0:T(8,128)(2,1)S(1)}, bf16[48,512]{1,0:T(8,128)(2,1)S(1)}, u32[]{:S(2)}, u32[]{:S(2)}) %collective-permute-start.5) | collective-permute-done | bytes 49184 | tf_op jit(solution)/shard_map/ppermute | solution.py:20
  25.3 0.6 collective-permute-start.10
  25.9 0.5 collective-permute-start.9
  26.4 3.7 %collective-permute-start.8 = (bf16[48,512]{1,0:T(8,128)(2,1)S(1)}, bf16[48,512]{1,0:T(8,128)(2,1)S(1)}, u32[]{:S(2)}, u32[]{:S(2)}) collective-permute-start(bf16[48,512]{1,0:T(8,128)(2,1)S(1)} %add_add_fusion), channel_id=1, source_target_pairs={{0,6},{1,7},{2,4},{3,5},{4,2},{5,3},{6,0},{7,1},{8,14},{9,15},{10,... | collective-permute-start | bytes 147464 | tf_op jit(solution)/shard_map/ppermute | solution.py:20
  30.1 0.7 collective-permute-start.6
  30.8 1.5 %collective-permute-done.8 = bf16[48,512]{1,0:T(8,128)(2,1)S(1)} collective-permute-done((bf16[48,512]{1,0:T(8,128)(2,1)S(1)}, bf16[48,512]{1,0:T(8,128)(2,1)S(1)}, u32[]{:S(2)}, u32[]{:S(2)}) %collective-permute-start.8) | collective-permute-done | bytes 49184 | tf_op jit(solution)/shard_map/ppermute | solution.py:20
  32.3 2.7 %collective-permute-done.7 = bf16[48,512]{1,0:T(8,128)(2,1)S(1)} collective-permute-done((bf16[48,512]{1,0:T(8,128)(2,1)S(1)}, bf16[48,512]{1,0:T(8,128)(2,1)S(1)}, u32[]{:S(2)}, u32[]{:S(2)}) %collective-permute-start.7) | collective-permute-done | bytes 49184 | tf_op jit(solution)/shard_map/ppermute | solution.py:20
  35.1 1.7 %collective-permute-done.10.refs_2_ = bf16[4,128,512]{2,1,0:T(8,128)(2,1)S(1)} collective-permute-done((bf16[4,128,512]{2,1,0:T(8,128)(2,1)S(1)}, bf16[4,128,512]{2,1,0:T(8,128)(2,1)S(1)}, u32[]{:S(2)}, u32[]{:S(2)}) %collective-permute-start.10) | collective-permute-done | bytes 524320 | tf_op jit(solution)/shard_map/ppermute | solution.py:20
  36.7 0.1 collective-permute-done.9.refs_1_
  36.9 2.6 %collective-permute-start.11 = (bf16[4,48,512]{2,1,0:T(8,128)(2,1)S(1)}, bf16[4,48,512]{2,1,0:T(8,128)(2,1)S(1)}, u32[]{:S(2)}, u32[]{:S(2)}) collective-permute-start(bf16[4,48,512]{2,1,0:T(8,128)(2,1)S(1)} %pad_maximum_fusion.1.refs_0_), channel_id=1, source_target_pairs={{0,24},{8,16},{16,8},{24,0},{1,25},{9,17},{17,9},{25,1},{2,26},{10... | collective-permute-start | bytes 589832 | tf_op jit(solution)/shard_map/ppermute | solution.py:20
  39.5 1.5 %collective-permute-start.12 = (bf16[4,48,512]{2,1,0:T(8,128)(2,1)S(1)}, bf16[4,48,512]{2,1,0:T(8,128)(2,1)S(1)}, u32[]{:S(2)}, u32[]{:S(2)}) collective-permute-start(bf16[4,48,512]{2,1,0:T(8,128)(2,1)S(1)} %pad_maximum_fusion.1.refs_0_), channel_id=1, source_target_pairs={{0,8},{8,0},{16,24},{24,16},{1,9},{9,1},{17,25},{25,17},{2,10},{10... | collective-permute-start | bytes 589832 | tf_op jit(solution)/shard_map/ppermute | solution.py:20
  41.0 3.4 %collective-permute-done.11.refs_3_ = bf16[4,48,512]{2,1,0:T(8,128)(2,1)S(1)} collective-permute-done((bf16[4,48,512]{2,1,0:T(8,128)(2,1)S(1)}, bf16[4,48,512]{2,1,0:T(8,128)(2,1)S(1)}, u32[]{:S(2)}, u32[]{:S(2)}) %collective-permute-start.11) | collective-permute-done | bytes 196640 | tf_op jit(solution)/shard_map/ppermute | solution.py:20
  44.4 2.0 %collective-permute-done.13.refs_2_ = bf16[4,48,512]{2,1,0:T(8,128)(2,1)S(1)} collective-permute-done((bf16[4,48,512]{2,1,0:T(8,128)(2,1)S(1)}, bf16[4,48,512]{2,1,0:T(8,128)(2,1)S(1)}, u32[]{:S(2)}, u32[]{:S(2)}) %collective-permute-start.13) | collective-permute-done | bytes 196640 | tf_op jit(solution)/shard_map/ppermute | solution.py:20
  46.4 0.4 collective-permute-done.12.refs_1_
  46.8 0.1 collective-permute-start.15
  46.9 0.4 collective-permute-start.17
  47.3 0.2 collective-permute-start.21
  47.5 0.4 collective-permute-start.22
  48.0 0.6 collective-permute-start.19
  48.5 1.6 %collective-permute-start.18 = (bf16[2,128,512]{2,1,0:T(8,128)(2,1)S(1)}, bf16[2,128,512]{2,1,0:T(8,128)(2,1)S(1)}, u32[]{:S(2)}, u32[]{:S(2)}) collective-permute-start(bf16[2,128,512]{2,1,0:T(8,128)(2,1)S(1)} %slice.6), channel_id=1, source_target_pairs={{0,16},{8,24},{16,0},{24,8},{1,17},{9,25},{17,1},{25,9},{2,18},{10... | collective-permute-start | bytes 786440 | tf_op jit(solution)/shard_map/ppermute | solution.py:20
  50.2 3.9 %section_first.1 = (bf16[192,4096]{1,0:T(8,128)(2,1)S(1)}, bf16[192,4096]{1,0:T(8,128)(2,1)S(1)}, f32[192,896]{1,0:T(8,128)S(1)}, f32[192,1]{1,0:T(8,128)S(1)}) custom-call(bf16[4,48,512]{2,1,0:T(8,128)(2,1)S(1)} %pad_maximum_fusion.1.refs_0_, bf16[4,48,512]{2,1,0:T(8,128)(2,1)S(1)} %collective-permute-done.12.refs_1_, ...), custom_call_target="tpu_custom_call" | custom-call | flops 2818572288 | tf_op jit(solution)/shard_map/section_first/pallas_call | solution.py:341
  54.1 2.2 %collective-permute-done.19.refs_4_ = bf16[2,128,512]{2,1,0:T(8,128)(2,1)S(1)} collective-permute-done((bf16[2,128,512]{2,1,0:T(8,128)(2,1)S(1)}, bf16[2,128,512]{2,1,0:T(8,128)(2,1)S(1)}, u32[]{:S(2)}, u32[]{:S(2)}) %collective-permute-start.19) | collective-permute-done | bytes 262176 | tf_op jit(solution)/shard_map/ppermute | solution.py:20
  56.3 0.4 collective-permute-done.18.refs_3_
  56.7 0.5 collective-permute-start.24
  57.3 1.0 collective-permute-done.23.refs_8_
  58.3 0.4 collective-permute-done.24.refs_9_
  58.6 1.4 %project_first.1 = (bf16[96,512]{1,0:T(8,128)(2,1)S(1)}, bf16[96,512]{1,0:T(8,128)(2,1)S(1)}, bf16[4096,512]{1,0:T(8,128)(2,1)S(1)}, f32[192,512]{1,0:T(8,128)S(...) custom-call(bf16[4,128,512]{2,1,0:T(8,128)(2,1)S(1)} %pad_maximum_fusion.refs_0_, ...), custom_call_target="tpu_custom_call" | custom-call | flops 805306368 | tf_op jit(solution)/shard_map/project_first/pallas_call | solution.py:341
  60.0 0.2 collective-permute-start.25
  60.2 1.2 %collective-permute-done.25.refs_1_ = bf16[96,512]{1,0:T(8,128)(2,1)S(1)} collective-permute-done((bf16[96,512]{1,0:T(8,128)(2,1)S(1)}, bf16[96,512]{1,0:T(8,128)(2,1)S(1)}, u32[]{:S(2)}, u32[]{:S(2)}) %collective-permute-start.25) | collective-permute-done | bytes 98336 | tf_op jit(solution)/shard_map/ppermute | solution.py:20
  61.4 3.5 %collective-permute-start.28 = (bf16[96,512]{1,0:T(8,128)(2,1)S(1)}, bf16[96,512]{1,0:T(8,128)(2,1)S(1)}, u32[]{:S(2)}, u32[]{:S(2)}) collective-permute-start(bf16[96,512]{1,0:T(8,128)(2,1)S(1)} %add.29.after), channel_id=1, source_target_pairs={{0,6},{1,7},{2,4},{3,5},{4,2},{5,3},{6,0},{7,1},{8,14},{9,15},{10,... | collective-permute-start | bytes 294920 | tf_op jit(solution)/shard_map/ppermute | solution.py:20
  65.0 0.9 collective-permute-start.26
  65.9 3.1 %collective-permute-done.28.refs_3_ = bf16[96,512]{1,0:T(8,128)(2,1)S(1)} collective-permute-done((bf16[96,512]{1,0:T(8,128)(2,1)S(1)}, bf16[96,512]{1,0:T(8,128)(2,1)S(1)}, u32[]{:S(2)}, u32[]{:S(2)}) %collective-permute-start.28) | collective-permute-done | bytes 98336 | tf_op jit(solution)/shard_map/ppermute | solution.py:20
  69.0 4.5 %collective-permute-done.27.refs_2_ = bf16[96,512]{1,0:T(8,128)(2,1)S(1)} collective-permute-done((bf16[96,512]{1,0:T(8,128)(2,1)S(1)}, bf16[96,512]{1,0:T(8,128)(2,1)S(1)}, u32[]{:S(2)}, u32[]{:S(2)}) %collective-permute-start.27) | collective-permute-done | bytes 98336 | tf_op jit(solution)/shard_map/ppermute | solution.py:20
  73.6 5.6 %collective-permute-start.31 = (bf16[96,512]{1,0:T(8,128)(2,1)S(1)}, bf16[96,512]{1,0:T(8,128)(2,1)S(1)}, u32[]{:S(2)}, u32[]{:S(2)}) collective-permute-start(bf16[96,512]{1,0:T(8,128)(2,1)S(1)} %add.30.after), channel_id=1, source_target_pairs={{0,24},{8,16},{1,25},{9,17},{2,26},{10,18},{3,27},{11,19},{4,28},{... | collective-permute-start | bytes 294920 | tf_op jit(solution)/shard_map/ppermute | solution.py:25
  79.2 1.3 %collective-permute-start.30 = (bf16[96,512]{1,0:T(8,128)(2,1)S(1)}, bf16[96,512]{1,0:T(8,128)(2,1)S(1)}, u32[]{:S(2)}, u32[]{:S(2)}) collective-permute-start(bf16[96,512]{1,0:T(8,128)(2,1)S(1)} %add.30.after), channel_id=1, source_target_pairs={{0,16},{8,24},{1,17},{9,25},{2,18},{10,26},{3,19},{11,27},{4,20},{... | collective-permute-start | bytes 294920 | tf_op jit(solution)/shard_map/ppermute | solution.py:25
  80.5 1.5 %collective-permute-start.29 = (bf16[96,512]{1,0:T(8,128)(2,1)S(1)}, bf16[96,512]{1,0:T(8,128)(2,1)S(1)}, u32[]{:S(2)}, u32[]{:S(2)}) collective-permute-start(bf16[96,512]{1,0:T(8,128)(2,1)S(1)} %add.30.after), channel_id=1, source_target_pairs={{0,8},{8,0},{16,24},{24,16},{1,9},{9,1},{17,25},{25,17},{2,10},{10... | collective-permute-start | bytes 294920 | tf_op jit(solution)/shard_map/ppermute | solution.py:20
  82.1 1.7 %collective-permute-done.30.straight = bf16[96,512]{1,0:T(8,128)(2,1)S(1)} collective-permute-done((bf16[96,512]{1,0:T(8,128)(2,1)S(1)}, bf16[96,512]{1,0:T(8,128)(2,1)S(1)}, u32[]{:S(2)}, u32[]{:S(2)}) %collective-permute-start.30) | collective-permute-done | bytes 98336 | tf_op jit(solution)/shard_map/ppermute | solution.py:25
  83.8 1.6 %collective-permute-done.29.partner = bf16[96,512]{1,0:T(8,128)(2,1)S(1)} collective-permute-done((bf16[96,512]{1,0:T(8,128)(2,1)S(1)}, bf16[96,512]{1,0:T(8,128)(2,1)S(1)}, u32[]{:S(2)}, u32[]{:S(2)}) %collective-permute-start.29) | collective-permute-done | bytes 98336 | tf_op jit(solution)/shard_map/ppermute | solution.py:20
  85.4 0.1 collective-permute-start.32
  85.5 1.3 %collective-permute-done.32.refs_1_ = bf16[96,512]{1,0:T(8,128)(2,1)S(1)} collective-permute-done((bf16[96,512]{1,0:T(8,128)(2,1)S(1)}, bf16[96,512]{1,0:T(8,128)(2,1)S(1)}, u32[]{:S(2)}, u32[]{:S(2)}) %collective-permute-start.32) | collective-permute-done | bytes 98336 | tf_op jit(solution)/shard_map/ppermute | solution.py:20
  86.8 1.0 section_next.1
  87.8 0.2 collective-permute-start.33
  88.0 1.1 %collective-permute-done.33.refs_1_ = bf16[96,512]{1,0:T(8,128)(2,1)S(1)} collective-permute-done((bf16[96,512]{1,0:T(8,128)(2,1)S(1)}, bf16[96,512]{1,0:T(8,128)(2,1)S(1)}, u32[]{:S(2)}, u32[]{:S(2)}) %collective-permute-start.33) | collective-permute-done | bytes 98336 | tf_op jit(solution)/shard_map/ppermute | solution.py:20
  89.2 2.5 %collective-permute-start.36 = (bf16[96,512]{1,0:T(8,128)(2,1)S(1)}, bf16[96,512]{1,0:T(8,128)(2,1)S(1)}, u32[]{:S(2)}, u32[]{:S(2)}) collective-permute-start(bf16[96,512]{1,0:T(8,128)(2,1)S(1)} %add.31.refs_0_), channel_id=1, source_target_pairs={{0,6},{1,7},{2,4},{3,5},{4,2},{5,3},{6,0},{7,1},{8,14},{9,15},{10,... | collective-permute-start | bytes 294920 | tf_op jit(solution)/shard_map/ppermute | solution.py:20
  91.6 2.0 %collective-permute-start.34 = (bf16[96,512]{1,0:T(8,128)(2,1)S(1)}, bf16[96,512]{1,0:T(8,128)(2,1)S(1)}, u32[]{:S(2)}, u32[]{:S(2)}) collective-permute-start(bf16[96,512]{1,0:T(8,128)(2,1)S(1)} %add.31.refs_0_), channel_id=1, source_target_pairs={{0,2},{1,3},{2,0},{3,1},{4,6},{5,7},{6,4},{7,5},{8,10},{9,11},{10,... | collective-permute-start | bytes 294920 | tf_op jit(solution)/shard_map/ppermute | solution.py:20
  93.6 3.1 %collective-permute-done.36.refs_3_ = bf16[96,512]{1,0:T(8,128)(2,1)S(1)} collective-permute-done((bf16[96,512]{1,0:T(8,128)(2,1)S(1)}, bf16[96,512]{1,0:T(8,128)(2,1)S(1)}, u32[]{:S(2)}, u32[]{:S(2)}) %collective-permute-start.36) | collective-permute-done | bytes 98336 | tf_op jit(solution)/shard_map/ppermute | solution.py:20
  96.7 3.9 %collective-permute-done.35.refs_2_ = bf16[96,512]{1,0:T(8,128)(2,1)S(1)} collective-permute-done((bf16[96,512]{1,0:T(8,128)(2,1)S(1)}, bf16[96,512]{1,0:T(8,128)(2,1)S(1)}, u32[]{:S(2)}, u32[]{:S(2)}) %collective-permute-start.35) | collective-permute-done | bytes 98336 | tf_op jit(solution)/shard_map/ppermute | solution.py:20
  100.7 1.4 %collective-permute-start.37 = (bf16[96,512]{1,0:T(8,128)(2,1)S(1)}, bf16[96,512]{1,0:T(8,128)(2,1)S(1)}, u32[]{:S(2)}, u32[]{:S(2)}) collective-permute-start(bf16[96,512]{1,0:T(8,128)(2,1)S(1)} %add.32.refs_0_), channel_id=1, source_target_pairs={{0,8},{8,0},{16,24},{24,16},{1,9},{9,1},{17,25},{25,17},{2,10},{10... | collective-permute-start | bytes 294920 | tf_op jit(solution)/shard_map/ppermute | solution.py:20
  102.1 3.3 %collective-permute-done.37.refs_1_ = bf16[96,512]{1,0:T(8,128)(2,1)S(1)} collective-permute-done((bf16[96,512]{1,0:T(8,128)(2,1)S(1)}, bf16[96,512]{1,0:T(8,128)(2,1)S(1)}, u32[]{:S(2)}, u32[]{:S(2)}) %collective-permute-start.37) | collective-permute-done | bytes 98336 | tf_op jit(solution)/shard_map/ppermute | solution.py:20
  105.4 0.1 collective-permute-start.38
  105.5 1.3 %collective-permute-done.38.refs_3_ = bf16[96,512]{1,0:T(8,128)(2,1)S(1)} collective-permute-done((bf16[96,512]{1,0:T(8,128)(2,1)S(1)}, bf16[96,512]{1,0:T(8,128)(2,1)S(1)}, u32[]{:S(2)}, u32[]{:S(2)}) %collective-permute-start.38) | collective-permute-done | bytes 98336 | tf_op jit(solution)/shard_map/ppermute | solution.py:20
  106.8 0.7 collect.1
  (41 shorter events, 0.4 us)
Async XLA Ops:
  0.0 1.0 copy-start
  1.1 16.0 %collective-permute-start.2 = (bf16[128,512]{1,0:T(8,128)(2,1)S(1)}, bf16[128,512]{1,0:T(8,128)(2,1)S(1)}, u32[]{:S(2)}, u32[]{:S(2)}) collective-permute-start(bf16[128,512]{1,0:T(8,128)(2,1)S(1)} %constant_dynamic-slice_fusion), channel_id=1, source_target_pairs={{0,6},{1,7},{2,4},{3,5},{4,2},{5,3},{6,0},{7,1},{8,14},{9,15},{10,... | collective-permute-start | bytes 393224 | tf_op jit(solution)/shard_map/ppermute | solution.py:20
  6.2 11.1 %collective-permute-start.1 = (bf16[128,512]{1,0:T(8,128)(2,1)S(1)}, bf16[128,512]{1,0:T(8,128)(2,1)S(1)}, u32[]{:S(2)}, u32[]{:S(2)}) collective-permute-start(bf16[128,512]{1,0:T(8,128)(2,1)S(1)} %constant_dynamic-slice_fusion), channel_id=1, source_target_pairs={{0,4},{1,5},{2,6},{3,7},{4,0},{5,1},{6,2},{7,3},{8,12},{9,13},{10,... | collective-permute-start | bytes 393224 | tf_op jit(solution)/shard_map/ppermute | solution.py:20
  6.2 11.1 %collective-permute-start = (bf16[128,512]{1,0:T(8,128)(2,1)S(1)}, bf16[128,512]{1,0:T(8,128)(2,1)S(1)}, u32[]{:S(2)}, u32[]{:S(2)}) collective-permute-start(bf16[128,512]{1,0:T(8,128)(2,1)S(1)} %constant_dynamic-slice_fusion), channel_id=1, source_target_pairs={{0,2},{1,3},{2,0},{3,1},{4,6},{5,7},{6,4},{7,5},{8,10},{9,11},{10,... | collective-permute-start | bytes 393224 | tf_op jit(solution)/shard_map/ppermute | solution.py:20
  6.8 0.7 copy-start.3
  7.5 42.7 %copy-start.2 = (f32[2,4096]{1,0:T(2,128)S(1)}, f32[2,4096]{1,0:T(2,128)}, u32[]{:S(2)}) copy-start(f32[2,4096]{1,0:T(2,128)} %gain.1) | copy-start | bytes 98308
  17.2 4.1 %collective-permute-start.3 = (bf16[48,512]{1,0:T(8,128)(2,1)S(1)}, bf16[48,512]{1,0:T(8,128)(2,1)S(1)}, u32[]{:S(2)}, u32[]{:S(2)}) collective-permute-start(bf16[48,512]{1,0:T(8,128)(2,1)S(1)} %get-tuple-element.53), channel_id=1, source_target_pairs={{0,8},{8,0},{16,24},{24,16},{1,9},{9,1},{17,25},{25,17},{2,10},{10... | collective-permute-start | bytes 147464 | tf_op jit(solution)/shard_map/ppermute | solution.py:20
  18.8 4.6 %collective-permute-start.4 = (bf16[48,512]{1,0:T(8,128)(2,1)S(1)}, bf16[48,512]{1,0:T(8,128)(2,1)S(1)}, u32[]{:S(2)}, u32[]{:S(2)}) collective-permute-start(bf16[48,512]{1,0:T(8,128)(2,1)S(1)} %get-tuple-element.54), channel_id=1, source_target_pairs={{0,16},{8,24},{16,0},{24,8},{1,17},{9,25},{17,1},{25,9},{2,18},{10... | collective-permute-start | bytes 147464 | tf_op jit(solution)/shard_map/ppermute | solution.py:20
  20.3 5.0 %collective-permute-start.5 = (bf16[48,512]{1,0:T(8,128)(2,1)S(1)}, bf16[48,512]{1,0:T(8,128)(2,1)S(1)}, u32[]{:S(2)}, u32[]{:S(2)}) collective-permute-start(bf16[48,512]{1,0:T(8,128)(2,1)S(1)} %get-tuple-element.55), channel_id=1, source_target_pairs={{0,24},{8,16},{16,8},{24,0},{1,25},{9,17},{17,9},{25,1},{2,26},{10... | collective-permute-start | bytes 147464 | tf_op jit(solution)/shard_map/ppermute | solution.py:20
  25.3 11.4 %collective-permute-start.10 = (bf16[4,128,512]{2,1,0:T(8,128)(2,1)S(1)}, bf16[4,128,512]{2,1,0:T(8,128)(2,1)S(1)}, u32[]{:S(2)}, u32[]{:S(2)}) collective-permute-start(bf16[4,128,512]{2,1,0:T(8,128)(2,1)S(1)} %pad_maximum_fusion.refs_0_), channel_id=1, source_target_pairs={{0,16},{8,24},{16,0},{24,8},{1,17},{9,25},{17,1},{25,9},{2,18},{10... | collective-permute-start | bytes 1572872 | tf_op jit(solution)/shard_map/ppermute | solution.py:20
  25.9 11.0 %collective-permute-start.9 = (bf16[4,128,512]{2,1,0:T(8,128)(2,1)S(1)}, bf16[4,128,512]{2,1,0:T(8,128)(2,1)S(1)}, u32[]{:S(2)}, u32[]{:S(2)}) collective-permute-start(bf16[4,128,512]{2,1,0:T(8,128)(2,1)S(1)} %pad_maximum_fusion.refs_0_), channel_id=1, source_target_pairs={{0,8},{8,0},{16,24},{24,16},{1,9},{9,1},{17,25},{25,17},{2,10},{10... | collective-permute-start | bytes 1572872 | tf_op jit(solution)/shard_map/ppermute | solution.py:20
  26.4 5.9 %collective-permute-start.8 = (bf16[48,512]{1,0:T(8,128)(2,1)S(1)}, bf16[48,512]{1,0:T(8,128)(2,1)S(1)}, u32[]{:S(2)}, u32[]{:S(2)}) collective-permute-start(bf16[48,512]{1,0:T(8,128)(2,1)S(1)} %add_add_fusion), channel_id=1, source_target_pairs={{0,6},{1,7},{2,4},{3,5},{4,2},{5,3},{6,0},{7,1},{8,14},{9,15},{10,... | collective-permute-start | bytes 147464 | tf_op jit(solution)/shard_map/ppermute | solution.py:20
  30.0 5.0 %collective-permute-start.7 = (bf16[48,512]{1,0:T(8,128)(2,1)S(1)}, bf16[48,512]{1,0:T(8,128)(2,1)S(1)}, u32[]{:S(2)}, u32[]{:S(2)}) collective-permute-start(bf16[48,512]{1,0:T(8,128)(2,1)S(1)} %add_add_fusion), channel_id=1, source_target_pairs={{0,4},{1,5},{2,6},{3,7},{4,0},{5,1},{6,2},{7,3},{8,12},{9,13},{10,... | collective-permute-start | bytes 147464 | tf_op jit(solution)/shard_map/ppermute | solution.py:20
  30.1 5.0 %collective-permute-start.6 = (bf16[48,512]{1,0:T(8,128)(2,1)S(1)}, bf16[48,512]{1,0:T(8,128)(2,1)S(1)}, u32[]{:S(2)}, u32[]{:S(2)}) collective-permute-start(bf16[48,512]{1,0:T(8,128)(2,1)S(1)} %add_add_fusion), channel_id=1, source_target_pairs={{0,2},{1,3},{2,0},{3,1},{4,6},{5,7},{6,4},{7,5},{8,10},{9,11},{10,... | collective-permute-start | bytes 147464 | tf_op jit(solution)/shard_map/ppermute | solution.py:20
  36.9 7.5 %collective-permute-start.11 = (bf16[4,48,512]{2,1,0:T(8,128)(2,1)S(1)}, bf16[4,48,512]{2,1,0:T(8,128)(2,1)S(1)}, u32[]{:S(2)}, u32[]{:S(2)}) collective-permute-start(bf16[4,48,512]{2,1,0:T(8,128)(2,1)S(1)} %pad_maximum_fusion.1.refs_0_), channel_id=1, source_target_pairs={{0,24},{8,16},{16,8},{24,0},{1,25},{9,17},{17,9},{25,1},{2,26},{10... | collective-permute-start | bytes 589832 | tf_op jit(solution)/shard_map/ppermute | solution.py:20
  39.5 6.9 %collective-permute-start.13 = (bf16[4,48,512]{2,1,0:T(8,128)(2,1)S(1)}, bf16[4,48,512]{2,1,0:T(8,128)(2,1)S(1)}, u32[]{:S(2)}, u32[]{:S(2)}) collective-permute-start(bf16[4,48,512]{2,1,0:T(8,128)(2,1)S(1)} %pad_maximum_fusion.1.refs_0_), channel_id=1, source_target_pairs={{0,16},{8,24},{16,0},{24,8},{1,17},{9,25},{17,1},{25,9},{2,18},{10... | collective-permute-start | bytes 589832 | tf_op jit(solution)/shard_map/ppermute | solution.py:20
  39.5 7.3 %collective-permute-start.12 = (bf16[4,48,512]{2,1,0:T(8,128)(2,1)S(1)}, bf16[4,48,512]{2,1,0:T(8,128)(2,1)S(1)}, u32[]{:S(2)}, u32[]{:S(2)}) collective-permute-start(bf16[4,48,512]{2,1,0:T(8,128)(2,1)S(1)} %pad_maximum_fusion.1.refs_0_), channel_id=1, source_target_pairs={{0,8},{8,0},{16,24},{24,16},{1,9},{9,1},{17,25},{25,17},{2,10},{10... | collective-permute-start | bytes 589832 | tf_op jit(solution)/shard_map/ppermute | solution.py:20
  41.0 6.6 %collective-permute-start.14 = (bf16[4,48,512]{2,1,0:T(8,128)(2,1)S(1)}, bf16[4,48,512]{2,1,0:T(8,128)(2,1)S(1)}, u32[]{:S(2)}, u32[]{:S(2)}) collective-permute-start(bf16[4,48,512]{2,1,0:T(8,128)(2,1)S(1)} %pad_maximum_fusion.1.refs_0_), channel_id=1, source_target_pairs={{0,1},{1,0},{2,3},{3,2},{4,5},{5,4},{6,7},{7,6},{8,9},{9,8},{10,11... | collective-permute-start | bytes 589832 | tf_op jit(solution)/shard_map/ppermute | solution.py:20
  46.4 1.6 %collective-permute-start.16 = (bf16[4,48,512]{2,1,0:T(8,128)(2,1)S(1)}, bf16[4,48,512]{2,1,0:T(8,128)(2,1)S(1)}, u32[]{:S(2)}, u32[]{:S(2)}) collective-permute-start(bf16[4,48,512]{2,1,0:T(8,128)(2,1)S(1)} %collective-permute-done.13.refs_2_), channel_id=1, source_target_pairs={{0,1},{1,0},{2,3},{3,2},{4,5},{5,4},{6,7},{7,6},{8,9},{9,8},{10,11... | collective-permute-start | bytes 589832 | tf_op jit(solution)/shard_map/ppermute | solution.py:20
  46.8 1.8 %collective-permute-start.15 = (bf16[4,48,512]{2,1,0:T(8,128)(2,1)S(1)}, bf16[4,48,512]{2,1,0:T(8,128)(2,1)S(1)}, u32[]{:S(2)}, u32[]{:S(2)}) collective-permute-start(bf16[4,48,512]{2,1,0:T(8,128)(2,1)S(1)} %collective-permute-done.12.refs_1_), channel_id=1, source_target_pairs={{0,1},{1,0},{2,3},{3,2},{4,5},{5,4},{6,7},{7,6},{8,9},{9,8},{10,11... | collective-permute-start | bytes 589832 | tf_op jit(solution)/shard_map/ppermute | solution.py:20
  46.9 3.3 %collective-permute-start.17 = (bf16[4,48,512]{2,1,0:T(8,128)(2,1)S(1)}, bf16[4,48,512]{2,1,0:T(8,128)(2,1)S(1)}, u32[]{:S(2)}, u32[]{:S(2)}) collective-permute-start(bf16[4,48,512]{2,1,0:T(8,128)(2,1)S(1)} %collective-permute-done.11.refs_3_), channel_id=1, source_target_pairs={{0,1},{1,0},{2,3},{3,2},{4,5},{5,4},{6,7},{7,6},{8,9},{9,8},{10,11... | collective-permute-start | bytes 589832 | tf_op jit(solution)/shard_map/ppermute | solution.py:20
  47.3 10.0 %collective-permute-start.21 = (bf16[4,128,512]{2,1,0:T(8,128)(2,1)S(1)}, bf16[4,128,512]{2,1,0:T(8,128)(2,1)S(1)}, u32[]{:S(2)}, u32[]{:S(2)}) collective-permute-start(bf16[4,128,512]{2,1,0:T(8,128)(2,1)S(1)} %collective-permute-done.9.refs_1_), channel_id=1, source_target_pairs={{0,1},{1,0},{2,3},{3,2},{4,5},{5,4},{6,7},{7,6},{8,9},{9,8},{10,11... | collective-permute-start | bytes 1572872 | tf_op jit(solution)/shard_map/ppermute | solution.py:20
  47.5 9.7 %collective-permute-start.22 = (bf16[4,128,512]{2,1,0:T(8,128)(2,1)S(1)}, bf16[4,128,512]{2,1,0:T(8,128)(2,1)S(1)}, u32[]{:S(2)}, u32[]{:S(2)}) collective-permute-start(bf16[4,128,512]{2,1,0:T(8,128)(2,1)S(1)} %collective-permute-done.10.refs_2_), channel_id=1, source_target_pairs={{0,1},{1,0},{2,3},{3,2},{4,5},{5,4},{6,7},{7,6},{8,9},{9,8},{10,11... | collective-permute-start | bytes 1572872 | tf_op jit(solution)/shard_map/ppermute | solution.py:20
  48.0 8.4 %collective-permute-start.19 = (bf16[2,128,512]{2,1,0:T(8,128)(2,1)S(1)}, bf16[2,128,512]{2,1,0:T(8,128)(2,1)S(1)}, u32[]{:S(2)}, u32[]{:S(2)}) collective-permute-start(bf16[2,128,512]{2,1,0:T(8,128)(2,1)S(1)} %slice.7), channel_id=1, source_target_pairs={{0,8},{8,0},{16,24},{24,16},{1,9},{9,1},{17,25},{25,17},{2,10},{10... | collective-permute-start | bytes 786440 | tf_op jit(solution)/shard_map/ppermute | solution.py:20
  48.5 8.2 %collective-permute-start.18 = (bf16[2,128,512]{2,1,0:T(8,128)(2,1)S(1)}, bf16[2,128,512]{2,1,0:T(8,128)(2,1)S(1)}, u32[]{:S(2)}, u32[]{:S(2)}) collective-permute-start(bf16[2,128,512]{2,1,0:T(8,128)(2,1)S(1)} %slice.6), channel_id=1, source_target_pairs={{0,16},{8,24},{16,0},{24,8},{1,17},{9,25},{17,1},{25,9},{2,18},{10... | collective-permute-start | bytes 786440 | tf_op jit(solution)/shard_map/ppermute | solution.py:20
  50.2 7.1 %collective-permute-start.20 = (bf16[4,128,512]{2,1,0:T(8,128)(2,1)S(1)}, bf16[4,128,512]{2,1,0:T(8,128)(2,1)S(1)}, u32[]{:S(2)}, u32[]{:S(2)}) collective-permute-start(bf16[4,128,512]{2,1,0:T(8,128)(2,1)S(1)} %pad_maximum_fusion.refs_0_), channel_id=1, source_target_pairs={{0,1},{1,0},{2,3},{3,2},{4,5},{5,4},{6,7},{7,6},{8,9},{9,8},{10,11... | collective-permute-start | bytes 1572872 | tf_op jit(solution)/shard_map/ppermute | solution.py:20
  56.7 1.5 %collective-permute-start.23 = (bf16[2,128,512]{2,1,0:T(8,128)(2,1)S(1)}, bf16[2,128,512]{2,1,0:T(8,128)(2,1)S(1)}, u32[]{:S(2)}, u32[]{:S(2)}) collective-permute-start(bf16[2,128,512]{2,1,0:T(8,128)(2,1)S(1)} %collective-permute-done.18.refs_3_), channel_id=1, source_target_pairs={{0,1},{1,0},{2,3},{3,2},{4,5},{5,4},{6,7},{7,6},{8,9},{9,8},{10,11... | collective-permute-start | bytes 786440 | tf_op jit(solution)/shard_map/ppermute | solution.py:20
  56.7 1.9 %collective-permute-start.24 = (bf16[2,128,512]{2,1,0:T(8,128)(2,1)S(1)}, bf16[2,128,512]{2,1,0:T(8,128)(2,1)S(1)}, u32[]{:S(2)}, u32[]{:S(2)}) collective-permute-start(bf16[2,128,512]{2,1,0:T(8,128)(2,1)S(1)} %collective-permute-done.19.refs_4_), channel_id=1, source_target_pairs={{0,1},{1,0},{2,3},{3,2},{4,5},{5,4},{6,7},{7,6},{8,9},{9,8},{10,11... | collective-permute-start | bytes 786440 | tf_op jit(solution)/shard_map/ppermute | solution.py:20
  60.0 1.4 %collective-permute-start.25 = (bf16[96,512]{1,0:T(8,128)(2,1)S(1)}, bf16[96,512]{1,0:T(8,128)(2,1)S(1)}, u32[]{:S(2)}, u32[]{:S(2)}) collective-permute-start(bf16[96,512]{1,0:T(8,128)(2,1)S(1)} %get-tuple-element.78), channel_id=1, source_target_pairs={{0,1},{1,0},{2,3},{3,2},{4,5},{5,4},{6,7},{7,6},{8,9},{9,8},{10,11... | collective-permute-start | bytes 294920 | tf_op jit(solution)/shard_map/ppermute | solution.py:20
  61.4 7.6 %collective-permute-start.28 = (bf16[96,512]{1,0:T(8,128)(2,1)S(1)}, bf16[96,512]{1,0:T(8,128)(2,1)S(1)}, u32[]{:S(2)}, u32[]{:S(2)}) collective-permute-start(bf16[96,512]{1,0:T(8,128)(2,1)S(1)} %add.29.after), channel_id=1, source_target_pairs={{0,6},{1,7},{2,4},{3,5},{4,2},{5,3},{6,0},{7,1},{8,14},{9,15},{10,... | collective-permute-start | bytes 294920 | tf_op jit(solution)/shard_map/ppermute | solution.py:20
  64.9 8.6 %collective-permute-start.27 = (bf16[96,512]{1,0:T(8,128)(2,1)S(1)}, bf16[96,512]{1,0:T(8,128)(2,1)S(1)}, u32[]{:S(2)}, u32[]{:S(2)}) collective-permute-start(bf16[96,512]{1,0:T(8,128)(2,1)S(1)} %add.29.after), channel_id=1, source_target_pairs={{0,4},{1,5},{2,6},{3,7},{4,0},{5,1},{6,2},{7,3},{8,12},{9,13},{10,... | collective-permute-start | bytes 294920 | tf_op jit(solution)/shard_map/ppermute | solution.py:20
  65.0 8.6 %collective-permute-start.26 = (bf16[96,512]{1,0:T(8,128)(2,1)S(1)}, bf16[96,512]{1,0:T(8,128)(2,1)S(1)}, u32[]{:S(2)}, u32[]{:S(2)}) collective-permute-start(bf16[96,512]{1,0:T(8,128)(2,1)S(1)} %add.29.after), channel_id=1, source_target_pairs={{0,2},{1,3},{2,0},{3,1},{4,6},{5,7},{6,4},{7,5},{8,10},{9,11},{10,... | collective-permute-start | bytes 294920 | tf_op jit(solution)/shard_map/ppermute | solution.py:20
  73.5 34.0 %copy-start.1 = (bf16[512,512]{1,0:T(8,128)(2,1)S(1)}, bf16[512,512]{1,0:T(8,128)(2,1)}, u32[]{:S(2)}) copy-start(bf16[512,512]{1,0:T(8,128)(2,1)} %param.11) | copy-start | bytes 1572868
  73.6 8.5 %collective-permute-start.31 = (bf16[96,512]{1,0:T(8,128)(2,1)S(1)}, bf16[96,512]{1,0:T(8,128)(2,1)S(1)}, u32[]{:S(2)}, u32[]{:S(2)}) collective-permute-start(bf16[96,512]{1,0:T(8,128)(2,1)S(1)} %add.30.after), channel_id=1, source_target_pairs={{0,24},{8,16},{1,25},{9,17},{2,26},{10,18},{3,27},{11,19},{4,28},{... | collective-permute-start | bytes 294920 | tf_op jit(solution)/shard_map/ppermute | solution.py:25
  79.2 4.6 %collective-permute-start.30 = (bf16[96,512]{1,0:T(8,128)(2,1)S(1)}, bf16[96,512]{1,0:T(8,128)(2,1)S(1)}, u32[]{:S(2)}, u32[]{:S(2)}) collective-permute-start(bf16[96,512]{1,0:T(8,128)(2,1)S(1)} %add.30.after), channel_id=1, source_target_pairs={{0,16},{8,24},{1,17},{9,25},{2,18},{10,26},{3,19},{11,27},{4,20},{... | collective-permute-start | bytes 294920 | tf_op jit(solution)/shard_map/ppermute | solution.py:25
  80.5 4.8 %collective-permute-start.29 = (bf16[96,512]{1,0:T(8,128)(2,1)S(1)}, bf16[96,512]{1,0:T(8,128)(2,1)S(1)}, u32[]{:S(2)}, u32[]{:S(2)}) collective-permute-start(bf16[96,512]{1,0:T(8,128)(2,1)S(1)} %add.30.after), channel_id=1, source_target_pairs={{0,8},{8,0},{16,24},{24,16},{1,9},{9,1},{17,25},{25,17},{2,10},{10... | collective-permute-start | bytes 294920 | tf_op jit(solution)/shard_map/ppermute | solution.py:20
  85.4 1.4 %collective-permute-start.32 = (bf16[96,512]{1,0:T(8,128)(2,1)S(1)}, bf16[96,512]{1,0:T(8,128)(2,1)S(1)}, u32[]{:S(2)}, u32[]{:S(2)}) collective-permute-start(bf16[96,512]{1,0:T(8,128)(2,1)S(1)} %hand.1.refs_0_), channel_id=1, source_target_pairs={{0,1},{1,0},{2,3},{3,2},{4,5},{5,4},{6,7},{7,6},{8,9},{9,8},{10,11... | collective-permute-start | bytes 294920 | tf_op jit(solution)/shard_map/ppermute | solution.py:20
  87.8 1.4 %collective-permute-start.33 = (bf16[96,512]{1,0:T(8,128)(2,1)S(1)}, bf16[96,512]{1,0:T(8,128)(2,1)S(1)}, u32[]{:S(2)}, u32[]{:S(2)}) collective-permute-start(bf16[96,512]{1,0:T(8,128)(2,1)S(1)} %get-tuple-element.90), channel_id=1, source_target_pairs={{0,1},{1,0},{2,3},{3,2},{4,5},{5,4},{6,7},{7,6},{8,9},{9,8},{10,11... | collective-permute-start | bytes 294920 | tf_op jit(solution)/shard_map/ppermute | solution.py:20
  89.2 7.6 %collective-permute-start.36 = (bf16[96,512]{1,0:T(8,128)(2,1)S(1)}, bf16[96,512]{1,0:T(8,128)(2,1)S(1)}, u32[]{:S(2)}, u32[]{:S(2)}) collective-permute-start(bf16[96,512]{1,0:T(8,128)(2,1)S(1)} %add.31.refs_0_), channel_id=1, source_target_pairs={{0,6},{1,7},{2,4},{3,5},{4,2},{5,3},{6,0},{7,1},{8,14},{9,15},{10,... | collective-permute-start | bytes 294920 | tf_op jit(solution)/shard_map/ppermute | solution.py:20
  91.6 9.1 %collective-permute-start.35 = (bf16[96,512]{1,0:T(8,128)(2,1)S(1)}, bf16[96,512]{1,0:T(8,128)(2,1)S(1)}, u32[]{:S(2)}, u32[]{:S(2)}) collective-permute-start(bf16[96,512]{1,0:T(8,128)(2,1)S(1)} %add.31.refs_0_), channel_id=1, source_target_pairs={{0,4},{1,5},{2,6},{3,7},{4,0},{5,1},{6,2},{7,3},{8,12},{9,13},{10,... | collective-permute-start | bytes 294920 | tf_op jit(solution)/shard_map/ppermute | solution.py:20
  91.6 9.1 %collective-permute-start.34 = (bf16[96,512]{1,0:T(8,128)(2,1)S(1)}, bf16[96,512]{1,0:T(8,128)(2,1)S(1)}, u32[]{:S(2)}, u32[]{:S(2)}) collective-permute-start(bf16[96,512]{1,0:T(8,128)(2,1)S(1)} %add.31.refs_0_), channel_id=1, source_target_pairs={{0,2},{1,3},{2,0},{3,1},{4,6},{5,7},{6,4},{7,5},{8,10},{9,11},{10,... | collective-permute-start | bytes 294920 | tf_op jit(solution)/shard_map/ppermute | solution.py:20
  100.7 4.7 %collective-permute-start.37 = (bf16[96,512]{1,0:T(8,128)(2,1)S(1)}, bf16[96,512]{1,0:T(8,128)(2,1)S(1)}, u32[]{:S(2)}, u32[]{:S(2)}) collective-permute-start(bf16[96,512]{1,0:T(8,128)(2,1)S(1)} %add.32.refs_0_), channel_id=1, source_target_pairs={{0,8},{8,0},{16,24},{24,16},{1,9},{9,1},{17,25},{25,17},{2,10},{10... | collective-permute-start | bytes 294920 | tf_op jit(solution)/shard_map/ppermute | solution.py:20
  105.4 1.4 %collective-permute-start.38 = (bf16[96,512]{1,0:T(8,128)(2,1)S(1)}, bf16[96,512]{1,0:T(8,128)(2,1)S(1)}, u32[]{:S(2)}, u32[]{:S(2)}) collective-permute-start(bf16[96,512]{1,0:T(8,128)(2,1)S(1)} %add.33.refs_2_), channel_id=1, source_target_pairs={{0,1},{1,0},{2,3},{3,2},{4,5},{5,4},{6,7},{7,6},{8,9},{9,8},{10,11... | collective-permute-start | bytes 294920 | tf_op jit(solution)/shard_map/ppermute | solution.py:20

commit v3 on v2

--- a/solution.py
+++ b/solution.py
@@ -81,9 +81,9 @@
         return carry
 
     buffer[...] = jnp.zeros_like(buffer)
-    lax.fori_loop(0, count, start, 0, unroll=8)
     for weight in weights:
         weight.start()
+    lax.fori_loop(0, count, start, 0, unroll=8)
     wanted = tokens_row[...] - low
     inside = (wanted >= 0) & (wanted < vocab)
     code = jnp.where(inside, lax.rem(wanted, TILE), TILE)
@@ -222,7 +222,7 @@
 
 def project_kernel(chips, *refs):
     shares, refs = refs[: 2 * GROUP + 2], refs[2 * GROUP + 2 :]
-    partial, embedded, own, send, bases, seen, high, low, projected, square = refs
+    partial, own, send, bases, projected = refs
     width, rank = bases.shape
     segment, place, core, share = position(chips)
     features = width // (2 * chips)
@@ -246,34 +246,31 @@
             projected[...] = product if k == 0 else projected[...] + product
         halves(projected, core, own, send)
 
+
+def enter_kernel(chips, *refs):
+    after, bases, gain, gate, embedded, through, seen, high, low, into, into_sum, square = refs
+    segment, place, core, share = position(chips)
+    through[...] = after[...]
+
     @pl.when(segment >= 2)
     def _():
-        for k in range(chunks):
+        gain_row = gain[pl.ds(segment // 2, 1), :]
+        for k in range(bases.shape[0] // CHUNK):
             span = slice(k * CHUNK, (k + 1) * CHUNK)
             table = bases[span, :]
-            turned = table.astype(F32).T.astype(BF16)
-            products = jnp.dot(turned, table, preferred_element_type=F32)
-            product = jnp.dot(embedded[:, span], table, preferred_element_type=F32)
-            square[...] = products if k == 0 else square[...] + products
-            seen[...] = product if k == 0 else seen[...] + product
+            turned = table.astype(F32).T
+            scaled = (turned * gain_row[:, span]).astype(BF16)
+            products = [
+                jnp.dot(scaled, gate[span, :], preferred_element_type=F32),
+                jnp.dot(turned.astype(BF16), table, preferred_element_type=F32),
+                jnp.dot(embedded[:, span], table, preferred_element_type=F32),
+            ]
+            for target, product in zip((into_sum, square, seen), products):
+                target[...] = product if k == 0 else target[...] + product
+        into[...] = into_sum[...].astype(BF16)
         coarse = square[...].astype(BF16)
         high[...] = coarse
         low[...] = (square[...] - coarse.astype(F32)).astype(BF16)
-
-
-def enter_kernel(chips, after, bases, gain, gate, through, into, into_sum):
-    segment, place, core, share = position(chips)
-    through[...] = after[...]
-
-    @pl.when(segment >= 2)
-    def _():
-        gain_row = gain[pl.ds(segment // 2, 1), :]
-        for k in range(bases.shape[0] // CHUNK):
-            span = slice(k * CHUNK, (k + 1) * CHUNK)
-            turned = (bases[span, :].astype(F32).T * gain_row[:, span]).astype(BF16)
-            product = jnp.dot(turned, gate[span, :], preferred_element_type=F32)
-            into_sum[...] = product if k == 0 else into_sum[...] + product
-        into[...] = into_sum[...].astype(BF16)
 
 
 def leave_kernel(chips, after, bases, down, through, out, out_sum):
@@ -294,26 +291,23 @@
     total[...] = tree_sum([term[...].astype(F32) for term in terms]).astype(BF16)
 
 
-def hand_kernel(step, chips, half_sum, partner, straight, crossed, result):
-    @pl.when(lax.axis_index("segment") // 2 <= step)
-    def _():
-        result[...] = (half_sum[...].astype(F32) + partner[...].astype(F32)).astype(BF16)
-
-    @pl.when(lax.axis_index("segment") // 2 > step)
-    def _():
-        result[...] = (straight[...].astype(F32) + crossed[...].astype(F32)).astype(BF16)
-
-
-def collect_kernel(chips, *refs):
-    *pairs, collected = refs
+def choose_kernel(step, chips, half_sum, *refs):
+    *terms, chosen = refs
+
+    @pl.when(lax.axis_index("segment") // 2 < step)
+    def _():
+        chosen[...] = half_sum[...]
+
+    @pl.when(lax.axis_index("segment") // 2 >= step)
+    def _():
+        chosen[...] = tree_sum([term[...].astype(F32) for term in terms]).astype(BF16)
+
+
+def collect_kernel(chips, near, far, collected):
     half = collected.shape[1] // 2
     segment, place, core, share = position(chips)
-    for section in range(len(pairs) // 2):
-
-        @pl.when(segment // 2 == section)
-        def _(section=section):
-            collected[0, pl.ds(pl.multiple_of(core * half, half), half), :] = pairs[2 * section][...]
-            collected[0, pl.ds(pl.multiple_of((1 - core) * half, half), half), :] = pairs[2 * section + 1][...]
+    collected[0, pl.ds(pl.multiple_of(core * half, half), half), :] = near[...]
+    collected[0, pl.ds(pl.multiple_of((1 - core) * half, half), half), :] = far[...]
 
 
 def next_kernel(width, chips, *refs):
@@ -350,6 +344,19 @@
     )(*inputs)
 
 
+def choose(step, half_sum, terms):
+    (chosen,) = kernel_call(
+        functools.partial(choose_kernel, step),
+        "choose",
+        [half_sum, *terms],
+        [jax.ShapeDtypeStruct(half_sum.shape, BF16)],
+        [],
+        0,
+        2,
+    )
+    return chosen
+
+
 def add(terms):
     (total,) = kernel_call(sum_kernel, "add", terms, [jax.ShapeDtypeStruct(terms[0].shape, BF16)], [], 0, 2)
     return total
@@ -374,13 +381,11 @@
     while mask < segments:
         blocks = [block + swap(block, "segment", mask) for block in blocks]
         mask *= 2
-    complete = tree_sum(
-        [block if m == 0 else swap(block, "segment", m) for m, block in enumerate(blocks)]
-    )
-    complete, bands = lax.optimization_barrier((complete, bands))
+    arrived = [blocks[0]] + [swap(blocks[m], "segment", m) for m in range(1, GROUP)]
+    arrived[1], bands = lax.optimization_barrier((arrived[1], bands))
+    complete = tree_sum(arrived)
     shares = [bands] + [swap(bands, "segment", m) for m in range(1, GROUP - 1)]
     along = jnp.stack([complete] + [swap(complete, "tensor", 2 * m) for m in range(1, chips)])
-    along, shares = lax.optimization_barrier((along, shares))
     mine = [along] + [swap(along, "segment", m) for m in range(1, GROUP)]
     mine[GROUP - 1], shares = lax.optimization_barrier((mine[GROUP - 1], shares))
     shares += [swap(shares[1][: chips // 2], "segment", 2), swap(shares[2][chips // 2 :], "segment", 1)]
@@ -404,23 +409,16 @@
     )
     shares = shares + [swap(piece, "tensor", 1) for piece in shares]
     half_shape = jax.ShapeDtypeStruct((count // 2, rank), BF16)
-    own, send, bases, *products = kernel_call(
+    own, send, bases = kernel_call(
         project_kernel,
         "project_first",
-        shares + [partial, embedded],
-        [
-            half_shape,
-            half_shape,
-            pltpu.VMEM((width, rank), BF16),
-            pltpu.VMEM((count, rank), F32),
-            pltpu.VMEM((rank, rank), BF16),
-            pltpu.VMEM((rank, rank), BF16),
-        ],
-        [pltpu.VMEM((count, rank), F32), pltpu.VMEM((rank, rank), F32)],
+        shares + [partial],
+        [half_shape, half_shape, pltpu.VMEM((width, rank), BF16)],
+        [pltpu.VMEM((count, rank), F32)],
         work * rank,
     )
 
-    kept = []
+    received = half_sum = None
     for step in range(sections):
         if step > 0:
             own, send = kernel_call(
@@ -434,16 +432,21 @@
         chip_sum = add([own, swap(send, "tensor", 1)])
         terms = [chip_sum] + [swap(chip_sum, "tensor", 2 * m) for m in range(1, chips)]
         if step == 0:
-            terms[0], into = kernel_call(
+            terms[0], *products = kernel_call(
                 enter_kernel,
                 "enter",
-                [chip_sum, bases, gain, gate],
-                [half_shape, pltpu.VMEM((rank, hidden), BF16)],
-                [pltpu.VMEM((rank, hidden), F32)],
-                2 * hidden * width * rank,
+                [chip_sum, bases, gain, gate, embedded],
+                [
+                    half_shape,
+                    pltpu.VMEM((count, rank), F32),
+                    pltpu.VMEM((rank, rank), BF16),
+                    pltpu.VMEM((rank, rank), BF16),
+                    pltpu.VMEM((rank, hidden), BF16),
+                ],
+                [pltpu.VMEM((rank, hidden), F32), pltpu.VMEM((rank, rank), F32)],
+                2 * rank * width * (hidden + rank + count),
             )
-        half_sum = add(terms)
-        partner = swap(half_sum, "segment", 1)
+        half_sum = add(terms) if step == 0 else choose(step, half_sum, terms)
         if step + 1 < sections:
             straight, crossed = onward(half_sum, 0), onward(half_sum, 1)
             if step == 0:
@@ -455,22 +458,19 @@
                     [pltpu.VMEM((hidden, rank), F32)],
                     2 * hidden * width * rank,
                 )
-                products += [into, out]
-            (result,) = kernel_call(
-                functools.partial(hand_kernel, step),
-                "hand",
-                [half_sum, partner, straight, crossed],
-                [half_shape],
-                [],
-                0,
-                2,
-            )
-        else:
-            result = add([half_sum, partner])
-        received = (result, swap(result, "tensor", 1))
-        kept += received
+                products += [out]
+                straight, half_sum = lax.optimization_barrier((straight, half_sum))
+            handed = add([straight, crossed])
+            received = [handed, swap(handed, "tensor", 1)]
+    result = add([half_sum, swap(half_sum, "segment", 1)])
     (collected,) = kernel_call(
-        collect_kernel, "collect", kept, [jax.ShapeDtypeStruct((1, count, rank), BF16)], [], 0, 2
+        collect_kernel,
+        "collect",
+        [result, swap(result, "tensor", 1)],
+        [jax.ShapeDtypeStruct((1, count, rank), BF16)],
+        [],
+        0,
+        2,
     )
     return collected
 

time: 108 us -> 100 us (0.926)
  waiting for transfers between devices: 46.8 us -> 42.6 us
  starting transfers between devices: 41.9 us -> 39.4 us
    ppermute x37 -> x36, waiting for transfers between devices: 45 us -> 39.8 us  [swap(): lax.ppermute(value, axis, [(i, i ^ mask) for i in range(lax.axis_size(axi...]
    ppermute x2, starting transfers between devices: 6.93 us -> 4.05 us  [onward(): lax.ppermute(value, 'segment', [(i, (i ^ flip) + 2) for i in range(size -...]
    ppermute x2, waiting for transfers between devices: 1.72 us -> 2.81 us  [onward(): lax.ppermute(value, 'segment', [(i, (i ^ flip) + 2) for i in range(size -...]
    ppermute x37 -> x36, starting transfers between devices: 35 us -> 35.3 us  [swap(): lax.ppermute(value, axis, [(i, i ^ mask) for i in range(lax.axis_size(axi...]
  transfers between devices with their start and end apart: 39 -> 38, of which waited for: 26 -> 22; matrix products, arithmetic and copies ran while one was open for 0% -> 0% of each run, Pallas kernels for 13% -> 13%
where the time goes in v3:
time: 100 us
  waiting for transfers between devices  42.6 us (43%)
  starting transfers between devices  39.4 us (39%)
  Pallas kernels  16 us (16%)
  local copies, waits for them, and re-layouts  1.77 us (2%)
    ppermute x36, waiting for transfers between devices, swap(): lax.ppermute(value, axis, [(i, i ^ mask) for i in range(lax.axis_size(axi...  39.8 us
    ppermute x36, starting transfers between devices, swap(): lax.ppermute(value, axis, [(i, i ^ mask) for i in range(lax.axis_size(axi...  35.3 us
    pallas_call x1, Pallas kernels, fetch_rows(): pl.pallas_call(functools.partial(fetch_kernel, block_rows, vocab), out_sh...  8.86 us
    pallas_call x12, Pallas kernels, kernel_call(): pl.pallas_call(functools.partial(kernel, lax.axis_size('tensor') // 2), o...  7.13 us
    ppermute x2, starting transfers between devices, onward(): lax.ppermute(value, 'segment', [(i, (i ^ flip) + 2) for i in range(size -...  4.05 us
    ppermute x2, waiting for transfers between devices, onward(): lax.ppermute(value, 'segment', [(i, (i ^ flip) + 2) for i in range(size -...  2.81 us
  transfers between devices with their start and end apart: 38, of which 22 were waited for; matrix products, arithmetic and copies ran while one was open for 0% of the time, Pallas kernels for 13%

profile of v3, /device:TPU:0, one launch (start us, length us, event | category | flops | bytes accessed | tf_op | source)
XLA Modules:
  0.0 100.0 jit_solution(7855994363943670404)
XLA Ops:
  0.0 1.0 %copy-done = bf16[512,512]{1,0:T(8,128)(2,1)S(1)} copy-done((bf16[512,512]{1,0:T(8,128)(2,1)S(1)}, bf16[512,512]{1,0:T(8,128)(2,1)}, u32[]{:S(2)}) %copy-start) | copy-done | bytes 524312
  1.1 5.1 %collective-permute-start.2 = (bf16[128,512]{1,0:T(8,128)(2,1)S(1)}, bf16[128,512]{1,0:T(8,128)(2,1)S(1)}, u32[]{:S(2)}, u32[]{:S(2)}) collective-permute-start(bf16[128,512]{1,0:T(8,128)(2,1)S(1)} %constant_dynamic-slice_fusion), channel_id=1, source_target_pairs={{0,6},{1,7},{2,4},{3,5},{4,2},{5,3},{6,0},{7,1},{8,14},{9,15},{10,... | collective-permute-start | bytes 393224 | tf_op jit(solution)/shard_map/ppermute | solution.py:20
  6.2 0.6 collective-permute-start
  6.8 0.7 copy-done.3
  7.5 8.9 %fetch_rows.1 = (bf16[48,512]{1,0:T(8,128)(2,1)S(1)}, bf16[48,512]{1,0:T(8,128)(2,1)S(1)}, bf16[48,512]{1,0:T(8,128)(2,1)S(1)}, bf16[48,512]{1,0:T(8,128)(2,1)S(...) custom-call(s32[192]{0:T(256)S(1)} %copy-done.3, s32[1,192]{1,0:T(1,128)S(1)} %bitcast.9, ...), custom_call_target="tpu_custom_call" | custom-call | tf_op jit(solution)/shard_map/fetch_rows/pallas_call | solution.py:153
  16.4 0.0 collective-permute-done.2
  16.4 0.9 collective-permute-done.1
  17.2 1.5 %collective-permute-start.3 = (bf16[48,512]{1,0:T(8,128)(2,1)S(1)}, bf16[48,512]{1,0:T(8,128)(2,1)S(1)}, u32[]{:S(2)}, u32[]{:S(2)}) collective-permute-start(bf16[48,512]{1,0:T(8,128)(2,1)S(1)} %get-tuple-element.51), channel_id=1, source_target_pairs={{0,8},{8,0},{16,24},{24,16},{1,9},{9,1},{17,25},{25,17},{2,10},{10... | collective-permute-start | bytes 147464 | tf_op jit(solution)/shard_map/ppermute | solution.py:20
  18.7 1.5 %collective-permute-start.4 = (bf16[48,512]{1,0:T(8,128)(2,1)S(1)}, bf16[48,512]{1,0:T(8,128)(2,1)S(1)}, u32[]{:S(2)}, u32[]{:S(2)}) collective-permute-start(bf16[48,512]{1,0:T(8,128)(2,1)S(1)} %get-tuple-element.57), channel_id=1, source_target_pairs={{0,16},{8,24},{16,0},{24,8},{1,17},{9,25},{17,1},{25,9},{2,18},{10... | collective-permute-start | bytes 147464 | tf_op jit(solution)/shard_map/ppermute | solution.py:20
  20.3 0.5 collective-permute-start.5
  20.7 0.1 pad_maximum_fusion.refs_0_
  20.8 0.5 collective-permute-done.3
  21.3 1.5 %collective-permute-start.11 = (bf16[4,128,512]{2,1,0:T(8,128)(2,1)S(1)}, bf16[4,128,512]{2,1,0:T(8,128)(2,1)S(1)}, u32[]{:S(2)}, u32[]{:S(2)}) collective-permute-start(bf16[4,128,512]{2,1,0:T(8,128)(2,1)S(1)} %pad_maximum_fusion.refs_0_), channel_id=1, source_target_pairs={{0,16},{8,24},{16,0},{24,8},{1,17},{9,25},{17,1},{25,9},{2,18},{10... | collective-permute-start | bytes 1572872 | tf_op jit(solution)/shard_map/ppermute | solution.py:20
  22.9 1.6 %collective-permute-start.10 = (bf16[4,128,512]{2,1,0:T(8,128)(2,1)S(1)}, bf16[4,128,512]{2,1,0:T(8,128)(2,1)S(1)}, u32[]{:S(2)}, u32[]{:S(2)}) collective-permute-start(bf16[4,128,512]{2,1,0:T(8,128)(2,1)S(1)} %pad_maximum_fusion.refs_0_), channel_id=1, source_target_pairs={{0,8},{8,0},{16,24},{24,16},{1,9},{9,1},{17,25},{25,17},{2,10},{10... | collective-permute-start | bytes 1572872 | tf_op jit(solution)/shard_map/ppermute | solution.py:20
  24.5 1.3 %collective-permute-done.5 = bf16[48,512]{1,0:T(8,128)(2,1)S(1)} collective-permute-done((bf16[48,512]{1,0:T(8,128)(2,1)S(1)}, bf16[48,512]{1,0:T(8,128)(2,1)S(1)}, u32[]{:S(2)}, u32[]{:S(2)}) %collective-permute-start.5) | collective-permute-done | bytes 49184 | tf_op jit(solution)/shard_map/ppermute | solution.py:20
  25.9 3.5 %collective-permute-start.8 = (bf16[48,512]{1,0:T(8,128)(2,1)S(1)}, bf16[48,512]{1,0:T(8,128)(2,1)S(1)}, u32[]{:S(2)}, u32[]{:S(2)}) collective-permute-start(bf16[48,512]{1,0:T(8,128)(2,1)S(1)} %add_add_fusion), channel_id=1, source_target_pairs={{0,6},{1,7},{2,4},{3,5},{4,2},{5,3},{6,0},{7,1},{8,14},{9,15},{10,... | collective-permute-start | bytes 147464 | tf_op jit(solution)/shard_map/ppermute | solution.py:20
  29.4 0.0 collective-permute-start.7
  29.4 0.9 collective-permute-start.6
  30.3 1.5 %collective-permute-done.8 = bf16[48,512]{1,0:T(8,128)(2,1)S(1)} collective-permute-done((bf16[48,512]{1,0:T(8,128)(2,1)S(1)}, bf16[48,512]{1,0:T(8,128)(2,1)S(1)}, u32[]{:S(2)}, u32[]{:S(2)}) %collective-permute-start.8) | collective-permute-done | bytes 49184 | tf_op jit(solution)/shard_map/ppermute | solution.py:20
  31.8 2.6 %collective-permute-done.7 = bf16[48,512]{1,0:T(8,128)(2,1)S(1)} collective-permute-done((bf16[48,512]{1,0:T(8,128)(2,1)S(1)}, bf16[48,512]{1,0:T(8,128)(2,1)S(1)}, u32[]{:S(2)}, u32[]{:S(2)}) %collective-permute-start.7) | collective-permute-done | bytes 49184 | tf_op jit(solution)/shard_map/ppermute | solution.py:20
  34.4 0.0 collective-permute-done.6
  34.4 0.6 collective-permute-start.13
  35.0 0.0 collective-permute-start.12
  35.0 3.0 %collective-permute-start.9 = (bf16[4,48,512]{2,1,0:T(8,128)(2,1)S(1)}, bf16[4,48,512]{2,1,0:T(8,128)(2,1)S(1)}, u32[]{:S(2)}, u32[]{:S(2)}) collective-permute-start(bf16[4,48,512]{2,1,0:T(8,128)(2,1)S(1)} %pad_maximum_fusion.1.refs_0_), channel_id=1, source_target_pairs={{0,24},{8,16},{16,8},{24,0},{1,25},{9,17},{17,9},{25,1},{2,26},{10... | collective-permute-start | bytes 589832 | tf_op jit(solution)/shard_map/ppermute | solution.py:20
  38.0 3.2 %collective-permute-done.13.refs_2_ = bf16[4,48,512]{2,1,0:T(8,128)(2,1)S(1)} collective-permute-done((bf16[4,48,512]{2,1,0:T(8,128)(2,1)S(1)}, bf16[4,48,512]{2,1,0:T(8,128)(2,1)S(1)}, u32[]{:S(2)}, u32[]{:S(2)}) %collective-permute-start.13) | collective-permute-done | bytes 196640 | tf_op jit(solution)/shard_map/ppermute | solution.py:20
  41.2 0.1 collective-permute-done.12.refs_1_
  41.3 0.4 collective-permute-start.16
  41.7 2.0 %collective-permute-done.9.refs_3_ = bf16[4,48,512]{2,1,0:T(8,128)(2,1)S(1)} collective-permute-done((bf16[4,48,512]{2,1,0:T(8,128)(2,1)S(1)}, bf16[4,48,512]{2,1,0:T(8,128)(2,1)S(1)}, u32[]{:S(2)}, u32[]{:S(2)}) %collective-permute-start.9) | collective-permute-done | bytes 196640 | tf_op jit(solution)/shard_map/ppermute | solution.py:20
  43.7 0.5 collective-permute-start.17
  44.3 0.1 collective-permute-start.21
  44.4 0.5 collective-permute-start.22
  44.9 1.1 %collective-permute-start.19 = (bf16[2,128,512]{2,1,0:T(8,128)(2,1)S(1)}, bf16[2,128,512]{2,1,0:T(8,128)(2,1)S(1)}, u32[]{:S(2)}, u32[]{:S(2)}) collective-permute-start(bf16[2,128,512]{2,1,0:T(8,128)(2,1)S(1)} %slice.7), channel_id=1, source_target_pairs={{0,8},{8,0},{16,24},{24,16},{1,9},{9,1},{17,25},{25,17},{2,10},{10... | collective-permute-start | bytes 786440 | tf_op jit(solution)/shard_map/ppermute | solution.py:20
  46.1 1.1 %collective-permute-start.18 = (bf16[2,128,512]{2,1,0:T(8,128)(2,1)S(1)}, bf16[2,128,512]{2,1,0:T(8,128)(2,1)S(1)}, u32[]{:S(2)}, u32[]{:S(2)}) collective-permute-start(bf16[2,128,512]{2,1,0:T(8,128)(2,1)S(1)} %slice.6), channel_id=1, source_target_pairs={{0,16},{8,24},{16,0},{24,8},{1,17},{9,25},{17,1},{25,9},{2,18},{10... | collective-permute-start | bytes 786440 | tf_op jit(solution)/shard_map/ppermute | solution.py:20
  47.2 3.9 %section_first.1 = (bf16[192,4096]{1,0:T(8,128)(2,1)S(1)}, bf16[192,4096]{1,0:T(8,128)(2,1)S(1)}, f32[192,896]{1,0:T(8,128)S(1)}, f32[192,1]{1,0:T(8,128)S(1)}) custom-call(bf16[4,48,512]{2,1,0:T(8,128)(2,1)S(1)} %pad_maximum_fusion.1.refs_0_, bf16[4,48,512]{2,1,0:T(8,128)(2,1)S(1)} %collective-permute-done.12.refs_1_, ...), custom_call_target="tpu_custom_call" | custom-call | flops 2818572288 | tf_op jit(solution)/shard_map/section_first/pallas_call | solution.py:335
  51.1 2.1 %collective-permute-done.19.refs_4_ = bf16[2,128,512]{2,1,0:T(8,128)(2,1)S(1)} collective-permute-done((bf16[2,128,512]{2,1,0:T(8,128)(2,1)S(1)}, bf16[2,128,512]{2,1,0:T(8,128)(2,1)S(1)}, u32[]{:S(2)}, u32[]{:S(2)}) %collective-permute-start.19) | collective-permute-done | bytes 262176 | tf_op jit(solution)/shard_map/ppermute | solution.py:20
  53.2 0.8 collective-permute-done.18.refs_3_
  54.1 0.5 collective-permute-start.24
  54.6 1.0 %collective-permute-done.23.refs_8_ = bf16[2,128,512]{2,1,0:T(8,128)(2,1)S(1)} collective-permute-done((bf16[2,128,512]{2,1,0:T(8,128)(2,1)S(1)}, bf16[2,128,512]{2,1,0:T(8,128)(2,1)S(1)}, u32[]{:S(2)}, u32[]{:S(2)}) %collective-permute-start.23) | collective-permute-done | bytes 262176 | tf_op jit(solution)/shard_map/ppermute | solution.py:20
  55.6 0.4 collective-permute-done.24.refs_9_
  56.0 1.4 %project_first.1 = (bf16[96,512]{1,0:T(8,128)(2,1)S(1)}, bf16[96,512]{1,0:T(8,128)(2,1)S(1)}, bf16[4096,512]{1,0:T(8,128)(2,1)S(1)}) custom-call(bf16[4,128,512]{2,1,0:T(8,128)(2,1)S(1)} %pad_maximum_fusion.refs_0_, bf16[4,128,512]{2,1,0:T(8,128)(2,1)S(1)} %collective-permute-done.10.refs_1_, bf16[4,128,512]{2,1,0:T(8,128)(2,1)S(1)} %collective-permute-done.11.refs_2_, ...), custom_call_target="tpu_custom_call" | custom-call | flops 805306368 | tf_op jit(solution)/shard_map/project_first/pallas_call | solution.py:335
  57.4 0.2 collective-permute-start.25
  57.6 1.2 %collective-permute-done.25.refs_1_ = bf16[96,512]{1,0:T(8,128)(2,1)S(1)} collective-permute-done((bf16[96,512]{1,0:T(8,128)(2,1)S(1)}, bf16[96,512]{1,0:T(8,128)(2,1)S(1)}, u32[]{:S(2)}, u32[]{:S(2)}) %collective-permute-start.25) | collective-permute-done | bytes 98336 | tf_op jit(solution)/shard_map/ppermute | solution.py:20
  58.7 3.4 %collective-permute-start.28 = (bf16[96,512]{1,0:T(8,128)(2,1)S(1)}, bf16[96,512]{1,0:T(8,128)(2,1)S(1)}, u32[]{:S(2)}, u32[]{:S(2)}) collective-permute-start(bf16[96,512]{1,0:T(8,128)(2,1)S(1)} %add.29.refs_0_), channel_id=1, source_target_pairs={{0,6},{1,7},{2,4},{3,5},{4,2},{5,3},{6,0},{7,1},{8,14},{9,15},{10,... | collective-permute-start | bytes 294920 | tf_op jit(solution)/shard_map/ppermute | solution.py:20
  62.2 1.0 %collective-permute-start.26 = (bf16[96,512]{1,0:T(8,128)(2,1)S(1)}, bf16[96,512]{1,0:T(8,128)(2,1)S(1)}, u32[]{:S(2)}, u32[]{:S(2)}) collective-permute-start(bf16[96,512]{1,0:T(8,128)(2,1)S(1)} %add.29.refs_0_), channel_id=1, source_target_pairs={{0,2},{1,3},{2,0},{3,1},{4,6},{5,7},{6,4},{7,5},{8,10},{9,11},{10,... | collective-permute-start | bytes 294920 | tf_op jit(solution)/shard_map/ppermute | solution.py:20
  63.2 3.1 %collective-permute-done.28.refs_3_ = bf16[96,512]{1,0:T(8,128)(2,1)S(1)} collective-permute-done((bf16[96,512]{1,0:T(8,128)(2,1)S(1)}, bf16[96,512]{1,0:T(8,128)(2,1)S(1)}, u32[]{:S(2)}, u32[]{:S(2)}) %collective-permute-start.28) | collective-permute-done | bytes 98336 | tf_op jit(solution)/shard_map/ppermute | solution.py:20
  66.4 4.3 %collective-permute-done.27.refs_2_ = bf16[96,512]{1,0:T(8,128)(2,1)S(1)} collective-permute-done((bf16[96,512]{1,0:T(8,128)(2,1)S(1)}, bf16[96,512]{1,0:T(8,128)(2,1)S(1)}, u32[]{:S(2)}, u32[]{:S(2)}) %collective-permute-start.27) | collective-permute-done | bytes 98336 | tf_op jit(solution)/shard_map/ppermute | solution.py:20
  70.7 0.1 add.30.after
  70.8 2.8 %collective-permute-start.30 = (bf16[96,512]{1,0:T(8,128)(2,1)S(1)}, bf16[96,512]{1,0:T(8,128)(2,1)S(1)}, u32[]{:S(2)}, u32[]{:S(2)}) collective-permute-start(bf16[96,512]{1,0:T(8,128)(2,1)S(1)} %add.30.after), channel_id=1, source_target_pairs={{0,24},{8,16},{1,25},{9,17},{2,26},{10,18},{3,27},{11,19},{4,28},{... | collective-permute-start | bytes 294920 | tf_op jit(solution)/shard_map/ppermute | solution.py:25
  73.5 1.3 %collective-permute-start.29 = (bf16[96,512]{1,0:T(8,128)(2,1)S(1)}, bf16[96,512]{1,0:T(8,128)(2,1)S(1)}, u32[]{:S(2)}, u32[]{:S(2)}) collective-permute-start(bf16[96,512]{1,0:T(8,128)(2,1)S(1)} %add.30.after), channel_id=1, source_target_pairs={{0,16},{8,24},{1,17},{9,25},{2,18},{10,26},{3,19},{11,27},{4,20},{... | collective-permute-start | bytes 294920 | tf_op jit(solution)/shard_map/ppermute | solution.py:25
  74.8 2.8 %collective-permute-done.29.refs_0_ = bf16[96,512]{1,0:T(8,128)(2,1)S(1)} collective-permute-done((bf16[96,512]{1,0:T(8,128)(2,1)S(1)}, bf16[96,512]{1,0:T(8,128)(2,1)S(1)}, u32[]{:S(2)}, u32[]{:S(2)}) %collective-permute-start.29) | collective-permute-done | bytes 98336 | tf_op jit(solution)/shard_map/ppermute | solution.py:25
  77.7 0.1 collective-permute-start.31
  77.8 1.3 %collective-permute-done.31.refs_1_ = bf16[96,512]{1,0:T(8,128)(2,1)S(1)} collective-permute-done((bf16[96,512]{1,0:T(8,128)(2,1)S(1)}, bf16[96,512]{1,0:T(8,128)(2,1)S(1)}, u32[]{:S(2)}, u32[]{:S(2)}) %collective-permute-start.31) | collective-permute-done | bytes 98336 | tf_op jit(solution)/shard_map/ppermute | solution.py:20
  79.1 1.0 section_next.1
  80.1 0.2 collective-permute-start.32
  80.3 1.1 %collective-permute-done.32.refs_1_ = bf16[96,512]{1,0:T(8,128)(2,1)S(1)} collective-permute-done((bf16[96,512]{1,0:T(8,128)(2,1)S(1)}, bf16[96,512]{1,0:T(8,128)(2,1)S(1)}, u32[]{:S(2)}, u32[]{:S(2)}) %collective-permute-start.32) | collective-permute-done | bytes 98336 | tf_op jit(solution)/shard_map/ppermute | solution.py:20
  81.4 3.2 %collective-permute-start.35 = (bf16[96,512]{1,0:T(8,128)(2,1)S(1)}, bf16[96,512]{1,0:T(8,128)(2,1)S(1)}, u32[]{:S(2)}, u32[]{:S(2)}) collective-permute-start(bf16[96,512]{1,0:T(8,128)(2,1)S(1)} %add.32.refs_0_), channel_id=1, source_target_pairs={{0,6},{1,7},{2,4},{3,5},{4,2},{5,3},{6,0},{7,1},{8,14},{9,15},{10,... | collective-permute-start | bytes 294920 | tf_op jit(solution)/shard_map/ppermute | solution.py:20
  84.7 1.2 %collective-permute-start.33 = (bf16[96,512]{1,0:T(8,128)(2,1)S(1)}, bf16[96,512]{1,0:T(8,128)(2,1)S(1)}, u32[]{:S(2)}, u32[]{:S(2)}) collective-permute-start(bf16[96,512]{1,0:T(8,128)(2,1)S(1)} %add.32.refs_0_), channel_id=1, source_target_pairs={{0,2},{1,3},{2,0},{3,1},{4,6},{5,7},{6,4},{7,5},{8,10},{9,11},{10,... | collective-permute-start | bytes 294920 | tf_op jit(solution)/shard_map/ppermute | solution.py:20
  85.9 3.1 %collective-permute-done.35.refs_3_ = bf16[96,512]{1,0:T(8,128)(2,1)S(1)} collective-permute-done((bf16[96,512]{1,0:T(8,128)(2,1)S(1)}, bf16[96,512]{1,0:T(8,128)(2,1)S(1)}, u32[]{:S(2)}, u32[]{:S(2)}) %collective-permute-start.35) | collective-permute-done | bytes 98336 | tf_op jit(solution)/shard_map/ppermute | solution.py:20
  89.1 4.1 %collective-permute-done.34.refs_2_ = bf16[96,512]{1,0:T(8,128)(2,1)S(1)} collective-permute-done((bf16[96,512]{1,0:T(8,128)(2,1)S(1)}, bf16[96,512]{1,0:T(8,128)(2,1)S(1)}, u32[]{:S(2)}, u32[]{:S(2)}) %collective-permute-start.34) | collective-permute-done | bytes 98336 | tf_op jit(solution)/shard_map/ppermute | solution.py:20
  93.2 1.1 %collective-permute-start.36 = (bf16[96,512]{1,0:T(8,128)(2,1)S(1)}, bf16[96,512]{1,0:T(8,128)(2,1)S(1)}, u32[]{:S(2)}, u32[]{:S(2)}) collective-permute-start(bf16[96,512]{1,0:T(8,128)(2,1)S(1)} %choose.1.refs_0_), channel_id=1, source_target_pairs={{0,8},{8,0},{16,24},{24,16},{1,9},{9,1},{17,25},{25,17},{2,10},{10... | collective-permute-start | bytes 294920 | tf_op jit(solution)/shard_map/ppermute | solution.py:20
  94.3 3.6 %collective-permute-done.36.refs_1_ = bf16[96,512]{1,0:T(8,128)(2,1)S(1)} collective-permute-done((bf16[96,512]{1,0:T(8,128)(2,1)S(1)}, bf16[96,512]{1,0:T(8,128)(2,1)S(1)}, u32[]{:S(2)}, u32[]{:S(2)}) %collective-permute-start.36) | collective-permute-done | bytes 98336 | tf_op jit(solution)/shard_map/ppermute | solution.py:20
  97.9 0.1 collective-permute-start.37
  98.0 1.3 %collective-permute-done.37.far = bf16[96,512]{1,0:T(8,128)(2,1)S(1)} collective-permute-done((bf16[96,512]{1,0:T(8,128)(2,1)S(1)}, bf16[96,512]{1,0:T(8,128)(2,1)S(1)}, u32[]{:S(2)}, u32[]{:S(2)}) %collective-permute-start.37) | collective-permute-done | bytes 98336 | tf_op jit(solution)/shard_map/ppermute | solution.py:20
  99.3 0.7 collect.1
  (39 shorter events, 0.3 us)
Async XLA Ops:
  0.0 1.0 %copy-start = (bf16[512,512]{1,0:T(8,128)(2,1)S(1)}, bf16[512,512]{1,0:T(8,128)(2,1)}, u32[]{:S(2)}) copy-start(bf16[512,512]{1,0:T(8,128)(2,1)} %param.11) | copy-start | bytes 1572868
  1.1 15.3 %collective-permute-start.2 = (bf16[128,512]{1,0:T(8,128)(2,1)S(1)}, bf16[128,512]{1,0:T(8,128)(2,1)S(1)}, u32[]{:S(2)}, u32[]{:S(2)}) collective-permute-start(bf16[128,512]{1,0:T(8,128)(2,1)S(1)} %constant_dynamic-slice_fusion), channel_id=1, source_target_pairs={{0,6},{1,7},{2,4},{3,5},{4,2},{5,3},{6,0},{7,1},{8,14},{9,15},{10,... | collective-permute-start | bytes 393224 | tf_op jit(solution)/shard_map/ppermute | solution.py:20
  6.2 11.1 %collective-permute-start.1 = (bf16[128,512]{1,0:T(8,128)(2,1)S(1)}, bf16[128,512]{1,0:T(8,128)(2,1)S(1)}, u32[]{:S(2)}, u32[]{:S(2)}) collective-permute-start(bf16[128,512]{1,0:T(8,128)(2,1)S(1)} %constant_dynamic-slice_fusion), channel_id=1, source_target_pairs={{0,4},{1,5},{2,6},{3,7},{4,0},{5,1},{6,2},{7,3},{8,12},{9,13},{10,... | collective-permute-start | bytes 393224 | tf_op jit(solution)/shard_map/ppermute | solution.py:20
  6.2 11.1 %collective-permute-start = (bf16[128,512]{1,0:T(8,128)(2,1)S(1)}, bf16[128,512]{1,0:T(8,128)(2,1)S(1)}, u32[]{:S(2)}, u32[]{:S(2)}) collective-permute-start(bf16[128,512]{1,0:T(8,128)(2,1)S(1)} %constant_dynamic-slice_fusion), channel_id=1, source_target_pairs={{0,2},{1,3},{2,0},{3,1},{4,6},{5,7},{6,4},{7,5},{8,10},{9,11},{10,... | collective-permute-start | bytes 393224 | tf_op jit(solution)/shard_map/ppermute | solution.py:20
  6.8 0.7 copy-start.3
  7.5 39.7 %copy-start.2 = (f32[2,4096]{1,0:T(2,128)S(1)}, f32[2,4096]{1,0:T(2,128)}, u32[]{:S(2)}) copy-start(f32[2,4096]{1,0:T(2,128)} %refs_2_.1) | copy-start | bytes 98308
  17.2 4.1 %collective-permute-start.3 = (bf16[48,512]{1,0:T(8,128)(2,1)S(1)}, bf16[48,512]{1,0:T(8,128)(2,1)S(1)}, u32[]{:S(2)}, u32[]{:S(2)}) collective-permute-start(bf16[48,512]{1,0:T(8,128)(2,1)S(1)} %get-tuple-element.51), channel_id=1, source_target_pairs={{0,8},{8,0},{16,24},{24,16},{1,9},{9,1},{17,25},{25,17},{2,10},{10... | collective-permute-start | bytes 147464 | tf_op jit(solution)/shard_map/ppermute | solution.py:20
  18.7 5.8 %collective-permute-start.4 = (bf16[48,512]{1,0:T(8,128)(2,1)S(1)}, bf16[48,512]{1,0:T(8,128)(2,1)S(1)}, u32[]{:S(2)}, u32[]{:S(2)}) collective-permute-start(bf16[48,512]{1,0:T(8,128)(2,1)S(1)} %get-tuple-element.57), channel_id=1, source_target_pairs={{0,16},{8,24},{16,0},{24,8},{1,17},{9,25},{17,1},{25,9},{2,18},{10... | collective-permute-start | bytes 147464 | tf_op jit(solution)/shard_map/ppermute | solution.py:20
  20.3 5.6 %collective-permute-start.5 = (bf16[48,512]{1,0:T(8,128)(2,1)S(1)}, bf16[48,512]{1,0:T(8,128)(2,1)S(1)}, u32[]{:S(2)}, u32[]{:S(2)}) collective-permute-start(bf16[48,512]{1,0:T(8,128)(2,1)S(1)} %get-tuple-element.58), channel_id=1, source_target_pairs={{0,24},{8,16},{16,8},{24,0},{1,25},{9,17},{17,9},{25,1},{2,26},{10... | collective-permute-start | bytes 147464 | tf_op jit(solution)/shard_map/ppermute | solution.py:20
  21.3 22.4 %collective-permute-start.11 = (bf16[4,128,512]{2,1,0:T(8,128)(2,1)S(1)}, bf16[4,128,512]{2,1,0:T(8,128)(2,1)S(1)}, u32[]{:S(2)}, u32[]{:S(2)}) collective-permute-start(bf16[4,128,512]{2,1,0:T(8,128)(2,1)S(1)} %pad_maximum_fusion.refs_0_), channel_id=1, source_target_pairs={{0,16},{8,24},{16,0},{24,8},{1,17},{9,25},{17,1},{25,9},{2,18},{10... | collective-permute-start | bytes 1572872 | tf_op jit(solution)/shard_map/ppermute | solution.py:20
  22.9 20.9 %collective-permute-start.10 = (bf16[4,128,512]{2,1,0:T(8,128)(2,1)S(1)}, bf16[4,128,512]{2,1,0:T(8,128)(2,1)S(1)}, u32[]{:S(2)}, u32[]{:S(2)}) collective-permute-start(bf16[4,128,512]{2,1,0:T(8,128)(2,1)S(1)} %pad_maximum_fusion.refs_0_), channel_id=1, source_target_pairs={{0,8},{8,0},{16,24},{24,16},{1,9},{9,1},{17,25},{25,17},{2,10},{10... | collective-permute-start | bytes 1572872 | tf_op jit(solution)/shard_map/ppermute | solution.py:20
  25.9 6.0 %collective-permute-start.8 = (bf16[48,512]{1,0:T(8,128)(2,1)S(1)}, bf16[48,512]{1,0:T(8,128)(2,1)S(1)}, u32[]{:S(2)}, u32[]{:S(2)}) collective-permute-start(bf16[48,512]{1,0:T(8,128)(2,1)S(1)} %add_add_fusion), channel_id=1, source_target_pairs={{0,6},{1,7},{2,4},{3,5},{4,2},{5,3},{6,0},{7,1},{8,14},{9,15},{10,... | collective-permute-start | bytes 147464 | tf_op jit(solution)/shard_map/ppermute | solution.py:20
  29.4 5.0 %collective-permute-start.7 = (bf16[48,512]{1,0:T(8,128)(2,1)S(1)}, bf16[48,512]{1,0:T(8,128)(2,1)S(1)}, u32[]{:S(2)}, u32[]{:S(2)}) collective-permute-start(bf16[48,512]{1,0:T(8,128)(2,1)S(1)} %add_add_fusion), channel_id=1, source_target_pairs={{0,4},{1,5},{2,6},{3,7},{4,0},{5,1},{6,2},{7,3},{8,12},{9,13},{10,... | collective-permute-start | bytes 147464 | tf_op jit(solution)/shard_map/ppermute | solution.py:20
  29.4 5.0 %collective-permute-start.6 = (bf16[48,512]{1,0:T(8,128)(2,1)S(1)}, bf16[48,512]{1,0:T(8,128)(2,1)S(1)}, u32[]{:S(2)}, u32[]{:S(2)}) collective-permute-start(bf16[48,512]{1,0:T(8,128)(2,1)S(1)} %add_add_fusion), channel_id=1, source_target_pairs={{0,2},{1,3},{2,0},{3,1},{4,6},{5,7},{6,4},{7,5},{8,10},{9,11},{10,... | collective-permute-start | bytes 147464 | tf_op jit(solution)/shard_map/ppermute | solution.py:20
  34.4 6.8 %collective-permute-start.13 = (bf16[4,48,512]{2,1,0:T(8,128)(2,1)S(1)}, bf16[4,48,512]{2,1,0:T(8,128)(2,1)S(1)}, u32[]{:S(2)}, u32[]{:S(2)}) collective-permute-start(bf16[4,48,512]{2,1,0:T(8,128)(2,1)S(1)} %pad_maximum_fusion.1.refs_0_), channel_id=1, source_target_pairs={{0,16},{8,24},{16,0},{24,8},{1,17},{9,25},{17,1},{25,9},{2,18},{10... | collective-permute-start | bytes 589832 | tf_op jit(solution)/shard_map/ppermute | solution.py:20
  35.0 6.3 %collective-permute-start.12 = (bf16[4,48,512]{2,1,0:T(8,128)(2,1)S(1)}, bf16[4,48,512]{2,1,0:T(8,128)(2,1)S(1)}, u32[]{:S(2)}, u32[]{:S(2)}) collective-permute-start(bf16[4,48,512]{2,1,0:T(8,128)(2,1)S(1)} %pad_maximum_fusion.1.refs_0_), channel_id=1, source_target_pairs={{0,8},{8,0},{16,24},{24,16},{1,9},{9,1},{17,25},{25,17},{2,10},{10... | collective-permute-start | bytes 589832 | tf_op jit(solution)/shard_map/ppermute | solution.py:20
  35.0 8.7 %collective-permute-start.9 = (bf16[4,48,512]{2,1,0:T(8,128)(2,1)S(1)}, bf16[4,48,512]{2,1,0:T(8,128)(2,1)S(1)}, u32[]{:S(2)}, u32[]{:S(2)}) collective-permute-start(bf16[4,48,512]{2,1,0:T(8,128)(2,1)S(1)} %pad_maximum_fusion.1.refs_0_), channel_id=1, source_target_pairs={{0,24},{8,16},{16,8},{24,0},{1,25},{9,17},{17,9},{25,1},{2,26},{10... | collective-permute-start | bytes 589832 | tf_op jit(solution)/shard_map/ppermute | solution.py:20
  41.2 3.2 %collective-permute-start.14 = (bf16[4,48,512]{2,1,0:T(8,128)(2,1)S(1)}, bf16[4,48,512]{2,1,0:T(8,128)(2,1)S(1)}, u32[]{:S(2)}, u32[]{:S(2)}) collective-permute-start(bf16[4,48,512]{2,1,0:T(8,128)(2,1)S(1)} %pad_maximum_fusion.1.refs_0_), channel_id=1, source_target_pairs={{0,1},{1,0},{2,3},{3,2},{4,5},{5,4},{6,7},{7,6},{8,9},{9,8},{10,11... | collective-permute-start | bytes 589832 | tf_op jit(solution)/shard_map/ppermute | solution.py:20
  41.3 3.6 %collective-permute-start.16 = (bf16[4,48,512]{2,1,0:T(8,128)(2,1)S(1)}, bf16[4,48,512]{2,1,0:T(8,128)(2,1)S(1)}, u32[]{:S(2)}, u32[]{:S(2)}) collective-permute-start(bf16[4,48,512]{2,1,0:T(8,128)(2,1)S(1)} %collective-permute-done.13.refs_2_), channel_id=1, source_target_pairs={{0,1},{1,0},{2,3},{3,2},{4,5},{5,4},{6,7},{7,6},{8,9},{9,8},{10,11... | collective-permute-start | bytes 589832 | tf_op jit(solution)/shard_map/ppermute | solution.py:20
  43.7 2.3 %collective-permute-start.15 = (bf16[4,48,512]{2,1,0:T(8,128)(2,1)S(1)}, bf16[4,48,512]{2,1,0:T(8,128)(2,1)S(1)}, u32[]{:S(2)}, u32[]{:S(2)}) collective-permute-start(bf16[4,48,512]{2,1,0:T(8,128)(2,1)S(1)} %collective-permute-done.12.refs_1_), channel_id=1, source_target_pairs={{0,1},{1,0},{2,3},{3,2},{4,5},{5,4},{6,7},{7,6},{8,9},{9,8},{10,11... | collective-permute-start | bytes 589832 | tf_op jit(solution)/shard_map/ppermute | solution.py:20
  43.7 3.4 %collective-permute-start.17 = (bf16[4,48,512]{2,1,0:T(8,128)(2,1)S(1)}, bf16[4,48,512]{2,1,0:T(8,128)(2,1)S(1)}, u32[]{:S(2)}, u32[]{:S(2)}) collective-permute-start(bf16[4,48,512]{2,1,0:T(8,128)(2,1)S(1)} %collective-permute-done.9.refs_3_), channel_id=1, source_target_pairs={{0,1},{1,0},{2,3},{3,2},{4,5},{5,4},{6,7},{7,6},{8,9},{9,8},{10,11... | collective-permute-start | bytes 589832 | tf_op jit(solution)/shard_map/ppermute | solution.py:20
  44.3 10.3 %collective-permute-start.21 = (bf16[4,128,512]{2,1,0:T(8,128)(2,1)S(1)}, bf16[4,128,512]{2,1,0:T(8,128)(2,1)S(1)}, u32[]{:S(2)}, u32[]{:S(2)}) collective-permute-start(bf16[4,128,512]{2,1,0:T(8,128)(2,1)S(1)} %collective-permute-done.10.refs_1_), channel_id=1, source_target_pairs={{0,1},{1,0},{2,3},{3,2},{4,5},{5,4},{6,7},{7,6},{8,9},{9,8},{10,11... | collective-permute-start | bytes 1572872 | tf_op jit(solution)/shard_map/ppermute | solution.py:20
  44.4 10.2 %collective-permute-start.22 = (bf16[4,128,512]{2,1,0:T(8,128)(2,1)S(1)}, bf16[4,128,512]{2,1,0:T(8,128)(2,1)S(1)}, u32[]{:S(2)}, u32[]{:S(2)}) collective-permute-start(bf16[4,128,512]{2,1,0:T(8,128)(2,1)S(1)} %collective-permute-done.11.refs_2_), channel_id=1, source_target_pairs={{0,1},{1,0},{2,3},{3,2},{4,5},{5,4},{6,7},{7,6},{8,9},{9,8},{10,11... | collective-permute-start | bytes 1572872 | tf_op jit(solution)/shard_map/ppermute | solution.py:20
  44.9 8.3 %collective-permute-start.19 = (bf16[2,128,512]{2,1,0:T(8,128)(2,1)S(1)}, bf16[2,128,512]{2,1,0:T(8,128)(2,1)S(1)}, u32[]{:S(2)}, u32[]{:S(2)}) collective-permute-start(bf16[2,128,512]{2,1,0:T(8,128)(2,1)S(1)} %slice.7), channel_id=1, source_target_pairs={{0,8},{8,0},{16,24},{24,16},{1,9},{9,1},{17,25},{25,17},{2,10},{10... | collective-permute-start | bytes 786440 | tf_op jit(solution)/shard_map/ppermute | solution.py:20
  46.1 8.0 %collective-permute-start.18 = (bf16[2,128,512]{2,1,0:T(8,128)(2,1)S(1)}, bf16[2,128,512]{2,1,0:T(8,128)(2,1)S(1)}, u32[]{:S(2)}, u32[]{:S(2)}) collective-permute-start(bf16[2,128,512]{2,1,0:T(8,128)(2,1)S(1)} %slice.6), channel_id=1, source_target_pairs={{0,16},{8,24},{16,0},{24,8},{1,17},{9,25},{17,1},{25,9},{2,18},{10... | collective-permute-start | bytes 786440 | tf_op jit(solution)/shard_map/ppermute | solution.py:20
  47.2 7.4 %collective-permute-start.20 = (bf16[4,128,512]{2,1,0:T(8,128)(2,1)S(1)}, bf16[4,128,512]{2,1,0:T(8,128)(2,1)S(1)}, u32[]{:S(2)}, u32[]{:S(2)}) collective-permute-start(bf16[4,128,512]{2,1,0:T(8,128)(2,1)S(1)} %pad_maximum_fusion.refs_0_), channel_id=1, source_target_pairs={{0,1},{1,0},{2,3},{3,2},{4,5},{5,4},{6,7},{7,6},{8,9},{9,8},{10,11... | collective-permute-start | bytes 1572872 | tf_op jit(solution)/shard_map/ppermute | solution.py:20
  54.1 1.5 %collective-permute-start.23 = (bf16[2,128,512]{2,1,0:T(8,128)(2,1)S(1)}, bf16[2,128,512]{2,1,0:T(8,128)(2,1)S(1)}, u32[]{:S(2)}, u32[]{:S(2)}) collective-permute-start(bf16[2,128,512]{2,1,0:T(8,128)(2,1)S(1)} %collective-permute-done.18.refs_3_), channel_id=1, source_target_pairs={{0,1},{1,0},{2,3},{3,2},{4,5},{5,4},{6,7},{7,6},{8,9},{9,8},{10,11... | collective-permute-start | bytes 786440 | tf_op jit(solution)/shard_map/ppermute | solution.py:20
  54.1 1.9 %collective-permute-start.24 = (bf16[2,128,512]{2,1,0:T(8,128)(2,1)S(1)}, bf16[2,128,512]{2,1,0:T(8,128)(2,1)S(1)}, u32[]{:S(2)}, u32[]{:S(2)}) collective-permute-start(bf16[2,128,512]{2,1,0:T(8,128)(2,1)S(1)} %collective-permute-done.19.refs_4_), channel_id=1, source_target_pairs={{0,1},{1,0},{2,3},{3,2},{4,5},{5,4},{6,7},{7,6},{8,9},{9,8},{10,11... | collective-permute-start | bytes 786440 | tf_op jit(solution)/shard_map/ppermute | solution.py:20
  57.4 1.4 %collective-permute-start.25 = (bf16[96,512]{1,0:T(8,128)(2,1)S(1)}, bf16[96,512]{1,0:T(8,128)(2,1)S(1)}, u32[]{:S(2)}, u32[]{:S(2)}) collective-permute-start(bf16[96,512]{1,0:T(8,128)(2,1)S(1)} %get-tuple-element.71), channel_id=1, source_target_pairs={{0,1},{1,0},{2,3},{3,2},{4,5},{5,4},{6,7},{7,6},{8,9},{9,8},{10,11... | collective-permute-start | bytes 294920 | tf_op jit(solution)/shard_map/ppermute | solution.py:20
  58.7 7.6 %collective-permute-start.28 = (bf16[96,512]{1,0:T(8,128)(2,1)S(1)}, bf16[96,512]{1,0:T(8,128)(2,1)S(1)}, u32[]{:S(2)}, u32[]{:S(2)}) collective-permute-start(bf16[96,512]{1,0:T(8,128)(2,1)S(1)} %add.29.refs_0_), channel_id=1, source_target_pairs={{0,6},{1,7},{2,4},{3,5},{4,2},{5,3},{6,0},{7,1},{8,14},{9,15},{10,... | collective-permute-start | bytes 294920 | tf_op jit(solution)/shard_map/ppermute | solution.py:20
  62.2 8.5 %collective-permute-start.27 = (bf16[96,512]{1,0:T(8,128)(2,1)S(1)}, bf16[96,512]{1,0:T(8,128)(2,1)S(1)}, u32[]{:S(2)}, u32[]{:S(2)}) collective-permute-start(bf16[96,512]{1,0:T(8,128)(2,1)S(1)} %add.29.refs_0_), channel_id=1, source_target_pairs={{0,4},{1,5},{2,6},{3,7},{4,0},{5,1},{6,2},{7,3},{8,12},{9,13},{10,... | collective-permute-start | bytes 294920 | tf_op jit(solution)/shard_map/ppermute | solution.py:20
  62.2 8.5 %collective-permute-start.26 = (bf16[96,512]{1,0:T(8,128)(2,1)S(1)}, bf16[96,512]{1,0:T(8,128)(2,1)S(1)}, u32[]{:S(2)}, u32[]{:S(2)}) collective-permute-start(bf16[96,512]{1,0:T(8,128)(2,1)S(1)} %add.29.refs_0_), channel_id=1, source_target_pairs={{0,2},{1,3},{2,0},{3,1},{4,6},{5,7},{6,4},{7,5},{8,10},{9,11},{10,... | collective-permute-start | bytes 294920 | tf_op jit(solution)/shard_map/ppermute | solution.py:20
  70.7 29.3 %copy-start.1 = (bf16[512,512]{1,0:T(8,128)(2,1)S(1)}, bf16[512,512]{1,0:T(8,128)(2,1)}, u32[]{:S(2)}) copy-start(bf16[512,512]{1,0:T(8,128)(2,1)} %param.11) | copy-start | bytes 1572868
  70.8 6.9 %collective-permute-start.30 = (bf16[96,512]{1,0:T(8,128)(2,1)S(1)}, bf16[96,512]{1,0:T(8,128)(2,1)S(1)}, u32[]{:S(2)}, u32[]{:S(2)}) collective-permute-start(bf16[96,512]{1,0:T(8,128)(2,1)S(1)} %add.30.after), channel_id=1, source_target_pairs={{0,24},{8,16},{1,25},{9,17},{2,26},{10,18},{3,27},{11,19},{4,28},{... | collective-permute-start | bytes 294920 | tf_op jit(solution)/shard_map/ppermute | solution.py:25
  73.5 4.1 %collective-permute-start.29 = (bf16[96,512]{1,0:T(8,128)(2,1)S(1)}, bf16[96,512]{1,0:T(8,128)(2,1)S(1)}, u32[]{:S(2)}, u32[]{:S(2)}) collective-permute-start(bf16[96,512]{1,0:T(8,128)(2,1)S(1)} %add.30.after), channel_id=1, source_target_pairs={{0,16},{8,24},{1,17},{9,25},{2,18},{10,26},{3,19},{11,27},{4,20},{... | collective-permute-start | bytes 294920 | tf_op jit(solution)/shard_map/ppermute | solution.py:25
  77.7 1.4 %collective-permute-start.31 = (bf16[96,512]{1,0:T(8,128)(2,1)S(1)}, bf16[96,512]{1,0:T(8,128)(2,1)S(1)}, u32[]{:S(2)}, u32[]{:S(2)}) collective-permute-start(bf16[96,512]{1,0:T(8,128)(2,1)S(1)} %add.31.refs_0_), channel_id=1, source_target_pairs={{0,1},{1,0},{2,3},{3,2},{4,5},{5,4},{6,7},{7,6},{8,9},{9,8},{10,11... | collective-permute-start | bytes 294920 | tf_op jit(solution)/shard_map/ppermute | solution.py:20
  80.1 1.4 %collective-permute-start.32 = (bf16[96,512]{1,0:T(8,128)(2,1)S(1)}, bf16[96,512]{1,0:T(8,128)(2,1)S(1)}, u32[]{:S(2)}, u32[]{:S(2)}) collective-permute-start(bf16[96,512]{1,0:T(8,128)(2,1)S(1)} %get-tuple-element.86), channel_id=1, source_target_pairs={{0,1},{1,0},{2,3},{3,2},{4,5},{5,4},{6,7},{7,6},{8,9},{9,8},{10,11... | collective-permute-start | bytes 294920 | tf_op jit(solution)/shard_map/ppermute | solution.py:20
  81.4 7.6 %collective-permute-start.35 = (bf16[96,512]{1,0:T(8,128)(2,1)S(1)}, bf16[96,512]{1,0:T(8,128)(2,1)S(1)}, u32[]{:S(2)}, u32[]{:S(2)}) collective-permute-start(bf16[96,512]{1,0:T(8,128)(2,1)S(1)} %add.32.refs_0_), channel_id=1, source_target_pairs={{0,6},{1,7},{2,4},{3,5},{4,2},{5,3},{6,0},{7,1},{8,14},{9,15},{10,... | collective-permute-start | bytes 294920 | tf_op jit(solution)/shard_map/ppermute | solution.py:20
  84.7 8.5 %collective-permute-start.34 = (bf16[96,512]{1,0:T(8,128)(2,1)S(1)}, bf16[96,512]{1,0:T(8,128)(2,1)S(1)}, u32[]{:S(2)}, u32[]{:S(2)}) collective-permute-start(bf16[96,512]{1,0:T(8,128)(2,1)S(1)} %add.32.refs_0_), channel_id=1, source_target_pairs={{0,4},{1,5},{2,6},{3,7},{4,0},{5,1},{6,2},{7,3},{8,12},{9,13},{10,... | collective-permute-start | bytes 294920 | tf_op jit(solution)/shard_map/ppermute | solution.py:20
  84.7 8.5 %collective-permute-start.33 = (bf16[96,512]{1,0:T(8,128)(2,1)S(1)}, bf16[96,512]{1,0:T(8,128)(2,1)S(1)}, u32[]{:S(2)}, u32[]{:S(2)}) collective-permute-start(bf16[96,512]{1,0:T(8,128)(2,1)S(1)} %add.32.refs_0_), channel_id=1, source_target_pairs={{0,2},{1,3},{2,0},{3,1},{4,6},{5,7},{6,4},{7,5},{8,10},{9,11},{10,... | collective-permute-start | bytes 294920 | tf_op jit(solution)/shard_map/ppermute | solution.py:20
  93.2 4.7 %collective-permute-start.36 = (bf16[96,512]{1,0:T(8,128)(2,1)S(1)}, bf16[96,512]{1,0:T(8,128)(2,1)S(1)}, u32[]{:S(2)}, u32[]{:S(2)}) collective-permute-start(bf16[96,512]{1,0:T(8,128)(2,1)S(1)} %choose.1.refs_0_), channel_id=1, source_target_pairs={{0,8},{8,0},{16,24},{24,16},{1,9},{9,1},{17,25},{25,17},{2,10},{10... | collective-permute-start | bytes 294920 | tf_op jit(solution)/shard_map/ppermute | solution.py:20
  97.9 1.4 %collective-permute-start.37 = (bf16[96,512]{1,0:T(8,128)(2,1)S(1)}, bf16[96,512]{1,0:T(8,128)(2,1)S(1)}, u32[]{:S(2)}, u32[]{:S(2)}) collective-permute-start(bf16[96,512]{1,0:T(8,128)(2,1)S(1)} %add.33.near), channel_id=1, source_target_pairs={{0,1},{1,0},{2,3},{3,2},{4,5},{5,4},{6,7},{7,6},{8,9},{9,8},{10,11... | collective-permute-start | bytes 294920 | tf_op jit(solution)/shard_map/ppermute | solution.py:20

commit v4 on v3

--- a/solution.py
+++ b/solution.py
@@ -387,7 +387,7 @@
     shares = [bands] + [swap(bands, "segment", m) for m in range(1, GROUP - 1)]
     along = jnp.stack([complete] + [swap(complete, "tensor", 2 * m) for m in range(1, chips)])
     mine = [along] + [swap(along, "segment", m) for m in range(1, GROUP)]
-    mine[GROUP - 1], shares = lax.optimization_barrier((mine[GROUP - 1], shares))
+    mine[GROUP - 1], _ = lax.optimization_barrier((mine[GROUP - 1], shares))
     shares += [swap(shares[1][: chips // 2], "segment", 2), swap(shares[2][chips // 2 :], "segment", 1)]
     theirs = [swap(piece, "tensor", 1) for piece in mine]
     work = 2 * count * width
@@ -402,7 +402,7 @@
             pltpu.VMEM((count, 1), F32),
         ],
         [],
-        2 * work * hidden,
+        0,
     )
     partial, shares[GROUP - 1], shares[GROUP] = lax.optimization_barrier(
         (partial, shares[GROUP - 1], shares[GROUP])

time: 100 us -> 99.7 us (level)
  no operation moved by 1% of the time
where the time goes in v4:
time: 99.7 us; the launch traced here: 99.4 us
  waiting for transfers between devices  41.9 us (42%)
  starting transfers between devices  39.1 us (39%)
  Pallas kernels  16.3 us (16%)
  local copies, waits for them, and re-layouts  1.77 us (2%)
    ppermute x36, waiting for transfers between devices, swap(): lax.ppermute(value, axis, [(i, i ^ mask) for i in range(lax.axis_size(axi...  39.2 us
    ppermute x36, starting transfers between devices, swap(): lax.ppermute(value, axis, [(i, i ^ mask) for i in range(lax.axis_size(axi...  34.7 us
    pallas_call x1, Pallas kernels, fetch_rows(): pl.pallas_call(functools.partial(fetch_kernel, block_rows, vocab), out_sh...  9.2 us
    pallas_call x12, Pallas kernels, kernel_call(): pl.pallas_call(functools.partial(kernel, lax.axis_size('tensor') // 2), o...  7.12 us
    ppermute x2, starting transfers between devices, onward(): lax.ppermute(value, 'segment', [(i, (i ^ flip) + 2) for i in range(size -...  4.37 us
    ppermute x2, waiting for transfers between devices, onward(): lax.ppermute(value, 'segment', [(i, (i ^ flip) + 2) for i in range(size -...  2.74 us
  transfers between devices with their start and end apart: 38, of which 22 were waited for; matrix products, arithmetic and copies ran while one was open for 0% of the time, Pallas kernels for 13%

profile of v4, /device:TPU:0, one launch (start us, length us, event | category | flops | bytes accessed | tf_op | source)
XLA Modules:
  0.0 99.4 jit_solution(16440408161435658244)
XLA Ops:
  0.0 1.0 %copy-done = bf16[512,512]{1,0:T(8,128)(2,1)S(1)} copy-done((bf16[512,512]{1,0:T(8,128)(2,1)S(1)}, bf16[512,512]{1,0:T(8,128)(2,1)}, u32[]{:S(2)}) %copy-start) | copy-done | bytes 524312
  1.1 5.1 %collective-permute-start.2 = (bf16[128,512]{1,0:T(8,128)(2,1)S(1)}, bf16[128,512]{1,0:T(8,128)(2,1)S(1)}, u32[]{:S(2)}, u32[]{:S(2)}) collective-permute-start(bf16[128,512]{1,0:T(8,128)(2,1)S(1)} %constant_dynamic-slice_fusion), channel_id=1, source_target_pairs={{0,6},{1,7},{2,4},{3,5},{4,2},{5,3},{6,0},{7,1},{8,14},{9,15},{10,... | collective-permute-start | bytes 393224 | tf_op jit(solution)/shard_map/ppermute | solution.py:20
  6.2 0.0 collective-permute-start.1
  6.2 0.6 collective-permute-start
  6.8 0.7 copy-done.3
  7.5 9.2 %fetch_rows.1 = (bf16[48,512]{1,0:T(8,128)(2,1)S(1)}, bf16[48,512]{1,0:T(8,128)(2,1)S(1)}, bf16[48,512]{1,0:T(8,128)(2,1)S(1)}, bf16[48,512]{1,0:T(8,128)(2,1)S(...) custom-call(s32[192]{0:T(256)S(1)} %copy-done.3, s32[1,192]{1,0:T(1,128)S(1)} %bitcast.9, ...), custom_call_target="tpu_custom_call" | custom-call | tf_op jit(solution)/shard_map/fetch_rows/pallas_call | solution.py:153
  16.7 0.0 collective-permute-done.2
  16.7 0.5 collective-permute-done.1
  17.2 1.5 %collective-permute-start.3 = (bf16[48,512]{1,0:T(8,128)(2,1)S(1)}, bf16[48,512]{1,0:T(8,128)(2,1)S(1)}, u32[]{:S(2)}, u32[]{:S(2)}) collective-permute-start(bf16[48,512]{1,0:T(8,128)(2,1)S(1)} %get-tuple-element.47), channel_id=1, source_target_pairs={{0,8},{8,0},{16,24},{24,16},{1,9},{9,1},{17,25},{25,17},{2,10},{10... | collective-permute-start | bytes 147464 | tf_op jit(solution)/shard_map/ppermute | solution.py:20
  18.7 1.5 %collective-permute-start.6 = (bf16[48,512]{1,0:T(8,128)(2,1)S(1)}, bf16[48,512]{1,0:T(8,128)(2,1)S(1)}, u32[]{:S(2)}, u32[]{:S(2)}) collective-permute-start(bf16[48,512]{1,0:T(8,128)(2,1)S(1)} %get-tuple-element.55), channel_id=1, source_target_pairs={{0,16},{8,24},{16,0},{24,8},{1,17},{9,25},{17,1},{25,9},{2,18},{10... | collective-permute-start | bytes 147464 | tf_op jit(solution)/shard_map/ppermute | solution.py:20
  20.3 0.5 collective-permute-start.7
  20.7 0.1 pad_maximum_fusion.refs_0_
  20.8 0.5 collective-permute-done.3
  21.3 1.5 %collective-permute-start.5 = (bf16[4,128,512]{2,1,0:T(8,128)(2,1)S(1)}, bf16[4,128,512]{2,1,0:T(8,128)(2,1)S(1)}, u32[]{:S(2)}, u32[]{:S(2)}) collective-permute-start(bf16[4,128,512]{2,1,0:T(8,128)(2,1)S(1)} %pad_maximum_fusion.refs_0_), channel_id=1, source_target_pairs={{0,16},{8,24},{16,0},{24,8},{1,17},{9,25},{17,1},{25,9},{2,18},{10... | collective-permute-start | bytes 1572872 | tf_op jit(solution)/shard_map/ppermute | solution.py:20
  22.9 1.6 %collective-permute-start.4 = (bf16[4,128,512]{2,1,0:T(8,128)(2,1)S(1)}, bf16[4,128,512]{2,1,0:T(8,128)(2,1)S(1)}, u32[]{:S(2)}, u32[]{:S(2)}) collective-permute-start(bf16[4,128,512]{2,1,0:T(8,128)(2,1)S(1)} %pad_maximum_fusion.refs_0_), channel_id=1, source_target_pairs={{0,8},{8,0},{16,24},{24,16},{1,9},{9,1},{17,25},{25,17},{2,10},{10... | collective-permute-start | bytes 1572872 | tf_op jit(solution)/shard_map/ppermute | solution.py:20
  24.5 0.0 collective-permute-done.6
  24.5 1.3 %collective-permute-done.7 = bf16[48,512]{1,0:T(8,128)(2,1)S(1)} collective-permute-done((bf16[48,512]{1,0:T(8,128)(2,1)S(1)}, bf16[48,512]{1,0:T(8,128)(2,1)S(1)}, u32[]{:S(2)}, u32[]{:S(2)}) %collective-permute-start.7) | collective-permute-done | bytes 49184 | tf_op jit(solution)/shard_map/ppermute | solution.py:20
  25.9 3.5 %collective-permute-start.10 = (bf16[48,512]{1,0:T(8,128)(2,1)S(1)}, bf16[48,512]{1,0:T(8,128)(2,1)S(1)}, u32[]{:S(2)}, u32[]{:S(2)}) collective-permute-start(bf16[48,512]{1,0:T(8,128)(2,1)S(1)} %add_add_fusion), channel_id=1, source_target_pairs={{0,6},{1,7},{2,4},{3,5},{4,2},{5,3},{6,0},{7,1},{8,14},{9,15},{10,... | collective-permute-start | bytes 147464 | tf_op jit(solution)/shard_map/ppermute | solution.py:20
  29.3 1.0 collective-permute-start.8
  30.3 1.5 %collective-permute-done.10 = bf16[48,512]{1,0:T(8,128)(2,1)S(1)} collective-permute-done((bf16[48,512]{1,0:T(8,128)(2,1)S(1)}, bf16[48,512]{1,0:T(8,128)(2,1)S(1)}, u32[]{:S(2)}, u32[]{:S(2)}) %collective-permute-start.10) | collective-permute-done | bytes 49184 | tf_op jit(solution)/shard_map/ppermute | solution.py:20
  31.8 2.5 %collective-permute-done.9 = bf16[48,512]{1,0:T(8,128)(2,1)S(1)} collective-permute-done((bf16[48,512]{1,0:T(8,128)(2,1)S(1)}, bf16[48,512]{1,0:T(8,128)(2,1)S(1)}, u32[]{:S(2)}, u32[]{:S(2)}) %collective-permute-start.9) | collective-permute-done | bytes 49184 | tf_op jit(solution)/shard_map/ppermute | solution.py:20
  34.4 0.1 collective-permute-start.13
  34.4 2.0 %collective-permute-start.12 = (bf16[4,48,512]{2,1,0:T(8,128)(2,1)S(1)}, bf16[4,48,512]{2,1,0:T(8,128)(2,1)S(1)}, u32[]{:S(2)}, u32[]{:S(2)}) collective-permute-start(bf16[4,48,512]{2,1,0:T(8,128)(2,1)S(1)} %pad_maximum_fusion.1.refs_0_), channel_id=1, source_target_pairs={{0,16},{8,24},{16,0},{24,8},{1,17},{9,25},{17,1},{25,9},{2,18},{10... | collective-permute-start | bytes 589832 | tf_op jit(solution)/shard_map/ppermute | solution.py:20
  36.4 1.5 %collective-permute-start.11 = (bf16[4,48,512]{2,1,0:T(8,128)(2,1)S(1)}, bf16[4,48,512]{2,1,0:T(8,128)(2,1)S(1)}, u32[]{:S(2)}, u32[]{:S(2)}) collective-permute-start(bf16[4,48,512]{2,1,0:T(8,128)(2,1)S(1)} %pad_maximum_fusion.1.refs_0_), channel_id=1, source_target_pairs={{0,8},{8,0},{16,24},{24,16},{1,9},{9,1},{17,25},{25,17},{2,10},{10... | collective-permute-start | bytes 589832 | tf_op jit(solution)/shard_map/ppermute | solution.py:20
  37.9 3.4 %collective-permute-done.13.refs_3_ = bf16[4,48,512]{2,1,0:T(8,128)(2,1)S(1)} collective-permute-done((bf16[4,48,512]{2,1,0:T(8,128)(2,1)S(1)}, bf16[4,48,512]{2,1,0:T(8,128)(2,1)S(1)}, u32[]{:S(2)}, u32[]{:S(2)}) %collective-permute-start.13) | collective-permute-done | bytes 196640 | tf_op jit(solution)/shard_map/ppermute | solution.py:20
  41.3 1.9 %collective-permute-done.12.refs_2_ = bf16[4,48,512]{2,1,0:T(8,128)(2,1)S(1)} collective-permute-done((bf16[4,48,512]{2,1,0:T(8,128)(2,1)S(1)}, bf16[4,48,512]{2,1,0:T(8,128)(2,1)S(1)}, u32[]{:S(2)}, u32[]{:S(2)}) %collective-permute-start.12) | collective-permute-done | bytes 196640 | tf_op jit(solution)/shard_map/ppermute | solution.py:20
  43.2 0.2 collective-permute-done.11.refs_1_
  43.4 0.3 collective-permute-start.15
  43.7 0.2 collective-permute-start.17
  43.9 1.2 %collective-permute-start.19 = (bf16[2,128,512]{2,1,0:T(8,128)(2,1)S(1)}, bf16[2,128,512]{2,1,0:T(8,128)(2,1)S(1)}, u32[]{:S(2)}, u32[]{:S(2)}) collective-permute-start(bf16[2,128,512]{2,1,0:T(8,128)(2,1)S(1)} %slice.9), channel_id=1, source_target_pairs={{0,8},{8,0},{16,24},{24,16},{1,9},{9,1},{17,25},{25,17},{2,10},{10... | collective-permute-start | bytes 786440 | tf_op jit(solution)/shard_map/ppermute | solution.py:20
  45.1 1.0 collective-permute-start.18
  46.1 0.5 collective-permute-start.22
  46.6 0.1 collective-permute-start.21
  46.7 3.9 %section_first.1 = (bf16[192,4096]{1,0:T(8,128)(2,1)S(1)}, bf16[192,4096]{1,0:T(8,128)(2,1)S(1)}, f32[192,896]{1,0:T(8,128)S(1)}, f32[192,1]{1,0:T(8,128)S(1)}) custom-call(bf16[4,48,512]{2,1,0:T(8,128)(2,1)S(1)} %pad_maximum_fusion.1.refs_0_, bf16[4,48,512]{2,1,0:T(8,128)(2,1)S(1)} %collective-permute-done.11.refs_1_, ...), custom_call_target="tpu_custom_call" | custom-call | tf_op jit(solution)/shard_map/section_first/pallas_call | solution.py:335
  50.6 1.9 %collective-permute-done.19.refs_4_ = bf16[2,128,512]{2,1,0:T(8,128)(2,1)S(1)} collective-permute-done((bf16[2,128,512]{2,1,0:T(8,128)(2,1)S(1)}, bf16[2,128,512]{2,1,0:T(8,128)(2,1)S(1)}, u32[]{:S(2)}, u32[]{:S(2)}) %collective-permute-start.19) | collective-permute-done | bytes 262176 | tf_op jit(solution)/shard_map/ppermute | solution.py:20
  52.5 0.7 collective-permute-done.18.refs_3_
  53.2 0.5 collective-permute-start.24
  53.8 1.0 %collective-permute-done.23.refs_8_ = bf16[2,128,512]{2,1,0:T(8,128)(2,1)S(1)} collective-permute-done((bf16[2,128,512]{2,1,0:T(8,128)(2,1)S(1)}, bf16[2,128,512]{2,1,0:T(8,128)(2,1)S(1)}, u32[]{:S(2)}, u32[]{:S(2)}) %collective-permute-start.23) | collective-permute-done | bytes 262176 | tf_op jit(solution)/shard_map/ppermute | solution.py:20
  54.8 0.4 collective-permute-done.24.refs_9_
  55.1 1.3 %project_first.1 = (bf16[96,512]{1,0:T(8,128)(2,1)S(1)}, bf16[96,512]{1,0:T(8,128)(2,1)S(1)}, bf16[4096,512]{1,0:T(8,128)(2,1)S(1)}) custom-call(bf16[4,128,512]{2,1,0:T(8,128)(2,1)S(1)} %pad_maximum_fusion.refs_0_, bf16[4,128,512]{2,1,0:T(8,128)(2,1)S(1)} %collective-permute-done.4.refs_1_, bf16[4,128,512]{2,1,0:T(8,128)(2,1)S(1)} %collective-permute-done.5.refs_2_, ...), custom_call_target="tpu_custom_call" | custom-call | flops 805306368 | tf_op jit(solution)/shard_map/project_first/pallas_call | solution.py:335
  56.5 0.2 collective-permute-start.25
  56.7 1.2 %collective-permute-done.25.refs_1_ = bf16[96,512]{1,0:T(8,128)(2,1)S(1)} collective-permute-done((bf16[96,512]{1,0:T(8,128)(2,1)S(1)}, bf16[96,512]{1,0:T(8,128)(2,1)S(1)}, u32[]{:S(2)}, u32[]{:S(2)}) %collective-permute-start.25) | collective-permute-done | bytes 98336 | tf_op jit(solution)/shard_map/ppermute | solution.py:20
  57.9 3.4 %collective-permute-start.28 = (bf16[96,512]{1,0:T(8,128)(2,1)S(1)}, bf16[96,512]{1,0:T(8,128)(2,1)S(1)}, u32[]{:S(2)}, u32[]{:S(2)}) collective-permute-start(bf16[96,512]{1,0:T(8,128)(2,1)S(1)} %add.29.refs_0_), channel_id=1, source_target_pairs={{0,6},{1,7},{2,4},{3,5},{4,2},{5,3},{6,0},{7,1},{8,14},{9,15},{10,... | collective-permute-start | bytes 294920 | tf_op jit(solution)/shard_map/ppermute | solution.py:20
  61.3 1.1 %collective-permute-start.26 = (bf16[96,512]{1,0:T(8,128)(2,1)S(1)}, bf16[96,512]{1,0:T(8,128)(2,1)S(1)}, u32[]{:S(2)}, u32[]{:S(2)}) collective-permute-start(bf16[96,512]{1,0:T(8,128)(2,1)S(1)} %add.29.refs_0_), channel_id=1, source_target_pairs={{0,2},{1,3},{2,0},{3,1},{4,6},{5,7},{6,4},{7,5},{8,10},{9,11},{10,... | collective-permute-start | bytes 294920 | tf_op jit(solution)/shard_map/ppermute | solution.py:20
  62.3 3.1 %collective-permute-done.28.refs_3_ = bf16[96,512]{1,0:T(8,128)(2,1)S(1)} collective-permute-done((bf16[96,512]{1,0:T(8,128)(2,1)S(1)}, bf16[96,512]{1,0:T(8,128)(2,1)S(1)}, u32[]{:S(2)}, u32[]{:S(2)}) %collective-permute-start.28) | collective-permute-done | bytes 98336 | tf_op jit(solution)/shard_map/ppermute | solution.py:20
  65.5 4.1 %collective-permute-done.27.refs_2_ = bf16[96,512]{1,0:T(8,128)(2,1)S(1)} collective-permute-done((bf16[96,512]{1,0:T(8,128)(2,1)S(1)}, bf16[96,512]{1,0:T(8,128)(2,1)S(1)}, u32[]{:S(2)}, u32[]{:S(2)}) %collective-permute-start.27) | collective-permute-done | bytes 98336 | tf_op jit(solution)/shard_map/ppermute | solution.py:20
  69.6 0.1 add.30.after
  69.7 3.1 %collective-permute-start.30 = (bf16[96,512]{1,0:T(8,128)(2,1)S(1)}, bf16[96,512]{1,0:T(8,128)(2,1)S(1)}, u32[]{:S(2)}, u32[]{:S(2)}) collective-permute-start(bf16[96,512]{1,0:T(8,128)(2,1)S(1)} %add.30.after), channel_id=1, source_target_pairs={{0,24},{8,16},{1,25},{9,17},{2,26},{10,18},{3,27},{11,19},{4,28},{... | collective-permute-start | bytes 294920 | tf_op jit(solution)/shard_map/ppermute | solution.py:25
  72.7 1.3 %collective-permute-start.29 = (bf16[96,512]{1,0:T(8,128)(2,1)S(1)}, bf16[96,512]{1,0:T(8,128)(2,1)S(1)}, u32[]{:S(2)}, u32[]{:S(2)}) collective-permute-start(bf16[96,512]{1,0:T(8,128)(2,1)S(1)} %add.30.after), channel_id=1, source_target_pairs={{0,16},{8,24},{1,17},{9,25},{2,18},{10,26},{3,19},{11,27},{4,20},{... | collective-permute-start | bytes 294920 | tf_op jit(solution)/shard_map/ppermute | solution.py:25
  74.1 2.7 %collective-permute-done.29.refs_0_ = bf16[96,512]{1,0:T(8,128)(2,1)S(1)} collective-permute-done((bf16[96,512]{1,0:T(8,128)(2,1)S(1)}, bf16[96,512]{1,0:T(8,128)(2,1)S(1)}, u32[]{:S(2)}, u32[]{:S(2)}) %collective-permute-start.29) | collective-permute-done | bytes 98336 | tf_op jit(solution)/shard_map/ppermute | solution.py:25
  76.8 0.1 collective-permute-start.31
  76.9 1.3 %collective-permute-done.31.refs_1_ = bf16[96,512]{1,0:T(8,128)(2,1)S(1)} collective-permute-done((bf16[96,512]{1,0:T(8,128)(2,1)S(1)}, bf16[96,512]{1,0:T(8,128)(2,1)S(1)}, u32[]{:S(2)}, u32[]{:S(2)}) %collective-permute-start.31) | collective-permute-done | bytes 98336 | tf_op jit(solution)/shard_map/ppermute | solution.py:20
  78.2 1.0 section_next.1
  79.2 0.2 collective-permute-start.32
  79.4 1.1 %collective-permute-done.32.refs_1_ = bf16[96,512]{1,0:T(8,128)(2,1)S(1)} collective-permute-done((bf16[96,512]{1,0:T(8,128)(2,1)S(1)}, bf16[96,512]{1,0:T(8,128)(2,1)S(1)}, u32[]{:S(2)}, u32[]{:S(2)}) %collective-permute-start.32) | collective-permute-done | bytes 98336 | tf_op jit(solution)/shard_map/ppermute | solution.py:20
  80.6 3.5 %collective-permute-start.35 = (bf16[96,512]{1,0:T(8,128)(2,1)S(1)}, bf16[96,512]{1,0:T(8,128)(2,1)S(1)}, u32[]{:S(2)}, u32[]{:S(2)}) collective-permute-start(bf16[96,512]{1,0:T(8,128)(2,1)S(1)} %add.32.refs_0_), channel_id=1, source_target_pairs={{0,6},{1,7},{2,4},{3,5},{4,2},{5,3},{6,0},{7,1},{8,14},{9,15},{10,... | collective-permute-start | bytes 294920 | tf_op jit(solution)/shard_map/ppermute | solution.py:20
  84.1 1.0 %collective-permute-start.33 = (bf16[96,512]{1,0:T(8,128)(2,1)S(1)}, bf16[96,512]{1,0:T(8,128)(2,1)S(1)}, u32[]{:S(2)}, u32[]{:S(2)}) collective-permute-start(bf16[96,512]{1,0:T(8,128)(2,1)S(1)} %add.32.refs_0_), channel_id=1, source_target_pairs={{0,2},{1,3},{2,0},{3,1},{4,6},{5,7},{6,4},{7,5},{8,10},{9,11},{10,... | collective-permute-start | bytes 294920 | tf_op jit(solution)/shard_map/ppermute | solution.py:20
  85.1 3.1 %collective-permute-done.35.refs_3_ = bf16[96,512]{1,0:T(8,128)(2,1)S(1)} collective-permute-done((bf16[96,512]{1,0:T(8,128)(2,1)S(1)}, bf16[96,512]{1,0:T(8,128)(2,1)S(1)}, u32[]{:S(2)}, u32[]{:S(2)}) %collective-permute-start.35) | collective-permute-done | bytes 98336 | tf_op jit(solution)/shard_map/ppermute | solution.py:20
  88.2 4.4 %collective-permute-done.34.refs_2_ = bf16[96,512]{1,0:T(8,128)(2,1)S(1)} collective-permute-done((bf16[96,512]{1,0:T(8,128)(2,1)S(1)}, bf16[96,512]{1,0:T(8,128)(2,1)S(1)}, u32[]{:S(2)}, u32[]{:S(2)}) %collective-permute-start.34) | collective-permute-done | bytes 98336 | tf_op jit(solution)/shard_map/ppermute | solution.py:20
  92.6 1.0 %collective-permute-start.36 = (bf16[96,512]{1,0:T(8,128)(2,1)S(1)}, bf16[96,512]{1,0:T(8,128)(2,1)S(1)}, u32[]{:S(2)}, u32[]{:S(2)}) collective-permute-start(bf16[96,512]{1,0:T(8,128)(2,1)S(1)} %choose.1.refs_0_), channel_id=1, source_target_pairs={{0,8},{8,0},{16,24},{24,16},{1,9},{9,1},{17,25},{25,17},{2,10},{10... | collective-permute-start | bytes 294920 | tf_op jit(solution)/shard_map/ppermute | solution.py:20
  93.6 3.6 %collective-permute-done.36.refs_1_ = bf16[96,512]{1,0:T(8,128)(2,1)S(1)} collective-permute-done((bf16[96,512]{1,0:T(8,128)(2,1)S(1)}, bf16[96,512]{1,0:T(8,128)(2,1)S(1)}, u32[]{:S(2)}, u32[]{:S(2)}) %collective-permute-start.36) | collective-permute-done | bytes 98336 | tf_op jit(solution)/shard_map/ppermute | solution.py:20
  97.3 0.1 collective-permute-start.37
  97.4 1.3 %collective-permute-done.37.far = bf16[96,512]{1,0:T(8,128)(2,1)S(1)} collective-permute-done((bf16[96,512]{1,0:T(8,128)(2,1)S(1)}, bf16[96,512]{1,0:T(8,128)(2,1)S(1)}, u32[]{:S(2)}, u32[]{:S(2)}) %collective-permute-start.37) | collective-permute-done | bytes 98336 | tf_op jit(solution)/shard_map/ppermute | solution.py:20
  98.7 0.7 collect.1
  (39 shorter events, 0.3 us)
Async XLA Ops:
  0.0 1.0 %copy-start = (bf16[512,512]{1,0:T(8,128)(2,1)S(1)}, bf16[512,512]{1,0:T(8,128)(2,1)}, u32[]{:S(2)}) copy-start(bf16[512,512]{1,0:T(8,128)(2,1)} %param.11) | copy-start | bytes 1572868
  1.1 15.7 %collective-permute-start.2 = (bf16[128,512]{1,0:T(8,128)(2,1)S(1)}, bf16[128,512]{1,0:T(8,128)(2,1)S(1)}, u32[]{:S(2)}, u32[]{:S(2)}) collective-permute-start(bf16[128,512]{1,0:T(8,128)(2,1)S(1)} %constant_dynamic-slice_fusion), channel_id=1, source_target_pairs={{0,6},{1,7},{2,4},{3,5},{4,2},{5,3},{6,0},{7,1},{8,14},{9,15},{10,... | collective-permute-start | bytes 393224 | tf_op jit(solution)/shard_map/ppermute | solution.py:20
  6.2 11.1 %collective-permute-start.1 = (bf16[128,512]{1,0:T(8,128)(2,1)S(1)}, bf16[128,512]{1,0:T(8,128)(2,1)S(1)}, u32[]{:S(2)}, u32[]{:S(2)}) collective-permute-start(bf16[128,512]{1,0:T(8,128)(2,1)S(1)} %constant_dynamic-slice_fusion), channel_id=1, source_target_pairs={{0,4},{1,5},{2,6},{3,7},{4,0},{5,1},{6,2},{7,3},{8,12},{9,13},{10,... | collective-permute-start | bytes 393224 | tf_op jit(solution)/shard_map/ppermute | solution.py:20
  6.2 11.1 %collective-permute-start = (bf16[128,512]{1,0:T(8,128)(2,1)S(1)}, bf16[128,512]{1,0:T(8,128)(2,1)S(1)}, u32[]{:S(2)}, u32[]{:S(2)}) collective-permute-start(bf16[128,512]{1,0:T(8,128)(2,1)S(1)} %constant_dynamic-slice_fusion), channel_id=1, source_target_pairs={{0,2},{1,3},{2,0},{3,1},{4,6},{5,7},{6,4},{7,5},{8,10},{9,11},{10,... | collective-permute-start | bytes 393224 | tf_op jit(solution)/shard_map/ppermute | solution.py:20
  6.8 0.7 copy-start.3
  7.5 39.2 %copy-start.2 = (f32[2,4096]{1,0:T(2,128)S(1)}, f32[2,4096]{1,0:T(2,128)}, u32[]{:S(2)}) copy-start(f32[2,4096]{1,0:T(2,128)} %refs_2_.1) | copy-start | bytes 98308
  17.2 4.1 %collective-permute-start.3 = (bf16[48,512]{1,0:T(8,128)(2,1)S(1)}, bf16[48,512]{1,0:T(8,128)(2,1)S(1)}, u32[]{:S(2)}, u32[]{:S(2)}) collective-permute-start(bf16[48,512]{1,0:T(8,128)(2,1)S(1)} %get-tuple-element.47), channel_id=1, source_target_pairs={{0,8},{8,0},{16,24},{24,16},{1,9},{9,1},{17,25},{25,17},{2,10},{10... | collective-permute-start | bytes 147464 | tf_op jit(solution)/shard_map/ppermute | solution.py:20
  18.7 5.8 %collective-permute-start.6 = (bf16[48,512]{1,0:T(8,128)(2,1)S(1)}, bf16[48,512]{1,0:T(8,128)(2,1)S(1)}, u32[]{:S(2)}, u32[]{:S(2)}) collective-permute-start(bf16[48,512]{1,0:T(8,128)(2,1)S(1)} %get-tuple-element.55), channel_id=1, source_target_pairs={{0,16},{8,24},{16,0},{24,8},{1,17},{9,25},{17,1},{25,9},{2,18},{10... | collective-permute-start | bytes 147464 | tf_op jit(solution)/shard_map/ppermute | solution.py:20
  20.3 5.6 %collective-permute-start.7 = (bf16[48,512]{1,0:T(8,128)(2,1)S(1)}, bf16[48,512]{1,0:T(8,128)(2,1)S(1)}, u32[]{:S(2)}, u32[]{:S(2)}) collective-permute-start(bf16[48,512]{1,0:T(8,128)(2,1)S(1)} %get-tuple-element.56), channel_id=1, source_target_pairs={{0,24},{8,16},{16,8},{24,0},{1,25},{9,17},{17,9},{25,1},{2,26},{10... | collective-permute-start | bytes 147464 | tf_op jit(solution)/shard_map/ppermute | solution.py:20
  21.3 22.4 %collective-permute-start.5 = (bf16[4,128,512]{2,1,0:T(8,128)(2,1)S(1)}, bf16[4,128,512]{2,1,0:T(8,128)(2,1)S(1)}, u32[]{:S(2)}, u32[]{:S(2)}) collective-permute-start(bf16[4,128,512]{2,1,0:T(8,128)(2,1)S(1)} %pad_maximum_fusion.refs_0_), channel_id=1, source_target_pairs={{0,16},{8,24},{16,0},{24,8},{1,17},{9,25},{17,1},{25,9},{2,18},{10... | collective-permute-start | bytes 1572872 | tf_op jit(solution)/shard_map/ppermute | solution.py:20
  22.9 20.8 %collective-permute-start.4 = (bf16[4,128,512]{2,1,0:T(8,128)(2,1)S(1)}, bf16[4,128,512]{2,1,0:T(8,128)(2,1)S(1)}, u32[]{:S(2)}, u32[]{:S(2)}) collective-permute-start(bf16[4,128,512]{2,1,0:T(8,128)(2,1)S(1)} %pad_maximum_fusion.refs_0_), channel_id=1, source_target_pairs={{0,8},{8,0},{16,24},{24,16},{1,9},{9,1},{17,25},{25,17},{2,10},{10... | collective-permute-start | bytes 1572872 | tf_op jit(solution)/shard_map/ppermute | solution.py:20
  25.9 6.0 %collective-permute-start.10 = (bf16[48,512]{1,0:T(8,128)(2,1)S(1)}, bf16[48,512]{1,0:T(8,128)(2,1)S(1)}, u32[]{:S(2)}, u32[]{:S(2)}) collective-permute-start(bf16[48,512]{1,0:T(8,128)(2,1)S(1)} %add_add_fusion), channel_id=1, source_target_pairs={{0,6},{1,7},{2,4},{3,5},{4,2},{5,3},{6,0},{7,1},{8,14},{9,15},{10,... | collective-permute-start | bytes 147464 | tf_op jit(solution)/shard_map/ppermute | solution.py:20
  29.3 5.0 %collective-permute-start.9 = (bf16[48,512]{1,0:T(8,128)(2,1)S(1)}, bf16[48,512]{1,0:T(8,128)(2,1)S(1)}, u32[]{:S(2)}, u32[]{:S(2)}) collective-permute-start(bf16[48,512]{1,0:T(8,128)(2,1)S(1)} %add_add_fusion), channel_id=1, source_target_pairs={{0,4},{1,5},{2,6},{3,7},{4,0},{5,1},{6,2},{7,3},{8,12},{9,13},{10,... | collective-permute-start | bytes 147464 | tf_op jit(solution)/shard_map/ppermute | solution.py:20
  29.3 5.0 %collective-permute-start.8 = (bf16[48,512]{1,0:T(8,128)(2,1)S(1)}, bf16[48,512]{1,0:T(8,128)(2,1)S(1)}, u32[]{:S(2)}, u32[]{:S(2)}) collective-permute-start(bf16[48,512]{1,0:T(8,128)(2,1)S(1)} %add_add_fusion), channel_id=1, source_target_pairs={{0,2},{1,3},{2,0},{3,1},{4,6},{5,7},{6,4},{7,5},{8,10},{9,11},{10,... | collective-permute-start | bytes 147464 | tf_op jit(solution)/shard_map/ppermute | solution.py:20
  34.4 6.9 %collective-permute-start.13 = (bf16[4,48,512]{2,1,0:T(8,128)(2,1)S(1)}, bf16[4,48,512]{2,1,0:T(8,128)(2,1)S(1)}, u32[]{:S(2)}, u32[]{:S(2)}) collective-permute-start(bf16[4,48,512]{2,1,0:T(8,128)(2,1)S(1)} %pad_maximum_fusion.1.refs_0_), channel_id=1, source_target_pairs={{0,24},{8,16},{16,8},{24,0},{1,25},{9,17},{17,9},{25,1},{2,26},{10... | collective-permute-start | bytes 589832 | tf_op jit(solution)/shard_map/ppermute | solution.py:20
  34.4 8.7 %collective-permute-start.12 = (bf16[4,48,512]{2,1,0:T(8,128)(2,1)S(1)}, bf16[4,48,512]{2,1,0:T(8,128)(2,1)S(1)}, u32[]{:S(2)}, u32[]{:S(2)}) collective-permute-start(bf16[4,48,512]{2,1,0:T(8,128)(2,1)S(1)} %pad_maximum_fusion.1.refs_0_), channel_id=1, source_target_pairs={{0,16},{8,24},{16,0},{24,8},{1,17},{9,25},{17,1},{25,9},{2,18},{10... | collective-permute-start | bytes 589832 | tf_op jit(solution)/shard_map/ppermute | solution.py:20
  36.4 6.9 %collective-permute-start.11 = (bf16[4,48,512]{2,1,0:T(8,128)(2,1)S(1)}, bf16[4,48,512]{2,1,0:T(8,128)(2,1)S(1)}, u32[]{:S(2)}, u32[]{:S(2)}) collective-permute-start(bf16[4,48,512]{2,1,0:T(8,128)(2,1)S(1)} %pad_maximum_fusion.1.refs_0_), channel_id=1, source_target_pairs={{0,8},{8,0},{16,24},{24,16},{1,9},{9,1},{17,25},{25,17},{2,10},{10... | collective-permute-start | bytes 589832 | tf_op jit(solution)/shard_map/ppermute | solution.py:20
  41.3 3.8 %collective-permute-start.14 = (bf16[4,48,512]{2,1,0:T(8,128)(2,1)S(1)}, bf16[4,48,512]{2,1,0:T(8,128)(2,1)S(1)}, u32[]{:S(2)}, u32[]{:S(2)}) collective-permute-start(bf16[4,48,512]{2,1,0:T(8,128)(2,1)S(1)} %pad_maximum_fusion.1.refs_0_), channel_id=1, source_target_pairs={{0,1},{1,0},{2,3},{3,2},{4,5},{5,4},{6,7},{7,6},{8,9},{9,8},{10,11... | collective-permute-start | bytes 589832 | tf_op jit(solution)/shard_map/ppermute | solution.py:20
  43.2 2.9 %collective-permute-start.16 = (bf16[4,48,512]{2,1,0:T(8,128)(2,1)S(1)}, bf16[4,48,512]{2,1,0:T(8,128)(2,1)S(1)}, u32[]{:S(2)}, u32[]{:S(2)}) collective-permute-start(bf16[4,48,512]{2,1,0:T(8,128)(2,1)S(1)} %collective-permute-done.12.refs_2_), channel_id=1, source_target_pairs={{0,1},{1,0},{2,3},{3,2},{4,5},{5,4},{6,7},{7,6},{8,9},{9,8},{10,11... | collective-permute-start | bytes 589832 | tf_op jit(solution)/shard_map/ppermute | solution.py:20
  43.4 2.8 %collective-permute-start.15 = (bf16[4,48,512]{2,1,0:T(8,128)(2,1)S(1)}, bf16[4,48,512]{2,1,0:T(8,128)(2,1)S(1)}, u32[]{:S(2)}, u32[]{:S(2)}) collective-permute-start(bf16[4,48,512]{2,1,0:T(8,128)(2,1)S(1)} %collective-permute-done.11.refs_1_), channel_id=1, source_target_pairs={{0,1},{1,0},{2,3},{3,2},{4,5},{5,4},{6,7},{7,6},{8,9},{9,8},{10,11... | collective-permute-start | bytes 589832 | tf_op jit(solution)/shard_map/ppermute | solution.py:20
  43.7 2.9 %collective-permute-start.17 = (bf16[4,48,512]{2,1,0:T(8,128)(2,1)S(1)}, bf16[4,48,512]{2,1,0:T(8,128)(2,1)S(1)}, u32[]{:S(2)}, u32[]{:S(2)}) collective-permute-start(bf16[4,48,512]{2,1,0:T(8,128)(2,1)S(1)} %collective-permute-done.13.refs_3_), channel_id=1, source_target_pairs={{0,1},{1,0},{2,3},{3,2},{4,5},{5,4},{6,7},{7,6},{8,9},{9,8},{10,11... | collective-permute-start | bytes 589832 | tf_op jit(solution)/shard_map/ppermute | solution.py:20
  43.9 8.6 %collective-permute-start.19 = (bf16[2,128,512]{2,1,0:T(8,128)(2,1)S(1)}, bf16[2,128,512]{2,1,0:T(8,128)(2,1)S(1)}, u32[]{:S(2)}, u32[]{:S(2)}) collective-permute-start(bf16[2,128,512]{2,1,0:T(8,128)(2,1)S(1)} %slice.9), channel_id=1, source_target_pairs={{0,8},{8,0},{16,24},{24,16},{1,9},{9,1},{17,25},{25,17},{2,10},{10... | collective-permute-start | bytes 786440 | tf_op jit(solution)/shard_map/ppermute | solution.py:20
  45.1 8.1 %collective-permute-start.18 = (bf16[2,128,512]{2,1,0:T(8,128)(2,1)S(1)}, bf16[2,128,512]{2,1,0:T(8,128)(2,1)S(1)}, u32[]{:S(2)}, u32[]{:S(2)}) collective-permute-start(bf16[2,128,512]{2,1,0:T(8,128)(2,1)S(1)} %slice.8), channel_id=1, source_target_pairs={{0,16},{8,24},{16,0},{24,8},{1,17},{9,25},{17,1},{25,9},{2,18},{10... | collective-permute-start | bytes 786440 | tf_op jit(solution)/shard_map/ppermute | solution.py:20
  46.1 7.6 %collective-permute-start.20 = (bf16[4,128,512]{2,1,0:T(8,128)(2,1)S(1)}, bf16[4,128,512]{2,1,0:T(8,128)(2,1)S(1)}, u32[]{:S(2)}, u32[]{:S(2)}) collective-permute-start(bf16[4,128,512]{2,1,0:T(8,128)(2,1)S(1)} %pad_maximum_fusion.refs_0_), channel_id=1, source_target_pairs={{0,1},{1,0},{2,3},{3,2},{4,5},{5,4},{6,7},{7,6},{8,9},{9,8},{10,11... | collective-permute-start | bytes 1572872 | tf_op jit(solution)/shard_map/ppermute | solution.py:20
  46.1 7.6 %collective-permute-start.22 = (bf16[4,128,512]{2,1,0:T(8,128)(2,1)S(1)}, bf16[4,128,512]{2,1,0:T(8,128)(2,1)S(1)}, u32[]{:S(2)}, u32[]{:S(2)}) collective-permute-start(bf16[4,128,512]{2,1,0:T(8,128)(2,1)S(1)} %collective-permute-done.5.refs_2_), channel_id=1, source_target_pairs={{0,1},{1,0},{2,3},{3,2},{4,5},{5,4},{6,7},{7,6},{8,9},{9,8},{10,11... | collective-permute-start | bytes 1572872 | tf_op jit(solution)/shard_map/ppermute | solution.py:20
  46.6 7.1 %collective-permute-start.21 = (bf16[4,128,512]{2,1,0:T(8,128)(2,1)S(1)}, bf16[4,128,512]{2,1,0:T(8,128)(2,1)S(1)}, u32[]{:S(2)}, u32[]{:S(2)}) collective-permute-start(bf16[4,128,512]{2,1,0:T(8,128)(2,1)S(1)} %collective-permute-done.4.refs_1_), channel_id=1, source_target_pairs={{0,1},{1,0},{2,3},{3,2},{4,5},{5,4},{6,7},{7,6},{8,9},{9,8},{10,11... | collective-permute-start | bytes 1572872 | tf_op jit(solution)/shard_map/ppermute | solution.py:20
  53.2 1.5 %collective-permute-start.23 = (bf16[2,128,512]{2,1,0:T(8,128)(2,1)S(1)}, bf16[2,128,512]{2,1,0:T(8,128)(2,1)S(1)}, u32[]{:S(2)}, u32[]{:S(2)}) collective-permute-start(bf16[2,128,512]{2,1,0:T(8,128)(2,1)S(1)} %collective-permute-done.18.refs_3_), channel_id=1, source_target_pairs={{0,1},{1,0},{2,3},{3,2},{4,5},{5,4},{6,7},{7,6},{8,9},{9,8},{10,11... | collective-permute-start | bytes 786440 | tf_op jit(solution)/shard_map/ppermute | solution.py:20
  53.2 1.9 %collective-permute-start.24 = (bf16[2,128,512]{2,1,0:T(8,128)(2,1)S(1)}, bf16[2,128,512]{2,1,0:T(8,128)(2,1)S(1)}, u32[]{:S(2)}, u32[]{:S(2)}) collective-permute-start(bf16[2,128,512]{2,1,0:T(8,128)(2,1)S(1)} %collective-permute-done.19.refs_4_), channel_id=1, source_target_pairs={{0,1},{1,0},{2,3},{3,2},{4,5},{5,4},{6,7},{7,6},{8,9},{9,8},{10,11... | collective-permute-start | bytes 786440 | tf_op jit(solution)/shard_map/ppermute | solution.py:20
  56.5 1.4 %collective-permute-start.25 = (bf16[96,512]{1,0:T(8,128)(2,1)S(1)}, bf16[96,512]{1,0:T(8,128)(2,1)S(1)}, u32[]{:S(2)}, u32[]{:S(2)}) collective-permute-start(bf16[96,512]{1,0:T(8,128)(2,1)S(1)} %get-tuple-element.65), channel_id=1, source_target_pairs={{0,1},{1,0},{2,3},{3,2},{4,5},{5,4},{6,7},{7,6},{8,9},{9,8},{10,11... | collective-permute-start | bytes 294920 | tf_op jit(solution)/shard_map/ppermute | solution.py:20
  57.9 7.6 %collective-permute-start.28 = (bf16[96,512]{1,0:T(8,128)(2,1)S(1)}, bf16[96,512]{1,0:T(8,128)(2,1)S(1)}, u32[]{:S(2)}, u32[]{:S(2)}) collective-permute-start(bf16[96,512]{1,0:T(8,128)(2,1)S(1)} %add.29.refs_0_), channel_id=1, source_target_pairs={{0,6},{1,7},{2,4},{3,5},{4,2},{5,3},{6,0},{7,1},{8,14},{9,15},{10,... | collective-permute-start | bytes 294920 | tf_op jit(solution)/shard_map/ppermute | solution.py:20
  61.3 8.3 %collective-permute-start.27 = (bf16[96,512]{1,0:T(8,128)(2,1)S(1)}, bf16[96,512]{1,0:T(8,128)(2,1)S(1)}, u32[]{:S(2)}, u32[]{:S(2)}) collective-permute-start(bf16[96,512]{1,0:T(8,128)(2,1)S(1)} %add.29.refs_0_), channel_id=1, source_target_pairs={{0,4},{1,5},{2,6},{3,7},{4,0},{5,1},{6,2},{7,3},{8,12},{9,13},{10,... | collective-permute-start | bytes 294920 | tf_op jit(solution)/shard_map/ppermute | solution.py:20
  61.3 8.3 %collective-permute-start.26 = (bf16[96,512]{1,0:T(8,128)(2,1)S(1)}, bf16[96,512]{1,0:T(8,128)(2,1)S(1)}, u32[]{:S(2)}, u32[]{:S(2)}) collective-permute-start(bf16[96,512]{1,0:T(8,128)(2,1)S(1)} %add.29.refs_0_), channel_id=1, source_target_pairs={{0,2},{1,3},{2,0},{3,1},{4,6},{5,7},{6,4},{7,5},{8,10},{9,11},{10,... | collective-permute-start | bytes 294920 | tf_op jit(solution)/shard_map/ppermute | solution.py:20
  69.6 29.8 %copy-start.1 = (bf16[512,512]{1,0:T(8,128)(2,1)S(1)}, bf16[512,512]{1,0:T(8,128)(2,1)}, u32[]{:S(2)}) copy-start(bf16[512,512]{1,0:T(8,128)(2,1)} %param.11) | copy-start | bytes 1572868
  69.7 7.2 %collective-permute-start.30 = (bf16[96,512]{1,0:T(8,128)(2,1)S(1)}, bf16[96,512]{1,0:T(8,128)(2,1)S(1)}, u32[]{:S(2)}, u32[]{:S(2)}) collective-permute-start(bf16[96,512]{1,0:T(8,128)(2,1)S(1)} %add.30.after), channel_id=1, source_target_pairs={{0,24},{8,16},{1,25},{9,17},{2,26},{10,18},{3,27},{11,19},{4,28},{... | collective-permute-start | bytes 294920 | tf_op jit(solution)/shard_map/ppermute | solution.py:25
  72.7 4.1 %collective-permute-start.29 = (bf16[96,512]{1,0:T(8,128)(2,1)S(1)}, bf16[96,512]{1,0:T(8,128)(2,1)S(1)}, u32[]{:S(2)}, u32[]{:S(2)}) collective-permute-start(bf16[96,512]{1,0:T(8,128)(2,1)S(1)} %add.30.after), channel_id=1, source_target_pairs={{0,16},{8,24},{1,17},{9,25},{2,18},{10,26},{3,19},{11,27},{4,20},{... | collective-permute-start | bytes 294920 | tf_op jit(solution)/shard_map/ppermute | solution.py:25
  76.8 1.4 %collective-permute-start.31 = (bf16[96,512]{1,0:T(8,128)(2,1)S(1)}, bf16[96,512]{1,0:T(8,128)(2,1)S(1)}, u32[]{:S(2)}, u32[]{:S(2)}) collective-permute-start(bf16[96,512]{1,0:T(8,128)(2,1)S(1)} %add.31.refs_0_), channel_id=1, source_target_pairs={{0,1},{1,0},{2,3},{3,2},{4,5},{5,4},{6,7},{7,6},{8,9},{9,8},{10,11... | collective-permute-start | bytes 294920 | tf_op jit(solution)/shard_map/ppermute | solution.py:20
  79.2 1.4 %collective-permute-start.32 = (bf16[96,512]{1,0:T(8,128)(2,1)S(1)}, bf16[96,512]{1,0:T(8,128)(2,1)S(1)}, u32[]{:S(2)}, u32[]{:S(2)}) collective-permute-start(bf16[96,512]{1,0:T(8,128)(2,1)S(1)} %get-tuple-element.80), channel_id=1, source_target_pairs={{0,1},{1,0},{2,3},{3,2},{4,5},{5,4},{6,7},{7,6},{8,9},{9,8},{10,11... | collective-permute-start | bytes 294920 | tf_op jit(solution)/shard_map/ppermute | solution.py:20
  80.6 7.6 %collective-permute-start.35 = (bf16[96,512]{1,0:T(8,128)(2,1)S(1)}, bf16[96,512]{1,0:T(8,128)(2,1)S(1)}, u32[]{:S(2)}, u32[]{:S(2)}) collective-permute-start(bf16[96,512]{1,0:T(8,128)(2,1)S(1)} %add.32.refs_0_), channel_id=1, source_target_pairs={{0,6},{1,7},{2,4},{3,5},{4,2},{5,3},{6,0},{7,1},{8,14},{9,15},{10,... | collective-permute-start | bytes 294920 | tf_op jit(solution)/shard_map/ppermute | solution.py:20
  84.1 8.5 %collective-permute-start.34 = (bf16[96,512]{1,0:T(8,128)(2,1)S(1)}, bf16[96,512]{1,0:T(8,128)(2,1)S(1)}, u32[]{:S(2)}, u32[]{:S(2)}) collective-permute-start(bf16[96,512]{1,0:T(8,128)(2,1)S(1)} %add.32.refs_0_), channel_id=1, source_target_pairs={{0,4},{1,5},{2,6},{3,7},{4,0},{5,1},{6,2},{7,3},{8,12},{9,13},{10,... | collective-permute-start | bytes 294920 | tf_op jit(solution)/shard_map/ppermute | solution.py:20
  84.1 8.5 %collective-permute-start.33 = (bf16[96,512]{1,0:T(8,128)(2,1)S(1)}, bf16[96,512]{1,0:T(8,128)(2,1)S(1)}, u32[]{:S(2)}, u32[]{:S(2)}) collective-permute-start(bf16[96,512]{1,0:T(8,128)(2,1)S(1)} %add.32.refs_0_), channel_id=1, source_target_pairs={{0,2},{1,3},{2,0},{3,1},{4,6},{5,7},{6,4},{7,5},{8,10},{9,11},{10,... | collective-permute-start | bytes 294920 | tf_op jit(solution)/shard_map/ppermute | solution.py:20
  92.6 4.7 %collective-permute-start.36 = (bf16[96,512]{1,0:T(8,128)(2,1)S(1)}, bf16[96,512]{1,0:T(8,128)(2,1)S(1)}, u32[]{:S(2)}, u32[]{:S(2)}) collective-permute-start(bf16[96,512]{1,0:T(8,128)(2,1)S(1)} %choose.1.refs_0_), channel_id=1, source_target_pairs={{0,8},{8,0},{16,24},{24,16},{1,9},{9,1},{17,25},{25,17},{2,10},{10... | collective-permute-start | bytes 294920 | tf_op jit(solution)/shard_map/ppermute | solution.py:20
  97.3 1.4 %collective-permute-start.37 = (bf16[96,512]{1,0:T(8,128)(2,1)S(1)}, bf16[96,512]{1,0:T(8,128)(2,1)S(1)}, u32[]{:S(2)}, u32[]{:S(2)}) collective-permute-start(bf16[96,512]{1,0:T(8,128)(2,1)S(1)} %add.33.near), channel_id=1, source_target_pairs={{0,1},{1,0},{2,3},{3,2},{4,5},{5,4},{6,7},{7,6},{8,9},{9,8},{10,11... | collective-permute-start | bytes 294920 | tf_op jit(solution)/shard_map/ppermute | solution.py:20

commit v5 on v4

--- a/solution.py
+++ b/solution.py
@@ -43,10 +43,9 @@
     ]
 
 
-def fetch_kernel(block_rows, vocab, tokens_smem, tokens_row, table, gate, down, *refs):
-    outs, (near_gate, near_down, buffer, sems, weight_sems) = refs[:GROUP], refs[GROUP:]
-    weights = split_copies(gate.at[0], near_gate, weight_sems.at[0])
-    weights += split_copies(down.at[0], near_down, weight_sems.at[1])
+def fetch_kernel(block_rows, vocab, tokens_smem, tokens_row, table, gate, *refs):
+    outs, (near_gate, buffer, sem, weight_sems) = refs[:GROUP], refs[GROUP:]
+    weights = split_copies(gate.at[0], near_gate, weight_sems)
     segment = lax.axis_index("segment")
     low = segment * vocab
     count = GROUP * block_rows
@@ -59,38 +58,33 @@
         first = pl.multiple_of((local // TILE) * TILE, TILE)
         place = pl.multiple_of(i * TILE, TILE)
         return pltpu.make_async_copy(
-            table.at[pl.ds(first, TILE), :], buffer.at[pl.ds(place, TILE), :], sems.at[i]
+            table.at[pl.ds(first, TILE), :], buffer.at[pl.ds(place, TILE), :], sem
         )
 
-    def start(i, carry):
+    def start(i, started):
         local, here = held(i)
 
         @pl.when(here)
         def _():
             copy(i, local).start()
 
-        return carry
+        return started + here.astype(jnp.int32)
 
     def finish(i, carry):
-        local, here = held(i)
-
-        @pl.when(here)
-        def _():
-            copy(i, local).wait()
-
+        copy(0, 0).wait()
         return carry
 
     buffer[...] = jnp.zeros_like(buffer)
     for weight in weights:
         weight.start()
-    lax.fori_loop(0, count, start, 0, unroll=8)
+    started = lax.fori_loop(0, count, start, jnp.int32(0), unroll=8)
     wanted = tokens_row[...] - low
     inside = (wanted >= 0) & (wanted < vocab)
     code = jnp.where(inside, lax.rem(wanted, TILE), TILE)
     rows = lax.broadcasted_iota(jnp.int32, (count, count), 0)
     columns = lax.broadcasted_iota(jnp.int32, (count, count), 1)
     code_column = jnp.sum(jnp.where(rows == columns, code, 0), axis=1, keepdims=True)
-    lax.fori_loop(0, count, finish, 0, unroll=8)
+    lax.fori_loop(0, started, finish, 0)
     home = lax.rem(segment, GROUP)
     wide = block_rows * TILE
     row_of = lax.broadcasted_iota(jnp.int32, (block_rows, wide), 0)
@@ -115,22 +109,22 @@
         weight.wait()
 
 
-def load_kernel(gate, down, near_gate, near_down, sems):
-    copies = split_copies(gate.at[0], near_gate, sems.at[0]) + split_copies(down.at[0], near_down, sems.at[1])
+def load_kernel(gate, near_gate, sems):
+    copies = split_copies(gate.at[0], near_gate, sems)
     for copy in copies:
         copy.start()
     for copy in copies:
         copy.wait()
 
 
-def fetch_rows(tokens, embedding, gate, down):
+def fetch_rows(tokens, embedding, gate):
     vocab, features = embedding.shape
     block_rows = tokens.shape[0] // GROUP
     vmem = pl.BlockSpec(memory_space=pltpu.VMEM)
     anywhere = pl.BlockSpec(memory_space=pl.ANY)
-    near = [pltpu.VMEM(gate.shape[1:], BF16), pltpu.VMEM(down.shape[1:], BF16)]
-    weight_sems = pltpu.SemaphoreType.DMA((2, PARTS))
-    params = pltpu.CompilerParams(vmem_limit_bytes=36 * 2**20)
+    near = pltpu.VMEM(gate.shape[1:], BF16)
+    weight_sems = pltpu.SemaphoreType.DMA((PARTS,))
+    params = pltpu.CompilerParams(vmem_limit_bytes=44 * 2**20)
     if vocab % TILE:
         segment = lax.axis_index("segment")
         local = tokens - segment * vocab
@@ -143,27 +137,27 @@
         near = pl.pallas_call(
             load_kernel,
             out_shape=near,
-            in_specs=[anywhere] * 2,
-            out_specs=[vmem] * 2,
+            in_specs=[anywhere],
+            out_specs=vmem,
             scratch_shapes=[weight_sems],
             compiler_params=params,
             name="load_weights",
-        )(gate, down)
-        return blocks, *near
-    *blocks, near_gate, near_down = pl.pallas_call(
+        )(gate)
+        return blocks, near
+    *blocks, near_gate = pl.pallas_call(
         functools.partial(fetch_kernel, block_rows, vocab),
-        out_shape=[jax.ShapeDtypeStruct((block_rows, features), BF16)] * GROUP + near,
-        in_specs=[pl.BlockSpec(memory_space=pltpu.SMEM), vmem] + [anywhere] * 3,
-        out_specs=[vmem] * (GROUP + 2),
+        out_shape=[jax.ShapeDtypeStruct((block_rows, features), BF16)] * GROUP + [near],
+        in_specs=[pl.BlockSpec(memory_space=pltpu.SMEM), vmem] + [anywhere] * 2,
+        out_specs=[vmem] * (GROUP + 1),
         scratch_shapes=[
             pltpu.VMEM((tokens.shape[0] * TILE, features), BF16),
-            pltpu.SemaphoreType.DMA((tokens.shape[0],)),
+            pltpu.SemaphoreType.DMA,
             weight_sems,
         ],
         compiler_params=params,
         name="fetch_rows",
-    )(tokens, tokens.reshape(1, -1), embedding, gate, down)
-    return blocks, near_gate, near_down
+    )(tokens, tokens.reshape(1, -1), embedding, gate)
+    return blocks, near_gate
 
 
 def position(chips):
@@ -180,7 +174,10 @@
 
 def first_kernel(chips, *refs):
     pieces, refs = refs[: 2 * GROUP], refs[2 * GROUP :]
-    gain, gate, down, partial, embedded, total, norms = refs
+    gain, gate, far_down, partial, embedded, total, norms, down, sems = refs
+    copies = split_copies(far_down.at[0], down, sems)
+    for copy in copies:
+        copy.start()
     tokens, width = embedded.shape
     segment, place, core, share = position(chips)
     features = width // (2 * chips)
@@ -203,6 +200,8 @@
         product = jnp.dot(scaled, gate[span, :], preferred_element_type=F32)
         total[...] = product if k == 0 else total[...] + product
     norms[...] = squares
+    for copy in copies:
+        copy.wait()
 
     @pl.when(segment < 2)
     def _():
@@ -330,18 +329,18 @@
     halves(projected, core, own, send)
 
 
-def kernel_call(kernel, name, inputs, outs, scratch, flops, vmem_limit=14):
+def kernel_call(kernel, name, inputs, outs, scratch, flops, vmem_limit=14, far=()):
     vmem = pl.BlockSpec(memory_space=pltpu.VMEM)
     return pl.pallas_call(
         functools.partial(kernel, lax.axis_size("tensor") // 2),
         out_shape=outs,
-        in_specs=[vmem] * len(inputs),
+        in_specs=[vmem] * len(inputs) + [pl.BlockSpec(memory_space=pl.ANY)] * len(far),
         out_specs=[vmem] * len(outs),
         scratch_shapes=scratch,
         compiler_params=pltpu.CompilerParams(vmem_limit_bytes=vmem_limit * 2**20),
         cost_estimate=pl.CostEstimate(flops=flops, bytes_accessed=0, transcendentals=0),
         name=name,
-    )(*inputs)
+    )(*inputs, *far)
 
 
 def choose(step, half_sum, terms):
@@ -374,8 +373,8 @@
     part = basis.shape[0] // GROUP
     quarter = lax.dynamic_slice_in_dim(basis, home * part, part, 0)
     bands = [quarter] + [swap(quarter, "tensor", 2 * m) for m in range(1, chips)]
-    blocks, gate, down = fetch_rows(tokens, embedding, gate_weight, down_weight)
-    blocks, bands = lax.optimization_barrier((blocks, bands))
+    blocks, gate = fetch_rows(tokens, embedding, gate_weight)
+    blocks, bands[2] = lax.optimization_barrier((blocks, bands[2]))
     bands = jnp.stack(bands)
     mask = GROUP
     while mask < segments:
@@ -391,18 +390,21 @@
     shares += [swap(shares[1][: chips // 2], "segment", 2), swap(shares[2][chips // 2 :], "segment", 1)]
     theirs = [swap(piece, "tensor", 1) for piece in mine]
     work = 2 * count * width
-    partial, embedded, total, norms = kernel_call(
+    partial, embedded, total, norms, down = kernel_call(
         first_kernel,
         "section_first",
-        mine + theirs + [gain, gate, down],
+        mine + theirs + [gain, gate],
         [
             pltpu.VMEM((count, width), BF16),
             pltpu.VMEM((count, width), BF16),
             pltpu.VMEM((count, hidden), F32),
             pltpu.VMEM((count, 1), F32),
+            pltpu.VMEM((hidden, width), BF16),
         ],
-        [],
+        [pltpu.SemaphoreType.DMA((PARTS,))],
         0,
+        14,
+        [down_weight],
     )
     partial, shares[GROUP - 1], shares[GROUP] = lax.optimization_barrier(
         (partial, shares[GROUP - 1], shares[GROUP])

time: 99.7 us -> 96.6 us (0.969)
  Pallas kernels: 16.3 us -> 14.2 us
    pallas_call x1, Pallas kernels: 9.2 us -> 5.27 us  [fetch_rows(): pl.pallas_call(functools.partial(fetch_kernel, block_rows, vocab), out_sh...]
    ppermute x36, waiting for transfers between devices: 39.2 us -> 37.1 us  [swap(): lax.ppermute(value, axis, [(i, i ^ mask) for i in range(lax.axis_size(axi...]
    pallas_call x12, Pallas kernels: 7.12 us -> 8.95 us  [kernel_call(): pl.pallas_call(functools.partial(kernel, lax.axis_size('tensor') // 2), o...]
    ppermute x2, waiting for transfers between devices: 2.74 us -> 3.93 us  [onward(): lax.ppermute(value, 'segment', [(i, (i ^ flip) + 2) for i in range(size -...]
  transfers between devices with their start and end apart: 38 -> 38, of which waited for: 22 -> 21; matrix products, arithmetic and copies ran while one was open for 0% -> 0% of each run, Pallas kernels for 13% -> 11%
where the time goes in v5:
time: 96.6 us; the launch traced here: 96.3 us
  waiting for transfers between devices  41 us (42%)
  starting transfers between devices  38.8 us (40%)
  Pallas kernels  14.2 us (15%)
  local copies, waits for them, and re-layouts  1.95 us (2%)
    ppermute x36, waiting for transfers between devices, swap(): lax.ppermute(value, axis, [(i, i ^ mask) for i in range(lax.axis_size(axi...  37.1 us
    ppermute x36, starting transfers between devices, swap(): lax.ppermute(value, axis, [(i, i ^ mask) for i in range(lax.axis_size(axi...  35.1 us
    pallas_call x12, Pallas kernels, kernel_call(): pl.pallas_call(functools.partial(kernel, lax.axis_size('tensor') // 2), o...  8.95 us
    pallas_call x1, Pallas kernels, fetch_rows(): pl.pallas_call(functools.partial(fetch_kernel, block_rows, vocab), out_sh...  5.27 us
    ppermute x2, waiting for transfers between devices, onward(): lax.ppermute(value, 'segment', [(i, (i ^ flip) + 2) for i in range(size -...  3.93 us
    ppermute x2, starting transfers between devices, onward(): lax.ppermute(value, 'segment', [(i, (i ^ flip) + 2) for i in range(size -...  3.68 us
  transfers between devices with their start and end apart: 38, of which 21 were waited for; matrix products, arithmetic and copies ran while one was open for 0% of the time, Pallas kernels for 11%

profile of v5, /device:TPU:0, one launch (start us, length us, event | category | flops | bytes accessed | tf_op | source)
XLA Modules:
  0.0 96.3 jit_solution(6301640859988628723)
XLA Ops:
  0.0 1.0 %copy-done = bf16[512,512]{1,0:T(8,128)(2,1)S(1)} copy-done((bf16[512,512]{1,0:T(8,128)(2,1)S(1)}, bf16[512,512]{1,0:T(8,128)(2,1)}, u32[]{:S(2)}) %copy-start) | copy-done | bytes 524312
  1.1 4.1 %collective-permute-start = (bf16[128,512]{1,0:T(8,128)(2,1)S(1)}, bf16[128,512]{1,0:T(8,128)(2,1)S(1)}, u32[]{:S(2)}, u32[]{:S(2)}) collective-permute-start(bf16[128,512]{1,0:T(8,128)(2,1)S(1)} %constant_dynamic-slice_fusion), channel_id=1, source_target_pairs={{0,4},{1,5},{2,6},{3,7},{4,0},{5,1},{6,2},{7,3},{8,12},{9,13},{10,... | collective-permute-start | bytes 393224 | tf_op jit(solution)/shard_map/ppermute | solution.py:20
  5.2 1.6 %collective-permute-start.2 = (bf16[128,512]{1,0:T(8,128)(2,1)S(1)}, bf16[128,512]{1,0:T(8,128)(2,1)S(1)}, u32[]{:S(2)}, u32[]{:S(2)}) collective-permute-start(bf16[128,512]{1,0:T(8,128)(2,1)S(1)} %constant_dynamic-slice_fusion), channel_id=1, source_target_pairs={{0,2},{1,3},{2,0},{3,1},{4,6},{5,7},{6,4},{7,5},{8,10},{9,11},{10,... | collective-permute-start | bytes 393224 | tf_op jit(solution)/shard_map/ppermute | solution.py:20
  6.7 0.0 collective-permute-start.3
  6.7 0.8 copy-done.3
  7.6 5.3 %fetch_rows.1 = (bf16[48,512]{1,0:T(8,128)(2,1)S(1)}, bf16[48,512]{1,0:T(8,128)(2,1)S(1)}, bf16[48,512]{1,0:T(8,128)(2,1)S(1)}, bf16[48,512]{1,0:T(8,128)(2,1)S(1)}, bf16[4096,896]{1,0:T(8,128)(2,1)S(1)}) custom-call(s32[192]{0:T(256)S(1)} %copy-done.3, s32[1,192]{1,0:T(1,128)S(1)} %bitcast.12, bf16[16032,512]{1,0:T(8,128)(2,1)} %table.1, ...), custom_call_target="tpu_custom_call" | custom-call | tf_op jit(solution)/shard_map/fetch_rows/pallas_call | solution.py:147
  12.9 0.2 collective-permute-done
  13.1 2.1 %collective-permute-start.1 = (bf16[48,512]{1,0:T(8,128)(2,1)S(1)}, bf16[48,512]{1,0:T(8,128)(2,1)S(1)}, u32[]{:S(2)}, u32[]{:S(2)}) collective-permute-start(bf16[48,512]{1,0:T(8,128)(2,1)S(1)} %get-tuple-element.44), channel_id=1, source_target_pairs={{0,8},{8,0},{16,24},{24,16},{1,9},{9,1},{17,25},{25,17},{2,10},{10... | collective-permute-start | bytes 147464 | tf_op jit(solution)/shard_map/ppermute | solution.py:20
  15.2 1.5 %collective-permute-start.6 = (bf16[48,512]{1,0:T(8,128)(2,1)S(1)}, bf16[48,512]{1,0:T(8,128)(2,1)S(1)}, u32[]{:S(2)}, u32[]{:S(2)}) collective-permute-start(bf16[48,512]{1,0:T(8,128)(2,1)S(1)} %get-tuple-element.49), channel_id=1, source_target_pairs={{0,16},{8,24},{16,0},{24,8},{1,17},{9,25},{17,1},{25,9},{2,18},{10... | collective-permute-start | bytes 147464 | tf_op jit(solution)/shard_map/ppermute | solution.py:20
  16.8 0.0 collective-permute-done.3
  16.8 0.1 pad_maximum_fusion.refs_0_
  16.9 0.6 collective-permute-done.1
  17.5 2.4 %collective-permute-start.5 = (bf16[4,128,512]{2,1,0:T(8,128)(2,1)S(1)}, bf16[4,128,512]{2,1,0:T(8,128)(2,1)S(1)}, u32[]{:S(2)}, u32[]{:S(2)}) collective-permute-start(bf16[4,128,512]{2,1,0:T(8,128)(2,1)S(1)} %pad_maximum_fusion.refs_0_), channel_id=1, source_target_pairs={{0,16},{8,24},{16,0},{24,8},{1,17},{9,25},{17,1},{25,9},{2,18},{10... | collective-permute-start | bytes 1572872 | tf_op jit(solution)/shard_map/ppermute | solution.py:20
  19.9 1.0 %collective-permute-start.4 = (bf16[4,128,512]{2,1,0:T(8,128)(2,1)S(1)}, bf16[4,128,512]{2,1,0:T(8,128)(2,1)S(1)}, u32[]{:S(2)}, u32[]{:S(2)}) collective-permute-start(bf16[4,128,512]{2,1,0:T(8,128)(2,1)S(1)} %pad_maximum_fusion.refs_0_), channel_id=1, source_target_pairs={{0,8},{8,0},{16,24},{24,16},{1,9},{9,1},{17,25},{25,17},{2,10},{10... | collective-permute-start | bytes 1572872 | tf_op jit(solution)/shard_map/ppermute | solution.py:20
  20.9 1.5 %collective-permute-done.7 = bf16[48,512]{1,0:T(8,128)(2,1)S(1)} collective-permute-done((bf16[48,512]{1,0:T(8,128)(2,1)S(1)}, bf16[48,512]{1,0:T(8,128)(2,1)S(1)}, u32[]{:S(2)}, u32[]{:S(2)}) %collective-permute-start.7) | collective-permute-done | bytes 49184 | tf_op jit(solution)/shard_map/ppermute | solution.py:20
  22.4 3.1 %collective-permute-start.10 = (bf16[48,512]{1,0:T(8,128)(2,1)S(1)}, bf16[48,512]{1,0:T(8,128)(2,1)S(1)}, u32[]{:S(2)}, u32[]{:S(2)}) collective-permute-start(bf16[48,512]{1,0:T(8,128)(2,1)S(1)} %add_add_fusion), channel_id=1, source_target_pairs={{0,6},{1,7},{2,4},{3,5},{4,2},{5,3},{6,0},{7,1},{8,14},{9,15},{10,... | collective-permute-start | bytes 147464 | tf_op jit(solution)/shard_map/ppermute | solution.py:20
  25.5 1.3 %collective-permute-start.8 = (bf16[48,512]{1,0:T(8,128)(2,1)S(1)}, bf16[48,512]{1,0:T(8,128)(2,1)S(1)}, u32[]{:S(2)}, u32[]{:S(2)}) collective-permute-start(bf16[48,512]{1,0:T(8,128)(2,1)S(1)} %add_add_fusion), channel_id=1, source_target_pairs={{0,2},{1,3},{2,0},{3,1},{4,6},{5,7},{6,4},{7,5},{8,10},{9,11},{10,... | collective-permute-start | bytes 147464 | tf_op jit(solution)/shard_map/ppermute | solution.py:20
  26.8 1.5 %collective-permute-done.10 = bf16[48,512]{1,0:T(8,128)(2,1)S(1)} collective-permute-done((bf16[48,512]{1,0:T(8,128)(2,1)S(1)}, bf16[48,512]{1,0:T(8,128)(2,1)S(1)}, u32[]{:S(2)}, u32[]{:S(2)}) %collective-permute-start.10) | collective-permute-done | bytes 49184 | tf_op jit(solution)/shard_map/ppermute | solution.py:20
  28.3 2.2 %collective-permute-done.9 = bf16[48,512]{1,0:T(8,128)(2,1)S(1)} collective-permute-done((bf16[48,512]{1,0:T(8,128)(2,1)S(1)}, bf16[48,512]{1,0:T(8,128)(2,1)S(1)}, u32[]{:S(2)}, u32[]{:S(2)}) %collective-permute-start.9) | collective-permute-done | bytes 49184 | tf_op jit(solution)/shard_map/ppermute | solution.py:20
  30.5 0.1 collective-permute-start.13
  30.6 2.0 %collective-permute-start.12 = (bf16[4,48,512]{2,1,0:T(8,128)(2,1)S(1)}, bf16[4,48,512]{2,1,0:T(8,128)(2,1)S(1)}, u32[]{:S(2)}, u32[]{:S(2)}) collective-permute-start(bf16[4,48,512]{2,1,0:T(8,128)(2,1)S(1)} %pad_maximum_fusion.1.refs_0_), channel_id=1, source_target_pairs={{0,16},{8,24},{16,0},{24,8},{1,17},{9,25},{17,1},{25,9},{2,18},{10... | collective-permute-start | bytes 589832 | tf_op jit(solution)/shard_map/ppermute | solution.py:20
  32.6 1.5 %collective-permute-start.11 = (bf16[4,48,512]{2,1,0:T(8,128)(2,1)S(1)}, bf16[4,48,512]{2,1,0:T(8,128)(2,1)S(1)}, u32[]{:S(2)}, u32[]{:S(2)}) collective-permute-start(bf16[4,48,512]{2,1,0:T(8,128)(2,1)S(1)} %pad_maximum_fusion.1.refs_0_), channel_id=1, source_target_pairs={{0,8},{8,0},{16,24},{24,16},{1,9},{9,1},{17,25},{25,17},{2,10},{10... | collective-permute-start | bytes 589832 | tf_op jit(solution)/shard_map/ppermute | solution.py:20
  34.1 3.4 %collective-permute-done.13.refs_3_ = bf16[4,48,512]{2,1,0:T(8,128)(2,1)S(1)} collective-permute-done((bf16[4,48,512]{2,1,0:T(8,128)(2,1)S(1)}, bf16[4,48,512]{2,1,0:T(8,128)(2,1)S(1)}, u32[]{:S(2)}, u32[]{:S(2)}) %collective-permute-start.13) | collective-permute-done | bytes 196640 | tf_op jit(solution)/shard_map/ppermute | solution.py:20
  37.5 1.8 %collective-permute-done.12.refs_2_ = bf16[4,48,512]{2,1,0:T(8,128)(2,1)S(1)} collective-permute-done((bf16[4,48,512]{2,1,0:T(8,128)(2,1)S(1)}, bf16[4,48,512]{2,1,0:T(8,128)(2,1)S(1)}, u32[]{:S(2)}, u32[]{:S(2)}) %collective-permute-start.12) | collective-permute-done | bytes 196640 | tf_op jit(solution)/shard_map/ppermute | solution.py:20
  39.3 0.3 collective-permute-done.11.refs_1_
  39.6 0.3 collective-permute-start.15
  39.8 0.3 collective-permute-start.17
  40.1 1.0 %collective-permute-start.19 = (bf16[2,128,512]{2,1,0:T(8,128)(2,1)S(1)}, bf16[2,128,512]{2,1,0:T(8,128)(2,1)S(1)}, u32[]{:S(2)}, u32[]{:S(2)}) collective-permute-start(bf16[2,128,512]{2,1,0:T(8,128)(2,1)S(1)} %slice.9), channel_id=1, source_target_pairs={{0,8},{8,0},{16,24},{24,16},{1,9},{9,1},{17,25},{25,17},{2,10},{10... | collective-permute-start | bytes 786440 | tf_op jit(solution)/shard_map/ppermute | solution.py:20
  41.2 1.2 %collective-permute-start.18 = (bf16[2,128,512]{2,1,0:T(8,128)(2,1)S(1)}, bf16[2,128,512]{2,1,0:T(8,128)(2,1)S(1)}, u32[]{:S(2)}, u32[]{:S(2)}) collective-permute-start(bf16[2,128,512]{2,1,0:T(8,128)(2,1)S(1)} %slice.8), channel_id=1, source_target_pairs={{0,16},{8,24},{16,0},{24,8},{1,17},{9,25},{17,1},{25,9},{2,18},{10... | collective-permute-start | bytes 786440 | tf_op jit(solution)/shard_map/ppermute | solution.py:20
  42.4 0.5 collective-permute-start.22
  42.9 0.1 collective-permute-start.21
  43.0 5.7 %section_first.1 = (bf16[192,4096]{1,0:T(8,128)(2,1)S(1)}, bf16[192,4096]{1,0:T(8,128)(2,1)S(1)}, f32[192,896]{1,0:T(8,128)S(1)}, f32[192,1]{1,0:T(8,128)S(1)}, bf16[896,4096]{1,0:T(8,128)(2,1)S(1)}) custom-call(bf16[4,48,512]{2,1,0:T(8,128)(2,1)S(1)} %pad_maximum_fusion.1.refs_0_, bf16[4,48,512]{2,1,0:T(8,128)(2,1)S(1)} %collective-permute-done.11.refs_1_, ...), custom_call_target="tpu_custom_call" | custom-call | tf_op jit(solution)/shard_map/section_first/pallas_call | solution.py:334
  48.7 0.5 collective-permute-done.18.refs_3_
  49.2 0.0 collective-permute-start.23
  49.2 0.5 collective-permute-start.24
  49.8 1.0 %collective-permute-done.23.refs_8_ = bf16[2,128,512]{2,1,0:T(8,128)(2,1)S(1)} collective-permute-done((bf16[2,128,512]{2,1,0:T(8,128)(2,1)S(1)}, bf16[2,128,512]{2,1,0:T(8,128)(2,1)S(1)}, u32[]{:S(2)}, u32[]{:S(2)}) %collective-permute-start.23) | collective-permute-done | bytes 262176 | tf_op jit(solution)/shard_map/ppermute | solution.py:20
  50.8 0.4 collective-permute-done.24.refs_9_
  51.1 1.3 %project_first.1 = (bf16[96,512]{1,0:T(8,128)(2,1)S(1)}, bf16[96,512]{1,0:T(8,128)(2,1)S(1)}, bf16[4096,512]{1,0:T(8,128)(2,1)S(1)}) custom-call(bf16[4,128,512]{2,1,0:T(8,128)(2,1)S(1)} %pad_maximum_fusion.refs_0_, bf16[4,128,512]{2,1,0:T(8,128)(2,1)S(1)} %collective-permute-done.4.refs_1_, bf16[4,128,512]{2,1,0:T(8,128)(2,1)S(1)} %collective-permute-done.5.refs_2_, ...), custom_call_target="tpu_custom_call" | custom-call | flops 805306368 | tf_op jit(solution)/shard_map/project_first/pallas_call | solution.py:334
  52.5 0.2 collective-permute-start.25
  52.7 1.2 %collective-permute-done.25.refs_1_ = bf16[96,512]{1,0:T(8,128)(2,1)S(1)} collective-permute-done((bf16[96,512]{1,0:T(8,128)(2,1)S(1)}, bf16[96,512]{1,0:T(8,128)(2,1)S(1)}, u32[]{:S(2)}, u32[]{:S(2)}) %collective-permute-start.25) | collective-permute-done | bytes 98336 | tf_op jit(solution)/shard_map/ppermute | solution.py:20
  53.9 3.6 %collective-permute-start.28 = (bf16[96,512]{1,0:T(8,128)(2,1)S(1)}, bf16[96,512]{1,0:T(8,128)(2,1)S(1)}, u32[]{:S(2)}, u32[]{:S(2)}) collective-permute-start(bf16[96,512]{1,0:T(8,128)(2,1)S(1)} %add.29.refs_0_), channel_id=1, source_target_pairs={{0,6},{1,7},{2,4},{3,5},{4,2},{5,3},{6,0},{7,1},{8,14},{9,15},{10,... | collective-permute-start | bytes 294920 | tf_op jit(solution)/shard_map/ppermute | solution.py:20
  57.5 0.9 collective-permute-start.27
  58.4 0.5 collective-permute-start.26
  58.9 1.8 %collective-permute-done.28.refs_3_ = bf16[96,512]{1,0:T(8,128)(2,1)S(1)} collective-permute-done((bf16[96,512]{1,0:T(8,128)(2,1)S(1)}, bf16[96,512]{1,0:T(8,128)(2,1)S(1)}, u32[]{:S(2)}, u32[]{:S(2)}) %collective-permute-start.28) | collective-permute-done | bytes 98336 | tf_op jit(solution)/shard_map/ppermute | solution.py:20
  60.7 6.2 %collective-permute-done.27.refs_2_ = bf16[96,512]{1,0:T(8,128)(2,1)S(1)} collective-permute-done((bf16[96,512]{1,0:T(8,128)(2,1)S(1)}, bf16[96,512]{1,0:T(8,128)(2,1)S(1)}, u32[]{:S(2)}, u32[]{:S(2)}) %collective-permute-start.27) | collective-permute-done | bytes 98336 | tf_op jit(solution)/shard_map/ppermute | solution.py:20
  66.9 0.1 add.30.after
  67.0 2.4 %collective-permute-start.30 = (bf16[96,512]{1,0:T(8,128)(2,1)S(1)}, bf16[96,512]{1,0:T(8,128)(2,1)S(1)}, u32[]{:S(2)}, u32[]{:S(2)}) collective-permute-start(bf16[96,512]{1,0:T(8,128)(2,1)S(1)} %add.30.after), channel_id=1, source_target_pairs={{0,24},{8,16},{1,25},{9,17},{2,26},{10,18},{3,27},{11,19},{4,28},{... | collective-permute-start | bytes 294920 | tf_op jit(solution)/shard_map/ppermute | solution.py:25
  69.3 1.3 %collective-permute-start.29 = (bf16[96,512]{1,0:T(8,128)(2,1)S(1)}, bf16[96,512]{1,0:T(8,128)(2,1)S(1)}, u32[]{:S(2)}, u32[]{:S(2)}) collective-permute-start(bf16[96,512]{1,0:T(8,128)(2,1)S(1)} %add.30.after), channel_id=1, source_target_pairs={{0,16},{8,24},{1,17},{9,25},{2,18},{10,26},{3,19},{11,27},{4,20},{... | collective-permute-start | bytes 294920 | tf_op jit(solution)/shard_map/ppermute | solution.py:25
  70.7 0.0 copy-start.1
  70.7 3.9 %collective-permute-done.29.refs_0_ = bf16[96,512]{1,0:T(8,128)(2,1)S(1)} collective-permute-done((bf16[96,512]{1,0:T(8,128)(2,1)S(1)}, bf16[96,512]{1,0:T(8,128)(2,1)S(1)}, u32[]{:S(2)}, u32[]{:S(2)}) %collective-permute-start.29) | collective-permute-done | bytes 98336 | tf_op jit(solution)/shard_map/ppermute | solution.py:25
  74.7 0.1 collective-permute-start.31
  74.7 1.3 %collective-permute-done.31.refs_1_ = bf16[96,512]{1,0:T(8,128)(2,1)S(1)} collective-permute-done((bf16[96,512]{1,0:T(8,128)(2,1)S(1)}, bf16[96,512]{1,0:T(8,128)(2,1)S(1)}, u32[]{:S(2)}, u32[]{:S(2)}) %collective-permute-start.31) | collective-permute-done | bytes 98336 | tf_op jit(solution)/shard_map/ppermute | solution.py:20
  76.0 1.0 %section_next.1 = (bf16[96,512]{1,0:T(8,128)(2,1)S(1)}, bf16[96,512]{1,0:T(8,128)(2,1)S(1)}) custom-call(bf16[96,512]{1,0:T(8,128)(2,1)S(1)} %add.31.refs_0_, bf16[96,512]{1,0:T(8,128)(2,1)S(1)} %collective-permute-done.31.refs_1_, f32[192,896]{1,0:T(8,128)S(1)} %get-tuple-element.66.refs_2_, f32[192,1]{1,0:T(8,128)S(1)} %get-tuple-element.67.refs_3_, ...), custom_call_target="tpu_custom_call" | custom-call | flops 553648128 | tf_op jit(solution)/shard_map/section_next/pallas_call | solution.py:334
  77.1 0.2 collective-permute-start.32
  77.3 1.1 %collective-permute-done.32.refs_1_ = bf16[96,512]{1,0:T(8,128)(2,1)S(1)} collective-permute-done((bf16[96,512]{1,0:T(8,128)(2,1)S(1)}, bf16[96,512]{1,0:T(8,128)(2,1)S(1)}, u32[]{:S(2)}, u32[]{:S(2)}) %collective-permute-start.32) | collective-permute-done | bytes 98336 | tf_op jit(solution)/shard_map/ppermute | solution.py:20
  78.4 2.2 %collective-permute-start.35 = (bf16[96,512]{1,0:T(8,128)(2,1)S(1)}, bf16[96,512]{1,0:T(8,128)(2,1)S(1)}, u32[]{:S(2)}, u32[]{:S(2)}) collective-permute-start(bf16[96,512]{1,0:T(8,128)(2,1)S(1)} %add.32.refs_0_), channel_id=1, source_target_pairs={{0,6},{1,7},{2,4},{3,5},{4,2},{5,3},{6,0},{7,1},{8,14},{9,15},{10,... | collective-permute-start | bytes 294920 | tf_op jit(solution)/shard_map/ppermute | solution.py:20
  80.6 2.3 %collective-permute-start.33 = (bf16[96,512]{1,0:T(8,128)(2,1)S(1)}, bf16[96,512]{1,0:T(8,128)(2,1)S(1)}, u32[]{:S(2)}, u32[]{:S(2)}) collective-permute-start(bf16[96,512]{1,0:T(8,128)(2,1)S(1)} %add.32.refs_0_), channel_id=1, source_target_pairs={{0,2},{1,3},{2,0},{3,1},{4,6},{5,7},{6,4},{7,5},{8,10},{9,11},{10,... | collective-permute-start | bytes 294920 | tf_op jit(solution)/shard_map/ppermute | solution.py:20
  82.9 3.1 %collective-permute-done.35.refs_3_ = bf16[96,512]{1,0:T(8,128)(2,1)S(1)} collective-permute-done((bf16[96,512]{1,0:T(8,128)(2,1)S(1)}, bf16[96,512]{1,0:T(8,128)(2,1)S(1)}, u32[]{:S(2)}, u32[]{:S(2)}) %collective-permute-start.35) | collective-permute-done | bytes 98336 | tf_op jit(solution)/shard_map/ppermute | solution.py:20
  86.0 3.3 %collective-permute-done.34.refs_2_ = bf16[96,512]{1,0:T(8,128)(2,1)S(1)} collective-permute-done((bf16[96,512]{1,0:T(8,128)(2,1)S(1)}, bf16[96,512]{1,0:T(8,128)(2,1)S(1)}, u32[]{:S(2)}, u32[]{:S(2)}) %collective-permute-start.34) | collective-permute-done | bytes 98336 | tf_op jit(solution)/shard_map/ppermute | solution.py:20
  89.4 0.5 collective-permute-start.36
  89.9 4.2 %collective-permute-done.36.refs_1_ = bf16[96,512]{1,0:T(8,128)(2,1)S(1)} collective-permute-done((bf16[96,512]{1,0:T(8,128)(2,1)S(1)}, bf16[96,512]{1,0:T(8,128)(2,1)S(1)}, u32[]{:S(2)}, u32[]{:S(2)}) %collective-permute-start.36) | collective-permute-done | bytes 98336 | tf_op jit(solution)/shard_map/ppermute | solution.py:20
  94.2 0.1 collective-permute-start.37
  94.3 1.3 %collective-permute-done.37.far = bf16[96,512]{1,0:T(8,128)(2,1)S(1)} collective-permute-done((bf16[96,512]{1,0:T(8,128)(2,1)S(1)}, bf16[96,512]{1,0:T(8,128)(2,1)S(1)}, u32[]{:S(2)}, u32[]{:S(2)}) %collective-permute-start.37) | collective-permute-done | bytes 98336 | tf_op jit(solution)/shard_map/ppermute | solution.py:20
  95.6 0.7 collect.1
  (45 shorter events, 0.3 us)
Async XLA Ops:
  0.0 1.0 %copy-start = (bf16[512,512]{1,0:T(8,128)(2,1)S(1)}, bf16[512,512]{1,0:T(8,128)(2,1)}, u32[]{:S(2)}) copy-start(bf16[512,512]{1,0:T(8,128)(2,1)} %param.11) | copy-start | bytes 1572868
  1.1 12.1 %collective-permute-start = (bf16[128,512]{1,0:T(8,128)(2,1)S(1)}, bf16[128,512]{1,0:T(8,128)(2,1)S(1)}, u32[]{:S(2)}, u32[]{:S(2)}) collective-permute-start(bf16[128,512]{1,0:T(8,128)(2,1)S(1)} %constant_dynamic-slice_fusion), channel_id=1, source_target_pairs={{0,4},{1,5},{2,6},{3,7},{4,0},{5,1},{6,2},{7,3},{8,12},{9,13},{10,... | collective-permute-start | bytes 393224 | tf_op jit(solution)/shard_map/ppermute | solution.py:20
  5.2 11.6 %collective-permute-start.2 = (bf16[128,512]{1,0:T(8,128)(2,1)S(1)}, bf16[128,512]{1,0:T(8,128)(2,1)S(1)}, u32[]{:S(2)}, u32[]{:S(2)}) collective-permute-start(bf16[128,512]{1,0:T(8,128)(2,1)S(1)} %constant_dynamic-slice_fusion), channel_id=1, source_target_pairs={{0,2},{1,3},{2,0},{3,1},{4,6},{5,7},{6,4},{7,5},{8,10},{9,11},{10,... | collective-permute-start | bytes 393224 | tf_op jit(solution)/shard_map/ppermute | solution.py:20
  6.7 10.0 %collective-permute-start.3 = (bf16[128,512]{1,0:T(8,128)(2,1)S(1)}, bf16[128,512]{1,0:T(8,128)(2,1)S(1)}, u32[]{:S(2)}, u32[]{:S(2)}) collective-permute-start(bf16[128,512]{1,0:T(8,128)(2,1)S(1)} %constant_dynamic-slice_fusion), channel_id=1, source_target_pairs={{0,6},{1,7},{2,4},{3,5},{4,2},{5,3},{6,0},{7,1},{8,14},{9,15},{10,... | collective-permute-start | bytes 393224 | tf_op jit(solution)/shard_map/ppermute | solution.py:20
  6.7 36.2 %slice-start = ((s8[7340032]{0:T(1024)(128)(4,1)}), s8[4194304]{0:T(1024)(128)(4,1)S(1)}, s32[]{:S(2)}) async-start(s8[7340032]{0:T(1024)(128)(4,1)} %bitcast.10), calls=%async_computation | async-start | bytes 8388608
  6.7 0.8 copy-start.3
  7.6 35.4 %slice-start.1 = ((s8[7340032]{0:T(1024)(128)(4,1)}), s8[3145728]{0:T(1024)(128)(4,1)S(1)}, s32[]{:S(2)}) async-start(s8[7340032]{0:T(1024)(128)(4,1)} %bitcast.10), calls=%async_computation.1 | async-start | bytes 6291456
  7.6 35.4 %copy-start.2 = (f32[2,4096]{1,0:T(2,128)S(1)}, f32[2,4096]{1,0:T(2,128)}, u32[]{:S(2)}) copy-start(f32[2,4096]{1,0:T(2,128)} %refs_2_.1) | copy-start | bytes 98308
  13.1 4.4 %collective-permute-start.1 = (bf16[48,512]{1,0:T(8,128)(2,1)S(1)}, bf16[48,512]{1,0:T(8,128)(2,1)S(1)}, u32[]{:S(2)}, u32[]{:S(2)}) collective-permute-start(bf16[48,512]{1,0:T(8,128)(2,1)S(1)} %get-tuple-element.44), channel_id=1, source_target_pairs={{0,8},{8,0},{16,24},{24,16},{1,9},{9,1},{17,25},{25,17},{2,10},{10... | collective-permute-start | bytes 147464 | tf_op jit(solution)/shard_map/ppermute | solution.py:20
  15.2 5.6 %collective-permute-start.6 = (bf16[48,512]{1,0:T(8,128)(2,1)S(1)}, bf16[48,512]{1,0:T(8,128)(2,1)S(1)}, u32[]{:S(2)}, u32[]{:S(2)}) collective-permute-start(bf16[48,512]{1,0:T(8,128)(2,1)S(1)} %get-tuple-element.49), channel_id=1, source_target_pairs={{0,16},{8,24},{16,0},{24,8},{1,17},{9,25},{17,1},{25,9},{2,18},{10... | collective-permute-start | bytes 147464 | tf_op jit(solution)/shard_map/ppermute | solution.py:20
  16.8 5.6 %collective-permute-start.7 = (bf16[48,512]{1,0:T(8,128)(2,1)S(1)}, bf16[48,512]{1,0:T(8,128)(2,1)S(1)}, u32[]{:S(2)}, u32[]{:S(2)}) collective-permute-start(bf16[48,512]{1,0:T(8,128)(2,1)S(1)} %get-tuple-element.50), channel_id=1, source_target_pairs={{0,24},{8,16},{16,8},{24,0},{1,25},{9,17},{17,9},{25,1},{2,26},{10... | collective-permute-start | bytes 147464 | tf_op jit(solution)/shard_map/ppermute | solution.py:20
  17.5 22.3 %collective-permute-start.5 = (bf16[4,128,512]{2,1,0:T(8,128)(2,1)S(1)}, bf16[4,128,512]{2,1,0:T(8,128)(2,1)S(1)}, u32[]{:S(2)}, u32[]{:S(2)}) collective-permute-start(bf16[4,128,512]{2,1,0:T(8,128)(2,1)S(1)} %pad_maximum_fusion.refs_0_), channel_id=1, source_target_pairs={{0,16},{8,24},{16,0},{24,8},{1,17},{9,25},{17,1},{25,9},{2,18},{10... | collective-permute-start | bytes 1572872 | tf_op jit(solution)/shard_map/ppermute | solution.py:20
  19.9 19.9 %collective-permute-start.4 = (bf16[4,128,512]{2,1,0:T(8,128)(2,1)S(1)}, bf16[4,128,512]{2,1,0:T(8,128)(2,1)S(1)}, u32[]{:S(2)}, u32[]{:S(2)}) collective-permute-start(bf16[4,128,512]{2,1,0:T(8,128)(2,1)S(1)} %pad_maximum_fusion.refs_0_), channel_id=1, source_target_pairs={{0,8},{8,0},{16,24},{24,16},{1,9},{9,1},{17,25},{25,17},{2,10},{10... | collective-permute-start | bytes 1572872 | tf_op jit(solution)/shard_map/ppermute | solution.py:20
  22.4 6.0 %collective-permute-start.10 = (bf16[48,512]{1,0:T(8,128)(2,1)S(1)}, bf16[48,512]{1,0:T(8,128)(2,1)S(1)}, u32[]{:S(2)}, u32[]{:S(2)}) collective-permute-start(bf16[48,512]{1,0:T(8,128)(2,1)S(1)} %add_add_fusion), channel_id=1, source_target_pairs={{0,6},{1,7},{2,4},{3,5},{4,2},{5,3},{6,0},{7,1},{8,14},{9,15},{10,... | collective-permute-start | bytes 147464 | tf_op jit(solution)/shard_map/ppermute | solution.py:20
  25.5 5.0 %collective-permute-start.9 = (bf16[48,512]{1,0:T(8,128)(2,1)S(1)}, bf16[48,512]{1,0:T(8,128)(2,1)S(1)}, u32[]{:S(2)}, u32[]{:S(2)}) collective-permute-start(bf16[48,512]{1,0:T(8,128)(2,1)S(1)} %add_add_fusion), channel_id=1, source_target_pairs={{0,4},{1,5},{2,6},{3,7},{4,0},{5,1},{6,2},{7,3},{8,12},{9,13},{10,... | collective-permute-start | bytes 147464 | tf_op jit(solution)/shard_map/ppermute | solution.py:20
  25.5 5.0 %collective-permute-start.8 = (bf16[48,512]{1,0:T(8,128)(2,1)S(1)}, bf16[48,512]{1,0:T(8,128)(2,1)S(1)}, u32[]{:S(2)}, u32[]{:S(2)}) collective-permute-start(bf16[48,512]{1,0:T(8,128)(2,1)S(1)} %add_add_fusion), channel_id=1, source_target_pairs={{0,2},{1,3},{2,0},{3,1},{4,6},{5,7},{6,4},{7,5},{8,10},{9,11},{10,... | collective-permute-start | bytes 147464 | tf_op jit(solution)/shard_map/ppermute | solution.py:20
  30.5 7.0 %collective-permute-start.13 = (bf16[4,48,512]{2,1,0:T(8,128)(2,1)S(1)}, bf16[4,48,512]{2,1,0:T(8,128)(2,1)S(1)}, u32[]{:S(2)}, u32[]{:S(2)}) collective-permute-start(bf16[4,48,512]{2,1,0:T(8,128)(2,1)S(1)} %pad_maximum_fusion.1.refs_0_), channel_id=1, source_target_pairs={{0,24},{8,16},{16,8},{24,0},{1,25},{9,17},{17,9},{25,1},{2,26},{10... | collective-permute-start | bytes 589832 | tf_op jit(solution)/shard_map/ppermute | solution.py:20
  30.6 8.7 %collective-permute-start.12 = (bf16[4,48,512]{2,1,0:T(8,128)(2,1)S(1)}, bf16[4,48,512]{2,1,0:T(8,128)(2,1)S(1)}, u32[]{:S(2)}, u32[]{:S(2)}) collective-permute-start(bf16[4,48,512]{2,1,0:T(8,128)(2,1)S(1)} %pad_maximum_fusion.1.refs_0_), channel_id=1, source_target_pairs={{0,16},{8,24},{16,0},{24,8},{1,17},{9,25},{17,1},{25,9},{2,18},{10... | collective-permute-start | bytes 589832 | tf_op jit(solution)/shard_map/ppermute | solution.py:20
  32.6 7.0 %collective-permute-start.11 = (bf16[4,48,512]{2,1,0:T(8,128)(2,1)S(1)}, bf16[4,48,512]{2,1,0:T(8,128)(2,1)S(1)}, u32[]{:S(2)}, u32[]{:S(2)}) collective-permute-start(bf16[4,48,512]{2,1,0:T(8,128)(2,1)S(1)} %pad_maximum_fusion.1.refs_0_), channel_id=1, source_target_pairs={{0,8},{8,0},{16,24},{24,16},{1,9},{9,1},{17,25},{25,17},{2,10},{10... | collective-permute-start | bytes 589832 | tf_op jit(solution)/shard_map/ppermute | solution.py:20
  37.5 3.6 %collective-permute-start.14 = (bf16[4,48,512]{2,1,0:T(8,128)(2,1)S(1)}, bf16[4,48,512]{2,1,0:T(8,128)(2,1)S(1)}, u32[]{:S(2)}, u32[]{:S(2)}) collective-permute-start(bf16[4,48,512]{2,1,0:T(8,128)(2,1)S(1)} %pad_maximum_fusion.1.refs_0_), channel_id=1, source_target_pairs={{0,1},{1,0},{2,3},{3,2},{4,5},{5,4},{6,7},{7,6},{8,9},{9,8},{10,11... | collective-permute-start | bytes 589832 | tf_op jit(solution)/shard_map/ppermute | solution.py:20
  39.3 3.1 %collective-permute-start.16 = (bf16[4,48,512]{2,1,0:T(8,128)(2,1)S(1)}, bf16[4,48,512]{2,1,0:T(8,128)(2,1)S(1)}, u32[]{:S(2)}, u32[]{:S(2)}) collective-permute-start(bf16[4,48,512]{2,1,0:T(8,128)(2,1)S(1)} %collective-permute-done.12.refs_2_), channel_id=1, source_target_pairs={{0,1},{1,0},{2,3},{3,2},{4,5},{5,4},{6,7},{7,6},{8,9},{9,8},{10,11... | collective-permute-start | bytes 589832 | tf_op jit(solution)/shard_map/ppermute | solution.py:20
  39.6 2.8 %collective-permute-start.15 = (bf16[4,48,512]{2,1,0:T(8,128)(2,1)S(1)}, bf16[4,48,512]{2,1,0:T(8,128)(2,1)S(1)}, u32[]{:S(2)}, u32[]{:S(2)}) collective-permute-start(bf16[4,48,512]{2,1,0:T(8,128)(2,1)S(1)} %collective-permute-done.11.refs_1_), channel_id=1, source_target_pairs={{0,1},{1,0},{2,3},{3,2},{4,5},{5,4},{6,7},{7,6},{8,9},{9,8},{10,11... | collective-permute-start | bytes 589832 | tf_op jit(solution)/shard_map/ppermute | solution.py:20
  39.8 3.1 %collective-permute-start.17 = (bf16[4,48,512]{2,1,0:T(8,128)(2,1)S(1)}, bf16[4,48,512]{2,1,0:T(8,128)(2,1)S(1)}, u32[]{:S(2)}, u32[]{:S(2)}) collective-permute-start(bf16[4,48,512]{2,1,0:T(8,128)(2,1)S(1)} %collective-permute-done.13.refs_3_), channel_id=1, source_target_pairs={{0,1},{1,0},{2,3},{3,2},{4,5},{5,4},{6,7},{7,6},{8,9},{9,8},{10,11... | collective-permute-start | bytes 589832 | tf_op jit(solution)/shard_map/ppermute | solution.py:20
  40.1 8.6 %collective-permute-start.19 = (bf16[2,128,512]{2,1,0:T(8,128)(2,1)S(1)}, bf16[2,128,512]{2,1,0:T(8,128)(2,1)S(1)}, u32[]{:S(2)}, u32[]{:S(2)}) collective-permute-start(bf16[2,128,512]{2,1,0:T(8,128)(2,1)S(1)} %slice.9), channel_id=1, source_target_pairs={{0,8},{8,0},{16,24},{24,16},{1,9},{9,1},{17,25},{25,17},{2,10},{10... | collective-permute-start | bytes 786440 | tf_op jit(solution)/shard_map/ppermute | solution.py:20
  41.2 8.1 %collective-permute-start.18 = (bf16[2,128,512]{2,1,0:T(8,128)(2,1)S(1)}, bf16[2,128,512]{2,1,0:T(8,128)(2,1)S(1)}, u32[]{:S(2)}, u32[]{:S(2)}) collective-permute-start(bf16[2,128,512]{2,1,0:T(8,128)(2,1)S(1)} %slice.8), channel_id=1, source_target_pairs={{0,16},{8,24},{16,0},{24,8},{1,17},{9,25},{17,1},{25,9},{2,18},{10... | collective-permute-start | bytes 786440 | tf_op jit(solution)/shard_map/ppermute | solution.py:20
  42.4 7.4 %collective-permute-start.20 = (bf16[4,128,512]{2,1,0:T(8,128)(2,1)S(1)}, bf16[4,128,512]{2,1,0:T(8,128)(2,1)S(1)}, u32[]{:S(2)}, u32[]{:S(2)}) collective-permute-start(bf16[4,128,512]{2,1,0:T(8,128)(2,1)S(1)} %pad_maximum_fusion.refs_0_), channel_id=1, source_target_pairs={{0,1},{1,0},{2,3},{3,2},{4,5},{5,4},{6,7},{7,6},{8,9},{9,8},{10,11... | collective-permute-start | bytes 1572872 | tf_op jit(solution)/shard_map/ppermute | solution.py:20
  42.4 7.4 %collective-permute-start.22 = (bf16[4,128,512]{2,1,0:T(8,128)(2,1)S(1)}, bf16[4,128,512]{2,1,0:T(8,128)(2,1)S(1)}, u32[]{:S(2)}, u32[]{:S(2)}) collective-permute-start(bf16[4,128,512]{2,1,0:T(8,128)(2,1)S(1)} %collective-permute-done.5.refs_2_), channel_id=1, source_target_pairs={{0,1},{1,0},{2,3},{3,2},{4,5},{5,4},{6,7},{7,6},{8,9},{9,8},{10,11... | collective-permute-start | bytes 1572872 | tf_op jit(solution)/shard_map/ppermute | solution.py:20
  42.9 6.9 %collective-permute-start.21 = (bf16[4,128,512]{2,1,0:T(8,128)(2,1)S(1)}, bf16[4,128,512]{2,1,0:T(8,128)(2,1)S(1)}, u32[]{:S(2)}, u32[]{:S(2)}) collective-permute-start(bf16[4,128,512]{2,1,0:T(8,128)(2,1)S(1)} %collective-permute-done.4.refs_1_), channel_id=1, source_target_pairs={{0,1},{1,0},{2,3},{3,2},{4,5},{5,4},{6,7},{7,6},{8,9},{9,8},{10,11... | collective-permute-start | bytes 1572872 | tf_op jit(solution)/shard_map/ppermute | solution.py:20
  49.2 1.5 %collective-permute-start.23 = (bf16[2,128,512]{2,1,0:T(8,128)(2,1)S(1)}, bf16[2,128,512]{2,1,0:T(8,128)(2,1)S(1)}, u32[]{:S(2)}, u32[]{:S(2)}) collective-permute-start(bf16[2,128,512]{2,1,0:T(8,128)(2,1)S(1)} %collective-permute-done.18.refs_3_), channel_id=1, source_target_pairs={{0,1},{1,0},{2,3},{3,2},{4,5},{5,4},{6,7},{7,6},{8,9},{9,8},{10,11... | collective-permute-start | bytes 786440 | tf_op jit(solution)/shard_map/ppermute | solution.py:20
  49.2 1.9 %collective-permute-start.24 = (bf16[2,128,512]{2,1,0:T(8,128)(2,1)S(1)}, bf16[2,128,512]{2,1,0:T(8,128)(2,1)S(1)}, u32[]{:S(2)}, u32[]{:S(2)}) collective-permute-start(bf16[2,128,512]{2,1,0:T(8,128)(2,1)S(1)} %collective-permute-done.19.refs_4_), channel_id=1, source_target_pairs={{0,1},{1,0},{2,3},{3,2},{4,5},{5,4},{6,7},{7,6},{8,9},{9,8},{10,11... | collective-permute-start | bytes 786440 | tf_op jit(solution)/shard_map/ppermute | solution.py:20
  52.5 1.4 %collective-permute-start.25 = (bf16[96,512]{1,0:T(8,128)(2,1)S(1)}, bf16[96,512]{1,0:T(8,128)(2,1)S(1)}, u32[]{:S(2)}, u32[]{:S(2)}) collective-permute-start(bf16[96,512]{1,0:T(8,128)(2,1)S(1)} %get-tuple-element.58), channel_id=1, source_target_pairs={{0,1},{1,0},{2,3},{3,2},{4,5},{5,4},{6,7},{7,6},{8,9},{9,8},{10,11... | collective-permute-start | bytes 294920 | tf_op jit(solution)/shard_map/ppermute | solution.py:20
  53.9 6.8 %collective-permute-start.28 = (bf16[96,512]{1,0:T(8,128)(2,1)S(1)}, bf16[96,512]{1,0:T(8,128)(2,1)S(1)}, u32[]{:S(2)}, u32[]{:S(2)}) collective-permute-start(bf16[96,512]{1,0:T(8,128)(2,1)S(1)} %add.29.refs_0_), channel_id=1, source_target_pairs={{0,6},{1,7},{2,4},{3,5},{4,2},{5,3},{6,0},{7,1},{8,14},{9,15},{10,... | collective-permute-start | bytes 294920 | tf_op jit(solution)/shard_map/ppermute | solution.py:20
  57.5 9.4 %collective-permute-start.27 = (bf16[96,512]{1,0:T(8,128)(2,1)S(1)}, bf16[96,512]{1,0:T(8,128)(2,1)S(1)}, u32[]{:S(2)}, u32[]{:S(2)}) collective-permute-start(bf16[96,512]{1,0:T(8,128)(2,1)S(1)} %add.29.refs_0_), channel_id=1, source_target_pairs={{0,4},{1,5},{2,6},{3,7},{4,0},{5,1},{6,2},{7,3},{8,12},{9,13},{10,... | collective-permute-start | bytes 294920 | tf_op jit(solution)/shard_map/ppermute | solution.py:20
  58.4 8.5 %collective-permute-start.26 = (bf16[96,512]{1,0:T(8,128)(2,1)S(1)}, bf16[96,512]{1,0:T(8,128)(2,1)S(1)}, u32[]{:S(2)}, u32[]{:S(2)}) collective-permute-start(bf16[96,512]{1,0:T(8,128)(2,1)S(1)} %add.29.refs_0_), channel_id=1, source_target_pairs={{0,2},{1,3},{2,0},{3,1},{4,6},{5,7},{6,4},{7,5},{8,10},{9,11},{10,... | collective-permute-start | bytes 294920 | tf_op jit(solution)/shard_map/ppermute | solution.py:20
  67.0 7.7 %collective-permute-start.30 = (bf16[96,512]{1,0:T(8,128)(2,1)S(1)}, bf16[96,512]{1,0:T(8,128)(2,1)S(1)}, u32[]{:S(2)}, u32[]{:S(2)}) collective-permute-start(bf16[96,512]{1,0:T(8,128)(2,1)S(1)} %add.30.after), channel_id=1, source_target_pairs={{0,24},{8,16},{1,25},{9,17},{2,26},{10,18},{3,27},{11,19},{4,28},{... | collective-permute-start | bytes 294920 | tf_op jit(solution)/shard_map/ppermute | solution.py:25
  69.3 5.3 %collective-permute-start.29 = (bf16[96,512]{1,0:T(8,128)(2,1)S(1)}, bf16[96,512]{1,0:T(8,128)(2,1)S(1)}, u32[]{:S(2)}, u32[]{:S(2)}) collective-permute-start(bf16[96,512]{1,0:T(8,128)(2,1)S(1)} %add.30.after), channel_id=1, source_target_pairs={{0,16},{8,24},{1,17},{9,25},{2,18},{10,26},{3,19},{11,27},{4,20},{... | collective-permute-start | bytes 294920 | tf_op jit(solution)/shard_map/ppermute | solution.py:25
  70.7 25.6 %copy-start.1 = (bf16[512,512]{1,0:T(8,128)(2,1)S(1)}, bf16[512,512]{1,0:T(8,128)(2,1)}, u32[]{:S(2)}) copy-start(bf16[512,512]{1,0:T(8,128)(2,1)} %param.11) | copy-start | bytes 1572868
  74.7 1.4 %collective-permute-start.31 = (bf16[96,512]{1,0:T(8,128)(2,1)S(1)}, bf16[96,512]{1,0:T(8,128)(2,1)S(1)}, u32[]{:S(2)}, u32[]{:S(2)}) collective-permute-start(bf16[96,512]{1,0:T(8,128)(2,1)S(1)} %add.31.refs_0_), channel_id=1, source_target_pairs={{0,1},{1,0},{2,3},{3,2},{4,5},{5,4},{6,7},{7,6},{8,9},{9,8},{10,11... | collective-permute-start | bytes 294920 | tf_op jit(solution)/shard_map/ppermute | solution.py:20
  77.1 1.4 %collective-permute-start.32 = (bf16[96,512]{1,0:T(8,128)(2,1)S(1)}, bf16[96,512]{1,0:T(8,128)(2,1)S(1)}, u32[]{:S(2)}, u32[]{:S(2)}) collective-permute-start(bf16[96,512]{1,0:T(8,128)(2,1)S(1)} %get-tuple-element.74), channel_id=1, source_target_pairs={{0,1},{1,0},{2,3},{3,2},{4,5},{5,4},{6,7},{7,6},{8,9},{9,8},{10,11... | collective-permute-start | bytes 294920 | tf_op jit(solution)/shard_map/ppermute | solution.py:20
  78.4 7.6 %collective-permute-start.35 = (bf16[96,512]{1,0:T(8,128)(2,1)S(1)}, bf16[96,512]{1,0:T(8,128)(2,1)S(1)}, u32[]{:S(2)}, u32[]{:S(2)}) collective-permute-start(bf16[96,512]{1,0:T(8,128)(2,1)S(1)} %add.32.refs_0_), channel_id=1, source_target_pairs={{0,6},{1,7},{2,4},{3,5},{4,2},{5,3},{6,0},{7,1},{8,14},{9,15},{10,... | collective-permute-start | bytes 294920 | tf_op jit(solution)/shard_map/ppermute | solution.py:20
  80.6 8.8 %collective-permute-start.34 = (bf16[96,512]{1,0:T(8,128)(2,1)S(1)}, bf16[96,512]{1,0:T(8,128)(2,1)S(1)}, u32[]{:S(2)}, u32[]{:S(2)}) collective-permute-start(bf16[96,512]{1,0:T(8,128)(2,1)S(1)} %add.32.refs_0_), channel_id=1, source_target_pairs={{0,4},{1,5},{2,6},{3,7},{4,0},{5,1},{6,2},{7,3},{8,12},{9,13},{10,... | collective-permute-start | bytes 294920 | tf_op jit(solution)/shard_map/ppermute | solution.py:20
  80.6 8.8 %collective-permute-start.33 = (bf16[96,512]{1,0:T(8,128)(2,1)S(1)}, bf16[96,512]{1,0:T(8,128)(2,1)S(1)}, u32[]{:S(2)}, u32[]{:S(2)}) collective-permute-start(bf16[96,512]{1,0:T(8,128)(2,1)S(1)} %add.32.refs_0_), channel_id=1, source_target_pairs={{0,2},{1,3},{2,0},{3,1},{4,6},{5,7},{6,4},{7,5},{8,10},{9,11},{10,... | collective-permute-start | bytes 294920 | tf_op jit(solution)/shard_map/ppermute | solution.py:20
  89.4 4.8 %collective-permute-start.36 = (bf16[96,512]{1,0:T(8,128)(2,1)S(1)}, bf16[96,512]{1,0:T(8,128)(2,1)S(1)}, u32[]{:S(2)}, u32[]{:S(2)}) collective-permute-start(bf16[96,512]{1,0:T(8,128)(2,1)S(1)} %choose.1.refs_0_), channel_id=1, source_target_pairs={{0,8},{8,0},{16,24},{24,16},{1,9},{9,1},{17,25},{25,17},{2,10},{10... | collective-permute-start | bytes 294920 | tf_op jit(solution)/shard_map/ppermute | solution.py:20
  94.2 1.4 %collective-permute-start.37 = (bf16[96,512]{1,0:T(8,128)(2,1)S(1)}, bf16[96,512]{1,0:T(8,128)(2,1)S(1)}, u32[]{:S(2)}, u32[]{:S(2)}) collective-permute-start(bf16[96,512]{1,0:T(8,128)(2,1)S(1)} %add.33.near), channel_id=1, source_target_pairs={{0,1},{1,0},{2,3},{3,2},{4,5},{5,4},{6,7},{7,6},{8,9},{9,8},{10,11... | collective-permute-start | bytes 294920 | tf_op jit(solution)/shard_map/ppermute | solution.py:20

commit v6 on v5

--- a/solution.py
+++ b/solution.py
@@ -374,7 +374,7 @@
     quarter = lax.dynamic_slice_in_dim(basis, home * part, part, 0)
     bands = [quarter] + [swap(quarter, "tensor", 2 * m) for m in range(1, chips)]
     blocks, gate = fetch_rows(tokens, embedding, gate_weight)
-    blocks, bands[2] = lax.optimization_barrier((blocks, bands[2]))
+    blocks, bands[3] = lax.optimization_barrier((blocks, bands[3]))
     bands = jnp.stack(bands)
     mask = GROUP
     while mask < segments:

time: 96.6 us -> 95.8 us (level)
  waiting for transfers between devices: 41 us -> 39.6 us
    ppermute x2, waiting for transfers between devices: 3.93 us -> 2.69 us  [onward(): lax.ppermute(value, 'segment', [(i, (i ^ flip) + 2) for i in range(size -...]
  transfers between devices with their start and end apart: 38 -> 38, of which waited for: 21 -> 20; matrix products, arithmetic and copies ran while one was open for 0% -> 0% of each run, Pallas kernels for 11% -> 12%
where the time goes in v6:
time: 95.8 us; the launch traced here: 95.5 us
  waiting for transfers between devices  39.6 us (41%)
  starting transfers between devices  39.3 us (41%)
  Pallas kernels  14.3 us (15%)
  local copies, waits for them, and re-layouts  1.95 us (2%)
    ppermute x36, waiting for transfers between devices, swap(): lax.ppermute(value, axis, [(i, i ^ mask) for i in range(lax.axis_size(axi...  36.9 us
    ppermute x36, starting transfers between devices, swap(): lax.ppermute(value, axis, [(i, i ^ mask) for i in range(lax.axis_size(axi...  34.6 us
    pallas_call x12, Pallas kernels, kernel_call(): pl.pallas_call(functools.partial(kernel, lax.axis_size('tensor') // 2), o...  8.98 us
    pallas_call x1, Pallas kernels, fetch_rows(): pl.pallas_call(functools.partial(fetch_kernel, block_rows, vocab), out_sh...  5.35 us
    ppermute x2, starting transfers between devices, onward(): lax.ppermute(value, 'segment', [(i, (i ^ flip) + 2) for i in range(size -...  4.64 us
    ppermute x2, waiting for transfers between devices, onward(): lax.ppermute(value, 'segment', [(i, (i ^ flip) + 2) for i in range(size -...  2.69 us
  transfers between devices with their start and end apart: 38, of which 20 were waited for; matrix products, arithmetic and copies ran while one was open for 0% of the time, Pallas kernels for 12%

profile of v6, /device:TPU:0, one launch (start us, length us, event | category | flops | bytes accessed | tf_op | source)
XLA Modules:
  0.0 95.5 jit_solution(13976344592867442902)
XLA Ops:
  0.0 1.0 %copy-done = bf16[512,512]{1,0:T(8,128)(2,1)S(1)} copy-done((bf16[512,512]{1,0:T(8,128)(2,1)S(1)}, bf16[512,512]{1,0:T(8,128)(2,1)}, u32[]{:S(2)}) %copy-start) | copy-done | bytes 524312
  1.1 5.1 %collective-permute-start = (bf16[128,512]{1,0:T(8,128)(2,1)S(1)}, bf16[128,512]{1,0:T(8,128)(2,1)S(1)}, u32[]{:S(2)}, u32[]{:S(2)}) collective-permute-start(bf16[128,512]{1,0:T(8,128)(2,1)S(1)} %constant_dynamic-slice_fusion), channel_id=1, source_target_pairs={{0,6},{1,7},{2,4},{3,5},{4,2},{5,3},{6,0},{7,1},{8,14},{9,15},{10,... | collective-permute-start | bytes 393224 | tf_op jit(solution)/shard_map/ppermute | solution.py:20
  6.2 0.6 collective-permute-start.3
  6.8 0.8 copy-done.3
  7.6 5.4 %fetch_rows.1 = (bf16[48,512]{1,0:T(8,128)(2,1)S(1)}, bf16[48,512]{1,0:T(8,128)(2,1)S(1)}, bf16[48,512]{1,0:T(8,128)(2,1)S(1)}, bf16[48,512]{1,0:T(8,128)(2,1)S(1)}, bf16[4096,896]{1,0:T(8,128)(2,1)S(1)}) custom-call(s32[192]{0:T(256)S(1)} %copy-done.3, s32[1,192]{1,0:T(1,128)S(1)} %bitcast.12, bf16[16032,512]{1,0:T(8,128)(2,1)} %table.1, ...), custom_call_target="tpu_custom_call" | custom-call | tf_op jit(solution)/shard_map/fetch_rows/pallas_call | solution.py:147
  13.0 0.0 collective-permute-done
  13.0 1.7 %collective-permute-start.1 = (bf16[48,512]{1,0:T(8,128)(2,1)S(1)}, bf16[48,512]{1,0:T(8,128)(2,1)S(1)}, u32[]{:S(2)}, u32[]{:S(2)}) collective-permute-start(bf16[48,512]{1,0:T(8,128)(2,1)S(1)} %get-tuple-element.44), channel_id=1, source_target_pairs={{0,8},{8,0},{16,24},{24,16},{1,9},{9,1},{17,25},{25,17},{2,10},{10... | collective-permute-start | bytes 147464 | tf_op jit(solution)/shard_map/ppermute | solution.py:20
  14.7 1.5 %collective-permute-start.6 = (bf16[48,512]{1,0:T(8,128)(2,1)S(1)}, bf16[48,512]{1,0:T(8,128)(2,1)S(1)}, u32[]{:S(2)}, u32[]{:S(2)}) collective-permute-start(bf16[48,512]{1,0:T(8,128)(2,1)S(1)} %get-tuple-element.49), channel_id=1, source_target_pairs={{0,16},{8,24},{16,0},{24,8},{1,17},{9,25},{17,1},{25,9},{2,18},{10... | collective-permute-start | bytes 147464 | tf_op jit(solution)/shard_map/ppermute | solution.py:20
  16.2 0.4 collective-permute-start.7
  16.6 0.0 collective-permute-done.2
  16.6 0.6 collective-permute-done.3
  17.2 0.1 pad_maximum_fusion.refs_0_
  17.3 1.6 %collective-permute-start.5 = (bf16[4,128,512]{2,1,0:T(8,128)(2,1)S(1)}, bf16[4,128,512]{2,1,0:T(8,128)(2,1)S(1)}, u32[]{:S(2)}, u32[]{:S(2)}) collective-permute-start(bf16[4,128,512]{2,1,0:T(8,128)(2,1)S(1)} %pad_maximum_fusion.refs_0_), channel_id=1, source_target_pairs={{0,16},{8,24},{16,0},{24,8},{1,17},{9,25},{17,1},{25,9},{2,18},{10... | collective-permute-start | bytes 1572872 | tf_op jit(solution)/shard_map/ppermute | solution.py:20
  18.9 1.5 %collective-permute-start.4 = (bf16[4,128,512]{2,1,0:T(8,128)(2,1)S(1)}, bf16[4,128,512]{2,1,0:T(8,128)(2,1)S(1)}, u32[]{:S(2)}, u32[]{:S(2)}) collective-permute-start(bf16[4,128,512]{2,1,0:T(8,128)(2,1)S(1)} %pad_maximum_fusion.refs_0_), channel_id=1, source_target_pairs={{0,8},{8,0},{16,24},{24,16},{1,9},{9,1},{17,25},{25,17},{2,10},{10... | collective-permute-start | bytes 1572872 | tf_op jit(solution)/shard_map/ppermute | solution.py:20
  20.4 0.0 collective-permute-done.6
  20.4 1.3 %collective-permute-done.7 = bf16[48,512]{1,0:T(8,128)(2,1)S(1)} collective-permute-done((bf16[48,512]{1,0:T(8,128)(2,1)S(1)}, bf16[48,512]{1,0:T(8,128)(2,1)S(1)}, u32[]{:S(2)}, u32[]{:S(2)}) %collective-permute-start.7) | collective-permute-done | bytes 49184 | tf_op jit(solution)/shard_map/ppermute | solution.py:20
  21.7 3.8 %collective-permute-start.10 = (bf16[48,512]{1,0:T(8,128)(2,1)S(1)}, bf16[48,512]{1,0:T(8,128)(2,1)S(1)}, u32[]{:S(2)}, u32[]{:S(2)}) collective-permute-start(bf16[48,512]{1,0:T(8,128)(2,1)S(1)} %add_add_fusion), channel_id=1, source_target_pairs={{0,6},{1,7},{2,4},{3,5},{4,2},{5,3},{6,0},{7,1},{8,14},{9,15},{10,... | collective-permute-start | bytes 147464 | tf_op jit(solution)/shard_map/ppermute | solution.py:20
  25.5 0.0 collective-permute-start.9
  25.5 0.6 collective-permute-start.8
  26.1 1.6 %collective-permute-done.10 = bf16[48,512]{1,0:T(8,128)(2,1)S(1)} collective-permute-done((bf16[48,512]{1,0:T(8,128)(2,1)S(1)}, bf16[48,512]{1,0:T(8,128)(2,1)S(1)}, u32[]{:S(2)}, u32[]{:S(2)}) %collective-permute-start.10) | collective-permute-done | bytes 49184 | tf_op jit(solution)/shard_map/ppermute | solution.py:20
  27.8 2.7 %collective-permute-done.9 = bf16[48,512]{1,0:T(8,128)(2,1)S(1)} collective-permute-done((bf16[48,512]{1,0:T(8,128)(2,1)S(1)}, bf16[48,512]{1,0:T(8,128)(2,1)S(1)}, u32[]{:S(2)}, u32[]{:S(2)}) %collective-permute-start.9) | collective-permute-done | bytes 49184 | tf_op jit(solution)/shard_map/ppermute | solution.py:20
  30.5 0.1 collective-permute-start.13
  30.6 1.7 %collective-permute-start.12 = (bf16[4,48,512]{2,1,0:T(8,128)(2,1)S(1)}, bf16[4,48,512]{2,1,0:T(8,128)(2,1)S(1)}, u32[]{:S(2)}, u32[]{:S(2)}) collective-permute-start(bf16[4,48,512]{2,1,0:T(8,128)(2,1)S(1)} %pad_maximum_fusion.1.refs_0_), channel_id=1, source_target_pairs={{0,16},{8,24},{16,0},{24,8},{1,17},{9,25},{17,1},{25,9},{2,18},{10... | collective-permute-start | bytes 589832 | tf_op jit(solution)/shard_map/ppermute | solution.py:20
  32.4 1.7 %collective-permute-start.11 = (bf16[4,48,512]{2,1,0:T(8,128)(2,1)S(1)}, bf16[4,48,512]{2,1,0:T(8,128)(2,1)S(1)}, u32[]{:S(2)}, u32[]{:S(2)}) collective-permute-start(bf16[4,48,512]{2,1,0:T(8,128)(2,1)S(1)} %pad_maximum_fusion.1.refs_0_), channel_id=1, source_target_pairs={{0,8},{8,0},{16,24},{24,16},{1,9},{9,1},{17,25},{25,17},{2,10},{10... | collective-permute-start | bytes 589832 | tf_op jit(solution)/shard_map/ppermute | solution.py:20
  34.1 4.4 %collective-permute-done.13.refs_3_ = bf16[4,48,512]{2,1,0:T(8,128)(2,1)S(1)} collective-permute-done((bf16[4,48,512]{2,1,0:T(8,128)(2,1)S(1)}, bf16[4,48,512]{2,1,0:T(8,128)(2,1)S(1)}, u32[]{:S(2)}, u32[]{:S(2)}) %collective-permute-start.13) | collective-permute-done | bytes 196640 | tf_op jit(solution)/shard_map/ppermute | solution.py:20
  38.5 1.0 %collective-permute-done.12.refs_2_ = bf16[4,48,512]{2,1,0:T(8,128)(2,1)S(1)} collective-permute-done((bf16[4,48,512]{2,1,0:T(8,128)(2,1)S(1)}, bf16[4,48,512]{2,1,0:T(8,128)(2,1)S(1)}, u32[]{:S(2)}, u32[]{:S(2)}) %collective-permute-start.12) | collective-permute-done | bytes 196640 | tf_op jit(solution)/shard_map/ppermute | solution.py:20
  39.5 0.5 collective-permute-done.11.refs_1_
  40.0 0.0 collective-permute-start.15
  40.1 0.5 collective-permute-start.17
  40.6 1.6 %collective-permute-start.19 = (bf16[2,128,512]{2,1,0:T(8,128)(2,1)S(1)}, bf16[2,128,512]{2,1,0:T(8,128)(2,1)S(1)}, u32[]{:S(2)}, u32[]{:S(2)}) collective-permute-start(bf16[2,128,512]{2,1,0:T(8,128)(2,1)S(1)} %slice.9), channel_id=1, source_target_pairs={{0,8},{8,0},{16,24},{24,16},{1,9},{9,1},{17,25},{25,17},{2,10},{10... | collective-permute-start | bytes 786440 | tf_op jit(solution)/shard_map/ppermute | solution.py:20
  42.2 0.6 collective-permute-start.18
  42.8 0.5 collective-permute-start.22
  43.3 0.1 collective-permute-start.21
  43.3 5.7 %section_first.1 = (bf16[192,4096]{1,0:T(8,128)(2,1)S(1)}, bf16[192,4096]{1,0:T(8,128)(2,1)S(1)}, f32[192,896]{1,0:T(8,128)S(1)}, f32[192,1]{1,0:T(8,128)S(1)}, bf16[896,4096]{1,0:T(8,128)(2,1)S(1)}) custom-call(bf16[4,48,512]{2,1,0:T(8,128)(2,1)S(1)} %pad_maximum_fusion.1.refs_0_, bf16[4,48,512]{2,1,0:T(8,128)(2,1)S(1)} %collective-permute-done.11.refs_1_, ...), custom_call_target="tpu_custom_call" | custom-call | tf_op jit(solution)/shard_map/section_first/pallas_call | solution.py:334
  49.1 1.1 %collective-permute-done.18.refs_3_ = bf16[2,128,512]{2,1,0:T(8,128)(2,1)S(1)} collective-permute-done((bf16[2,128,512]{2,1,0:T(8,128)(2,1)S(1)}, bf16[2,128,512]{2,1,0:T(8,128)(2,1)S(1)}, u32[]{:S(2)}, u32[]{:S(2)}) %collective-permute-start.18) | collective-permute-done | bytes 262176 | tf_op jit(solution)/shard_map/ppermute | solution.py:20
  50.2 0.5 collective-permute-start.24
  50.8 1.0 %collective-permute-done.23.refs_8_ = bf16[2,128,512]{2,1,0:T(8,128)(2,1)S(1)} collective-permute-done((bf16[2,128,512]{2,1,0:T(8,128)(2,1)S(1)}, bf16[2,128,512]{2,1,0:T(8,128)(2,1)S(1)}, u32[]{:S(2)}, u32[]{:S(2)}) %collective-permute-start.23) | collective-permute-done | bytes 262176 | tf_op jit(solution)/shard_map/ppermute | solution.py:20
  51.8 0.4 collective-permute-done.24.refs_9_
  52.1 1.3 %project_first.1 = (bf16[96,512]{1,0:T(8,128)(2,1)S(1)}, bf16[96,512]{1,0:T(8,128)(2,1)S(1)}, bf16[4096,512]{1,0:T(8,128)(2,1)S(1)}) custom-call(bf16[4,128,512]{2,1,0:T(8,128)(2,1)S(1)} %pad_maximum_fusion.refs_0_, bf16[4,128,512]{2,1,0:T(8,128)(2,1)S(1)} %collective-permute-done.4.refs_1_, bf16[4,128,512]{2,1,0:T(8,128)(2,1)S(1)} %collective-permute-done.5.refs_2_, ...), custom_call_target="tpu_custom_call" | custom-call | flops 805306368 | tf_op jit(solution)/shard_map/project_first/pallas_call | solution.py:334
  53.5 0.2 collective-permute-start.25
  53.7 1.2 %collective-permute-done.25.refs_1_ = bf16[96,512]{1,0:T(8,128)(2,1)S(1)} collective-permute-done((bf16[96,512]{1,0:T(8,128)(2,1)S(1)}, bf16[96,512]{1,0:T(8,128)(2,1)S(1)}, u32[]{:S(2)}, u32[]{:S(2)}) %collective-permute-start.25) | collective-permute-done | bytes 98336 | tf_op jit(solution)/shard_map/ppermute | solution.py:20
  54.9 2.7 %collective-permute-start.28 = (bf16[96,512]{1,0:T(8,128)(2,1)S(1)}, bf16[96,512]{1,0:T(8,128)(2,1)S(1)}, u32[]{:S(2)}, u32[]{:S(2)}) collective-permute-start(bf16[96,512]{1,0:T(8,128)(2,1)S(1)} %add.29.refs_0_), channel_id=1, source_target_pairs={{0,6},{1,7},{2,4},{3,5},{4,2},{5,3},{6,0},{7,1},{8,14},{9,15},{10,... | collective-permute-start | bytes 294920 | tf_op jit(solution)/shard_map/ppermute | solution.py:20
  57.5 1.8 %collective-permute-start.26 = (bf16[96,512]{1,0:T(8,128)(2,1)S(1)}, bf16[96,512]{1,0:T(8,128)(2,1)S(1)}, u32[]{:S(2)}, u32[]{:S(2)}) collective-permute-start(bf16[96,512]{1,0:T(8,128)(2,1)S(1)} %add.29.refs_0_), channel_id=1, source_target_pairs={{0,2},{1,3},{2,0},{3,1},{4,6},{5,7},{6,4},{7,5},{8,10},{9,11},{10,... | collective-permute-start | bytes 294920 | tf_op jit(solution)/shard_map/ppermute | solution.py:20
  59.3 3.1 %collective-permute-done.28.refs_3_ = bf16[96,512]{1,0:T(8,128)(2,1)S(1)} collective-permute-done((bf16[96,512]{1,0:T(8,128)(2,1)S(1)}, bf16[96,512]{1,0:T(8,128)(2,1)S(1)}, u32[]{:S(2)}, u32[]{:S(2)}) %collective-permute-start.28) | collective-permute-done | bytes 98336 | tf_op jit(solution)/shard_map/ppermute | solution.py:20
  62.5 3.3 %collective-permute-done.27.refs_2_ = bf16[96,512]{1,0:T(8,128)(2,1)S(1)} collective-permute-done((bf16[96,512]{1,0:T(8,128)(2,1)S(1)}, bf16[96,512]{1,0:T(8,128)(2,1)S(1)}, u32[]{:S(2)}, u32[]{:S(2)}) %collective-permute-start.27) | collective-permute-done | bytes 98336 | tf_op jit(solution)/shard_map/ppermute | solution.py:20
  65.8 0.1 add.30.after
  65.9 3.3 %collective-permute-start.30 = (bf16[96,512]{1,0:T(8,128)(2,1)S(1)}, bf16[96,512]{1,0:T(8,128)(2,1)S(1)}, u32[]{:S(2)}, u32[]{:S(2)}) collective-permute-start(bf16[96,512]{1,0:T(8,128)(2,1)S(1)} %add.30.after), channel_id=1, source_target_pairs={{0,24},{8,16},{1,25},{9,17},{2,26},{10,18},{3,27},{11,19},{4,28},{... | collective-permute-start | bytes 294920 | tf_op jit(solution)/shard_map/ppermute | solution.py:25
  69.2 1.3 %collective-permute-start.29 = (bf16[96,512]{1,0:T(8,128)(2,1)S(1)}, bf16[96,512]{1,0:T(8,128)(2,1)S(1)}, u32[]{:S(2)}, u32[]{:S(2)}) collective-permute-start(bf16[96,512]{1,0:T(8,128)(2,1)S(1)} %add.30.after), channel_id=1, source_target_pairs={{0,16},{8,24},{1,17},{9,25},{2,18},{10,26},{3,19},{11,27},{4,20},{... | collective-permute-start | bytes 294920 | tf_op jit(solution)/shard_map/ppermute | solution.py:25
  70.5 0.0 copy-start.1
  70.5 2.7 %collective-permute-done.29.refs_0_ = bf16[96,512]{1,0:T(8,128)(2,1)S(1)} collective-permute-done((bf16[96,512]{1,0:T(8,128)(2,1)S(1)}, bf16[96,512]{1,0:T(8,128)(2,1)S(1)}, u32[]{:S(2)}, u32[]{:S(2)}) %collective-permute-start.29) | collective-permute-done | bytes 98336 | tf_op jit(solution)/shard_map/ppermute | solution.py:25
  73.3 0.1 collective-permute-start.31
  73.3 1.3 %collective-permute-done.31.refs_1_ = bf16[96,512]{1,0:T(8,128)(2,1)S(1)} collective-permute-done((bf16[96,512]{1,0:T(8,128)(2,1)S(1)}, bf16[96,512]{1,0:T(8,128)(2,1)S(1)}, u32[]{:S(2)}, u32[]{:S(2)}) %collective-permute-start.31) | collective-permute-done | bytes 98336 | tf_op jit(solution)/shard_map/ppermute | solution.py:20
  74.6 1.1 %section_next.1 = (bf16[96,512]{1,0:T(8,128)(2,1)S(1)}, bf16[96,512]{1,0:T(8,128)(2,1)S(1)}) custom-call(bf16[96,512]{1,0:T(8,128)(2,1)S(1)} %add.31.refs_0_, bf16[96,512]{1,0:T(8,128)(2,1)S(1)} %collective-permute-done.31.refs_1_, f32[192,896]{1,0:T(8,128)S(1)} %get-tuple-element.66.refs_2_, f32[192,1]{1,0:T(8,128)S(1)} %get-tuple-element.67.refs_3_, ...), custom_call_target="tpu_custom_call" | custom-call | flops 553648128 | tf_op jit(solution)/shard_map/section_next/pallas_call | solution.py:334
  75.7 0.2 collective-permute-start.32
  75.9 1.2 %collective-permute-done.32.refs_1_ = bf16[96,512]{1,0:T(8,128)(2,1)S(1)} collective-permute-done((bf16[96,512]{1,0:T(8,128)(2,1)S(1)}, bf16[96,512]{1,0:T(8,128)(2,1)S(1)}, u32[]{:S(2)}, u32[]{:S(2)}) %collective-permute-start.32) | collective-permute-done | bytes 98336 | tf_op jit(solution)/shard_map/ppermute | solution.py:20
  77.1 3.1 %collective-permute-start.35 = (bf16[96,512]{1,0:T(8,128)(2,1)S(1)}, bf16[96,512]{1,0:T(8,128)(2,1)S(1)}, u32[]{:S(2)}, u32[]{:S(2)}) collective-permute-start(bf16[96,512]{1,0:T(8,128)(2,1)S(1)} %add.32.refs_0_), channel_id=1, source_target_pairs={{0,6},{1,7},{2,4},{3,5},{4,2},{5,3},{6,0},{7,1},{8,14},{9,15},{10,... | collective-permute-start | bytes 294920 | tf_op jit(solution)/shard_map/ppermute | solution.py:20
  80.2 1.3 %collective-permute-start.33 = (bf16[96,512]{1,0:T(8,128)(2,1)S(1)}, bf16[96,512]{1,0:T(8,128)(2,1)S(1)}, u32[]{:S(2)}, u32[]{:S(2)}) collective-permute-start(bf16[96,512]{1,0:T(8,128)(2,1)S(1)} %add.32.refs_0_), channel_id=1, source_target_pairs={{0,2},{1,3},{2,0},{3,1},{4,6},{5,7},{6,4},{7,5},{8,10},{9,11},{10,... | collective-permute-start | bytes 294920 | tf_op jit(solution)/shard_map/ppermute | solution.py:20
  81.5 3.1 %collective-permute-done.35.refs_3_ = bf16[96,512]{1,0:T(8,128)(2,1)S(1)} collective-permute-done((bf16[96,512]{1,0:T(8,128)(2,1)S(1)}, bf16[96,512]{1,0:T(8,128)(2,1)S(1)}, u32[]{:S(2)}, u32[]{:S(2)}) %collective-permute-start.35) | collective-permute-done | bytes 98336 | tf_op jit(solution)/shard_map/ppermute | solution.py:20
  84.7 4.0 %collective-permute-done.34.refs_2_ = bf16[96,512]{1,0:T(8,128)(2,1)S(1)} collective-permute-done((bf16[96,512]{1,0:T(8,128)(2,1)S(1)}, bf16[96,512]{1,0:T(8,128)(2,1)S(1)}, u32[]{:S(2)}, u32[]{:S(2)}) %collective-permute-start.34) | collective-permute-done | bytes 98336 | tf_op jit(solution)/shard_map/ppermute | solution.py:20
  88.7 1.1 %collective-permute-start.36 = (bf16[96,512]{1,0:T(8,128)(2,1)S(1)}, bf16[96,512]{1,0:T(8,128)(2,1)S(1)}, u32[]{:S(2)}, u32[]{:S(2)}) collective-permute-start(bf16[96,512]{1,0:T(8,128)(2,1)S(1)} %choose.1.refs_0_), channel_id=1, source_target_pairs={{0,8},{8,0},{16,24},{24,16},{1,9},{9,1},{17,25},{25,17},{2,10},{10... | collective-permute-start | bytes 294920 | tf_op jit(solution)/shard_map/ppermute | solution.py:20
  89.8 3.6 %collective-permute-done.36.refs_1_ = bf16[96,512]{1,0:T(8,128)(2,1)S(1)} collective-permute-done((bf16[96,512]{1,0:T(8,128)(2,1)S(1)}, bf16[96,512]{1,0:T(8,128)(2,1)S(1)}, u32[]{:S(2)}, u32[]{:S(2)}) %collective-permute-start.36) | collective-permute-done | bytes 98336 | tf_op jit(solution)/shard_map/ppermute | solution.py:20
  93.5 0.1 collective-permute-start.37
  93.5 1.3 %collective-permute-done.37.far = bf16[96,512]{1,0:T(8,128)(2,1)S(1)} collective-permute-done((bf16[96,512]{1,0:T(8,128)(2,1)S(1)}, bf16[96,512]{1,0:T(8,128)(2,1)S(1)}, u32[]{:S(2)}, u32[]{:S(2)}) %collective-permute-start.37) | collective-permute-done | bytes 98336 | tf_op jit(solution)/shard_map/ppermute | solution.py:20
  94.8 0.7 collect.1
  (45 shorter events, 0.3 us)
Async XLA Ops:
  0.0 1.0 %copy-start = (bf16[512,512]{1,0:T(8,128)(2,1)S(1)}, bf16[512,512]{1,0:T(8,128)(2,1)}, u32[]{:S(2)}) copy-start(bf16[512,512]{1,0:T(8,128)(2,1)} %param.11) | copy-start | bytes 1572868
  1.1 12.0 %collective-permute-start = (bf16[128,512]{1,0:T(8,128)(2,1)S(1)}, bf16[128,512]{1,0:T(8,128)(2,1)S(1)}, u32[]{:S(2)}, u32[]{:S(2)}) collective-permute-start(bf16[128,512]{1,0:T(8,128)(2,1)S(1)} %constant_dynamic-slice_fusion), channel_id=1, source_target_pairs={{0,6},{1,7},{2,4},{3,5},{4,2},{5,3},{6,0},{7,1},{8,14},{9,15},{10,... | collective-permute-start | bytes 393224 | tf_op jit(solution)/shard_map/ppermute | solution.py:20
  6.2 10.4 %collective-permute-start.2 = (bf16[128,512]{1,0:T(8,128)(2,1)S(1)}, bf16[128,512]{1,0:T(8,128)(2,1)S(1)}, u32[]{:S(2)}, u32[]{:S(2)}) collective-permute-start(bf16[128,512]{1,0:T(8,128)(2,1)S(1)} %constant_dynamic-slice_fusion), channel_id=1, source_target_pairs={{0,2},{1,3},{2,0},{3,1},{4,6},{5,7},{6,4},{7,5},{8,10},{9,11},{10,... | collective-permute-start | bytes 393224 | tf_op jit(solution)/shard_map/ppermute | solution.py:20
  6.2 11.1 %collective-permute-start.3 = (bf16[128,512]{1,0:T(8,128)(2,1)S(1)}, bf16[128,512]{1,0:T(8,128)(2,1)S(1)}, u32[]{:S(2)}, u32[]{:S(2)}) collective-permute-start(bf16[128,512]{1,0:T(8,128)(2,1)S(1)} %constant_dynamic-slice_fusion), channel_id=1, source_target_pairs={{0,4},{1,5},{2,6},{3,7},{4,0},{5,1},{6,2},{7,3},{8,12},{9,13},{10,... | collective-permute-start | bytes 393224 | tf_op jit(solution)/shard_map/ppermute | solution.py:20
  6.8 36.5 %slice-start = ((s8[7340032]{0:T(1024)(128)(4,1)}), s8[4194304]{0:T(1024)(128)(4,1)S(1)}, s32[]{:S(2)}) async-start(s8[7340032]{0:T(1024)(128)(4,1)} %bitcast.10), calls=%async_computation | async-start | bytes 8388608
  6.8 0.8 copy-start.3
  7.6 35.7 %slice-start.1 = ((s8[7340032]{0:T(1024)(128)(4,1)}), s8[3145728]{0:T(1024)(128)(4,1)S(1)}, s32[]{:S(2)}) async-start(s8[7340032]{0:T(1024)(128)(4,1)} %bitcast.10), calls=%async_computation.1 | async-start | bytes 6291456
  7.6 35.7 %copy-start.2 = (f32[2,4096]{1,0:T(2,128)S(1)}, f32[2,4096]{1,0:T(2,128)}, u32[]{:S(2)}) copy-start(f32[2,4096]{1,0:T(2,128)} %refs_2_.1) | copy-start | bytes 98308
  13.0 4.3 %collective-permute-start.1 = (bf16[48,512]{1,0:T(8,128)(2,1)S(1)}, bf16[48,512]{1,0:T(8,128)(2,1)S(1)}, u32[]{:S(2)}, u32[]{:S(2)}) collective-permute-start(bf16[48,512]{1,0:T(8,128)(2,1)S(1)} %get-tuple-element.44), channel_id=1, source_target_pairs={{0,8},{8,0},{16,24},{24,16},{1,9},{9,1},{17,25},{25,17},{2,10},{10... | collective-permute-start | bytes 147464 | tf_op jit(solution)/shard_map/ppermute | solution.py:20
  14.7 5.7 %collective-permute-start.6 = (bf16[48,512]{1,0:T(8,128)(2,1)S(1)}, bf16[48,512]{1,0:T(8,128)(2,1)S(1)}, u32[]{:S(2)}, u32[]{:S(2)}) collective-permute-start(bf16[48,512]{1,0:T(8,128)(2,1)S(1)} %get-tuple-element.49), channel_id=1, source_target_pairs={{0,16},{8,24},{16,0},{24,8},{1,17},{9,25},{17,1},{25,9},{2,18},{10... | collective-permute-start | bytes 147464 | tf_op jit(solution)/shard_map/ppermute | solution.py:20
  16.2 5.4 %collective-permute-start.7 = (bf16[48,512]{1,0:T(8,128)(2,1)S(1)}, bf16[48,512]{1,0:T(8,128)(2,1)S(1)}, u32[]{:S(2)}, u32[]{:S(2)}) collective-permute-start(bf16[48,512]{1,0:T(8,128)(2,1)S(1)} %get-tuple-element.50), channel_id=1, source_target_pairs={{0,24},{8,16},{16,8},{24,0},{1,25},{9,17},{17,9},{25,1},{2,26},{10... | collective-permute-start | bytes 147464 | tf_op jit(solution)/shard_map/ppermute | solution.py:20
  17.3 22.7 %collective-permute-start.5 = (bf16[4,128,512]{2,1,0:T(8,128)(2,1)S(1)}, bf16[4,128,512]{2,1,0:T(8,128)(2,1)S(1)}, u32[]{:S(2)}, u32[]{:S(2)}) collective-permute-start(bf16[4,128,512]{2,1,0:T(8,128)(2,1)S(1)} %pad_maximum_fusion.refs_0_), channel_id=1, source_target_pairs={{0,16},{8,24},{16,0},{24,8},{1,17},{9,25},{17,1},{25,9},{2,18},{10... | collective-permute-start | bytes 1572872 | tf_op jit(solution)/shard_map/ppermute | solution.py:20
  18.9 21.1 %collective-permute-start.4 = (bf16[4,128,512]{2,1,0:T(8,128)(2,1)S(1)}, bf16[4,128,512]{2,1,0:T(8,128)(2,1)S(1)}, u32[]{:S(2)}, u32[]{:S(2)}) collective-permute-start(bf16[4,128,512]{2,1,0:T(8,128)(2,1)S(1)} %pad_maximum_fusion.refs_0_), channel_id=1, source_target_pairs={{0,8},{8,0},{16,24},{24,16},{1,9},{9,1},{17,25},{25,17},{2,10},{10... | collective-permute-start | bytes 1572872 | tf_op jit(solution)/shard_map/ppermute | solution.py:20
  21.7 6.1 %collective-permute-start.10 = (bf16[48,512]{1,0:T(8,128)(2,1)S(1)}, bf16[48,512]{1,0:T(8,128)(2,1)S(1)}, u32[]{:S(2)}, u32[]{:S(2)}) collective-permute-start(bf16[48,512]{1,0:T(8,128)(2,1)S(1)} %add_add_fusion), channel_id=1, source_target_pairs={{0,6},{1,7},{2,4},{3,5},{4,2},{5,3},{6,0},{7,1},{8,14},{9,15},{10,... | collective-permute-start | bytes 147464 | tf_op jit(solution)/shard_map/ppermute | solution.py:20
  25.5 5.0 %collective-permute-start.9 = (bf16[48,512]{1,0:T(8,128)(2,1)S(1)}, bf16[48,512]{1,0:T(8,128)(2,1)S(1)}, u32[]{:S(2)}, u32[]{:S(2)}) collective-permute-start(bf16[48,512]{1,0:T(8,128)(2,1)S(1)} %add_add_fusion), channel_id=1, source_target_pairs={{0,4},{1,5},{2,6},{3,7},{4,0},{5,1},{6,2},{7,3},{8,12},{9,13},{10,... | collective-permute-start | bytes 147464 | tf_op jit(solution)/shard_map/ppermute | solution.py:20
  25.5 5.0 %collective-permute-start.8 = (bf16[48,512]{1,0:T(8,128)(2,1)S(1)}, bf16[48,512]{1,0:T(8,128)(2,1)S(1)}, u32[]{:S(2)}, u32[]{:S(2)}) collective-permute-start(bf16[48,512]{1,0:T(8,128)(2,1)S(1)} %add_add_fusion), channel_id=1, source_target_pairs={{0,2},{1,3},{2,0},{3,1},{4,6},{5,7},{6,4},{7,5},{8,10},{9,11},{10,... | collective-permute-start | bytes 147464 | tf_op jit(solution)/shard_map/ppermute | solution.py:20
  30.5 8.0 %collective-permute-start.13 = (bf16[4,48,512]{2,1,0:T(8,128)(2,1)S(1)}, bf16[4,48,512]{2,1,0:T(8,128)(2,1)S(1)}, u32[]{:S(2)}, u32[]{:S(2)}) collective-permute-start(bf16[4,48,512]{2,1,0:T(8,128)(2,1)S(1)} %pad_maximum_fusion.1.refs_0_), channel_id=1, source_target_pairs={{0,24},{8,16},{16,8},{24,0},{1,25},{9,17},{17,9},{25,1},{2,26},{10... | collective-permute-start | bytes 589832 | tf_op jit(solution)/shard_map/ppermute | solution.py:20
  30.6 8.9 %collective-permute-start.12 = (bf16[4,48,512]{2,1,0:T(8,128)(2,1)S(1)}, bf16[4,48,512]{2,1,0:T(8,128)(2,1)S(1)}, u32[]{:S(2)}, u32[]{:S(2)}) collective-permute-start(bf16[4,48,512]{2,1,0:T(8,128)(2,1)S(1)} %pad_maximum_fusion.1.refs_0_), channel_id=1, source_target_pairs={{0,16},{8,24},{16,0},{24,8},{1,17},{9,25},{17,1},{25,9},{2,18},{10... | collective-permute-start | bytes 589832 | tf_op jit(solution)/shard_map/ppermute | solution.py:20
  32.4 7.7 %collective-permute-start.11 = (bf16[4,48,512]{2,1,0:T(8,128)(2,1)S(1)}, bf16[4,48,512]{2,1,0:T(8,128)(2,1)S(1)}, u32[]{:S(2)}, u32[]{:S(2)}) collective-permute-start(bf16[4,48,512]{2,1,0:T(8,128)(2,1)S(1)} %pad_maximum_fusion.1.refs_0_), channel_id=1, source_target_pairs={{0,8},{8,0},{16,24},{24,16},{1,9},{9,1},{17,25},{25,17},{2,10},{10... | collective-permute-start | bytes 589832 | tf_op jit(solution)/shard_map/ppermute | solution.py:20
  38.5 3.6 %collective-permute-start.14 = (bf16[4,48,512]{2,1,0:T(8,128)(2,1)S(1)}, bf16[4,48,512]{2,1,0:T(8,128)(2,1)S(1)}, u32[]{:S(2)}, u32[]{:S(2)}) collective-permute-start(bf16[4,48,512]{2,1,0:T(8,128)(2,1)S(1)} %pad_maximum_fusion.1.refs_0_), channel_id=1, source_target_pairs={{0,1},{1,0},{2,3},{3,2},{4,5},{5,4},{6,7},{7,6},{8,9},{9,8},{10,11... | collective-permute-start | bytes 589832 | tf_op jit(solution)/shard_map/ppermute | solution.py:20
  39.5 3.2 %collective-permute-start.16 = (bf16[4,48,512]{2,1,0:T(8,128)(2,1)S(1)}, bf16[4,48,512]{2,1,0:T(8,128)(2,1)S(1)}, u32[]{:S(2)}, u32[]{:S(2)}) collective-permute-start(bf16[4,48,512]{2,1,0:T(8,128)(2,1)S(1)} %collective-permute-done.12.refs_2_), channel_id=1, source_target_pairs={{0,1},{1,0},{2,3},{3,2},{4,5},{5,4},{6,7},{7,6},{8,9},{9,8},{10,11... | collective-permute-start | bytes 589832 | tf_op jit(solution)/shard_map/ppermute | solution.py:20
  40.0 2.7 %collective-permute-start.15 = (bf16[4,48,512]{2,1,0:T(8,128)(2,1)S(1)}, bf16[4,48,512]{2,1,0:T(8,128)(2,1)S(1)}, u32[]{:S(2)}, u32[]{:S(2)}) collective-permute-start(bf16[4,48,512]{2,1,0:T(8,128)(2,1)S(1)} %collective-permute-done.11.refs_1_), channel_id=1, source_target_pairs={{0,1},{1,0},{2,3},{3,2},{4,5},{5,4},{6,7},{7,6},{8,9},{9,8},{10,11... | collective-permute-start | bytes 589832 | tf_op jit(solution)/shard_map/ppermute | solution.py:20
  40.1 3.2 %collective-permute-start.17 = (bf16[4,48,512]{2,1,0:T(8,128)(2,1)S(1)}, bf16[4,48,512]{2,1,0:T(8,128)(2,1)S(1)}, u32[]{:S(2)}, u32[]{:S(2)}) collective-permute-start(bf16[4,48,512]{2,1,0:T(8,128)(2,1)S(1)} %collective-permute-done.13.refs_3_), channel_id=1, source_target_pairs={{0,1},{1,0},{2,3},{3,2},{4,5},{5,4},{6,7},{7,6},{8,9},{9,8},{10,11... | collective-permute-start | bytes 589832 | tf_op jit(solution)/shard_map/ppermute | solution.py:20
  40.6 8.5 %collective-permute-start.19 = (bf16[2,128,512]{2,1,0:T(8,128)(2,1)S(1)}, bf16[2,128,512]{2,1,0:T(8,128)(2,1)S(1)}, u32[]{:S(2)}, u32[]{:S(2)}) collective-permute-start(bf16[2,128,512]{2,1,0:T(8,128)(2,1)S(1)} %slice.9), channel_id=1, source_target_pairs={{0,8},{8,0},{16,24},{24,16},{1,9},{9,1},{17,25},{25,17},{2,10},{10... | collective-permute-start | bytes 786440 | tf_op jit(solution)/shard_map/ppermute | solution.py:20
  42.2 8.1 %collective-permute-start.18 = (bf16[2,128,512]{2,1,0:T(8,128)(2,1)S(1)}, bf16[2,128,512]{2,1,0:T(8,128)(2,1)S(1)}, u32[]{:S(2)}, u32[]{:S(2)}) collective-permute-start(bf16[2,128,512]{2,1,0:T(8,128)(2,1)S(1)} %slice.8), channel_id=1, source_target_pairs={{0,16},{8,24},{16,0},{24,8},{1,17},{9,25},{17,1},{25,9},{2,18},{10... | collective-permute-start | bytes 786440 | tf_op jit(solution)/shard_map/ppermute | solution.py:20
  42.7 8.0 %collective-permute-start.20 = (bf16[4,128,512]{2,1,0:T(8,128)(2,1)S(1)}, bf16[4,128,512]{2,1,0:T(8,128)(2,1)S(1)}, u32[]{:S(2)}, u32[]{:S(2)}) collective-permute-start(bf16[4,128,512]{2,1,0:T(8,128)(2,1)S(1)} %pad_maximum_fusion.refs_0_), channel_id=1, source_target_pairs={{0,1},{1,0},{2,3},{3,2},{4,5},{5,4},{6,7},{7,6},{8,9},{9,8},{10,11... | collective-permute-start | bytes 1572872 | tf_op jit(solution)/shard_map/ppermute | solution.py:20
  42.8 8.0 %collective-permute-start.22 = (bf16[4,128,512]{2,1,0:T(8,128)(2,1)S(1)}, bf16[4,128,512]{2,1,0:T(8,128)(2,1)S(1)}, u32[]{:S(2)}, u32[]{:S(2)}) collective-permute-start(bf16[4,128,512]{2,1,0:T(8,128)(2,1)S(1)} %collective-permute-done.5.refs_2_), channel_id=1, source_target_pairs={{0,1},{1,0},{2,3},{3,2},{4,5},{5,4},{6,7},{7,6},{8,9},{9,8},{10,11... | collective-permute-start | bytes 1572872 | tf_op jit(solution)/shard_map/ppermute | solution.py:20
  43.3 7.5 %collective-permute-start.21 = (bf16[4,128,512]{2,1,0:T(8,128)(2,1)S(1)}, bf16[4,128,512]{2,1,0:T(8,128)(2,1)S(1)}, u32[]{:S(2)}, u32[]{:S(2)}) collective-permute-start(bf16[4,128,512]{2,1,0:T(8,128)(2,1)S(1)} %collective-permute-done.4.refs_1_), channel_id=1, source_target_pairs={{0,1},{1,0},{2,3},{3,2},{4,5},{5,4},{6,7},{7,6},{8,9},{9,8},{10,11... | collective-permute-start | bytes 1572872 | tf_op jit(solution)/shard_map/ppermute | solution.py:20
  50.2 1.5 %collective-permute-start.23 = (bf16[2,128,512]{2,1,0:T(8,128)(2,1)S(1)}, bf16[2,128,512]{2,1,0:T(8,128)(2,1)S(1)}, u32[]{:S(2)}, u32[]{:S(2)}) collective-permute-start(bf16[2,128,512]{2,1,0:T(8,128)(2,1)S(1)} %collective-permute-done.18.refs_3_), channel_id=1, source_target_pairs={{0,1},{1,0},{2,3},{3,2},{4,5},{5,4},{6,7},{7,6},{8,9},{9,8},{10,11... | collective-permute-start | bytes 786440 | tf_op jit(solution)/shard_map/ppermute | solution.py:20
  50.2 1.9 %collective-permute-start.24 = (bf16[2,128,512]{2,1,0:T(8,128)(2,1)S(1)}, bf16[2,128,512]{2,1,0:T(8,128)(2,1)S(1)}, u32[]{:S(2)}, u32[]{:S(2)}) collective-permute-start(bf16[2,128,512]{2,1,0:T(8,128)(2,1)S(1)} %collective-permute-done.19.refs_4_), channel_id=1, source_target_pairs={{0,1},{1,0},{2,3},{3,2},{4,5},{5,4},{6,7},{7,6},{8,9},{9,8},{10,11... | collective-permute-start | bytes 786440 | tf_op jit(solution)/shard_map/ppermute | solution.py:20
  53.5 1.4 %collective-permute-start.25 = (bf16[96,512]{1,0:T(8,128)(2,1)S(1)}, bf16[96,512]{1,0:T(8,128)(2,1)S(1)}, u32[]{:S(2)}, u32[]{:S(2)}) collective-permute-start(bf16[96,512]{1,0:T(8,128)(2,1)S(1)} %get-tuple-element.58), channel_id=1, source_target_pairs={{0,1},{1,0},{2,3},{3,2},{4,5},{5,4},{6,7},{7,6},{8,9},{9,8},{10,11... | collective-permute-start | bytes 294920 | tf_op jit(solution)/shard_map/ppermute | solution.py:20
  54.9 7.6 %collective-permute-start.28 = (bf16[96,512]{1,0:T(8,128)(2,1)S(1)}, bf16[96,512]{1,0:T(8,128)(2,1)S(1)}, u32[]{:S(2)}, u32[]{:S(2)}) collective-permute-start(bf16[96,512]{1,0:T(8,128)(2,1)S(1)} %add.29.refs_0_), channel_id=1, source_target_pairs={{0,6},{1,7},{2,4},{3,5},{4,2},{5,3},{6,0},{7,1},{8,14},{9,15},{10,... | collective-permute-start | bytes 294920 | tf_op jit(solution)/shard_map/ppermute | solution.py:20
  57.5 8.3 %collective-permute-start.27 = (bf16[96,512]{1,0:T(8,128)(2,1)S(1)}, bf16[96,512]{1,0:T(8,128)(2,1)S(1)}, u32[]{:S(2)}, u32[]{:S(2)}) collective-permute-start(bf16[96,512]{1,0:T(8,128)(2,1)S(1)} %add.29.refs_0_), channel_id=1, source_target_pairs={{0,4},{1,5},{2,6},{3,7},{4,0},{5,1},{6,2},{7,3},{8,12},{9,13},{10,... | collective-permute-start | bytes 294920 | tf_op jit(solution)/shard_map/ppermute | solution.py:20
  57.5 8.3 %collective-permute-start.26 = (bf16[96,512]{1,0:T(8,128)(2,1)S(1)}, bf16[96,512]{1,0:T(8,128)(2,1)S(1)}, u32[]{:S(2)}, u32[]{:S(2)}) collective-permute-start(bf16[96,512]{1,0:T(8,128)(2,1)S(1)} %add.29.refs_0_), channel_id=1, source_target_pairs={{0,2},{1,3},{2,0},{3,1},{4,6},{5,7},{6,4},{7,5},{8,10},{9,11},{10,... | collective-permute-start | bytes 294920 | tf_op jit(solution)/shard_map/ppermute | solution.py:20
  65.9 7.4 %collective-permute-start.30 = (bf16[96,512]{1,0:T(8,128)(2,1)S(1)}, bf16[96,512]{1,0:T(8,128)(2,1)S(1)}, u32[]{:S(2)}, u32[]{:S(2)}) collective-permute-start(bf16[96,512]{1,0:T(8,128)(2,1)S(1)} %add.30.after), channel_id=1, source_target_pairs={{0,24},{8,16},{1,25},{9,17},{2,26},{10,18},{3,27},{11,19},{4,28},{... | collective-permute-start | bytes 294920 | tf_op jit(solution)/shard_map/ppermute | solution.py:25
  69.2 4.0 %collective-permute-start.29 = (bf16[96,512]{1,0:T(8,128)(2,1)S(1)}, bf16[96,512]{1,0:T(8,128)(2,1)S(1)}, u32[]{:S(2)}, u32[]{:S(2)}) collective-permute-start(bf16[96,512]{1,0:T(8,128)(2,1)S(1)} %add.30.after), channel_id=1, source_target_pairs={{0,16},{8,24},{1,17},{9,25},{2,18},{10,26},{3,19},{11,27},{4,20},{... | collective-permute-start | bytes 294920 | tf_op jit(solution)/shard_map/ppermute | solution.py:25
  70.5 25.0 %copy-start.1 = (bf16[512,512]{1,0:T(8,128)(2,1)S(1)}, bf16[512,512]{1,0:T(8,128)(2,1)}, u32[]{:S(2)}) copy-start(bf16[512,512]{1,0:T(8,128)(2,1)} %param.11) | copy-start | bytes 1572868
  73.3 1.4 %collective-permute-start.31 = (bf16[96,512]{1,0:T(8,128)(2,1)S(1)}, bf16[96,512]{1,0:T(8,128)(2,1)S(1)}, u32[]{:S(2)}, u32[]{:S(2)}) collective-permute-start(bf16[96,512]{1,0:T(8,128)(2,1)S(1)} %add.31.refs_0_), channel_id=1, source_target_pairs={{0,1},{1,0},{2,3},{3,2},{4,5},{5,4},{6,7},{7,6},{8,9},{9,8},{10,11... | collective-permute-start | bytes 294920 | tf_op jit(solution)/shard_map/ppermute | solution.py:20
  75.7 1.4 %collective-permute-start.32 = (bf16[96,512]{1,0:T(8,128)(2,1)S(1)}, bf16[96,512]{1,0:T(8,128)(2,1)S(1)}, u32[]{:S(2)}, u32[]{:S(2)}) collective-permute-start(bf16[96,512]{1,0:T(8,128)(2,1)S(1)} %get-tuple-element.74), channel_id=1, source_target_pairs={{0,1},{1,0},{2,3},{3,2},{4,5},{5,4},{6,7},{7,6},{8,9},{9,8},{10,11... | collective-permute-start | bytes 294920 | tf_op jit(solution)/shard_map/ppermute | solution.py:20
  77.1 7.6 %collective-permute-start.35 = (bf16[96,512]{1,0:T(8,128)(2,1)S(1)}, bf16[96,512]{1,0:T(8,128)(2,1)S(1)}, u32[]{:S(2)}, u32[]{:S(2)}) collective-permute-start(bf16[96,512]{1,0:T(8,128)(2,1)S(1)} %add.32.refs_0_), channel_id=1, source_target_pairs={{0,6},{1,7},{2,4},{3,5},{4,2},{5,3},{6,0},{7,1},{8,14},{9,15},{10,... | collective-permute-start | bytes 294920 | tf_op jit(solution)/shard_map/ppermute | solution.py:20
  80.2 8.5 %collective-permute-start.34 = (bf16[96,512]{1,0:T(8,128)(2,1)S(1)}, bf16[96,512]{1,0:T(8,128)(2,1)S(1)}, u32[]{:S(2)}, u32[]{:S(2)}) collective-permute-start(bf16[96,512]{1,0:T(8,128)(2,1)S(1)} %add.32.refs_0_), channel_id=1, source_target_pairs={{0,4},{1,5},{2,6},{3,7},{4,0},{5,1},{6,2},{7,3},{8,12},{9,13},{10,... | collective-permute-start | bytes 294920 | tf_op jit(solution)/shard_map/ppermute | solution.py:20
  80.2 8.5 %collective-permute-start.33 = (bf16[96,512]{1,0:T(8,128)(2,1)S(1)}, bf16[96,512]{1,0:T(8,128)(2,1)S(1)}, u32[]{:S(2)}, u32[]{:S(2)}) collective-permute-start(bf16[96,512]{1,0:T(8,128)(2,1)S(1)} %add.32.refs_0_), channel_id=1, source_target_pairs={{0,2},{1,3},{2,0},{3,1},{4,6},{5,7},{6,4},{7,5},{8,10},{9,11},{10,... | collective-permute-start | bytes 294920 | tf_op jit(solution)/shard_map/ppermute | solution.py:20
  88.7 4.7 %collective-permute-start.36 = (bf16[96,512]{1,0:T(8,128)(2,1)S(1)}, bf16[96,512]{1,0:T(8,128)(2,1)S(1)}, u32[]{:S(2)}, u32[]{:S(2)}) collective-permute-start(bf16[96,512]{1,0:T(8,128)(2,1)S(1)} %choose.1.refs_0_), channel_id=1, source_target_pairs={{0,8},{8,0},{16,24},{24,16},{1,9},{9,1},{17,25},{25,17},{2,10},{10... | collective-permute-start | bytes 294920 | tf_op jit(solution)/shard_map/ppermute | solution.py:20
  93.5 1.4 %collective-permute-start.37 = (bf16[96,512]{1,0:T(8,128)(2,1)S(1)}, bf16[96,512]{1,0:T(8,128)(2,1)S(1)}, u32[]{:S(2)}, u32[]{:S(2)}) collective-permute-start(bf16[96,512]{1,0:T(8,128)(2,1)S(1)} %add.33.near), channel_id=1, source_target_pairs={{0,1},{1,0},{2,3},{3,2},{4,5},{5,4},{6,7},{7,6},{8,9},{9,8},{10,11... | collective-permute-start | bytes 294920 | tf_op jit(solution)/shard_map/ppermute | solution.py:20
